TPU v7x, 32 devices: a whole 2x2x4 slice. The times are simulated.
32 devices in a mesh: section: 2 (over x), expert: 16 (over z, y, core).
Axes of the slice: x: 2, y: 2, z: 4, core: 2. Of those that a mesh axis runs over, the one named last changes fastest.
Arguments:
- in_flight: bfloat16 [2, 2, 512, 1024], P('section', None, 'expert'), may hold values from -6 to 6
- arriving: bfloat16 [1, 2, 512, 1024], P(None, None, 'expert'), may hold values from -6 to 6
- norm_gain: float32 [2, 1024], P('section'), may hold values from 0.1 to 1.9
- gate_up: bfloat16 [2, 16, 1024, 1536], P('section', 'expert'), may hold values from -0.1875 to 0.1875
- w_down: bfloat16 [2, 16, 768, 1024], P('section', 'expert'), may hold values from -0.21875 to 0.21875
- expert_ids: int32 [2, 2, 2, 512, 8], P(None, 'section', None, 'expert'), may hold values from 0 to 15, all different within a row; in each aligned block of 32 rows (0 to 31, 32 to 63, ..., all dimensions but the last counted through in order) at most 16 rows name the same one
- route_weights: float32 [2, 2, 2, 512, 8], P(None, 'section', None, 'expert'), may hold values from 0.05 to 1
Outputs:
- section_outputs: bfloat16 [2, 2, 2, 512, 1024], P(None, 'section', None, 'expert')
Inputs may be any that keep to these rules, and one draw needn't show every extreme that they name: `expert_ids`: each token names 8 different experts. In each micro-batch of each step and section, the tokens of one aligned block of 32 (the rows of one device) name one expert at most 16 times.
All inputs are finite; a program needn't handle non-finite values.
Results may differ from a plain program's by a relative error of at most 0.007.
Values may be sent and summed in bfloat16 or wider, within the bound.
No kernel may reach another device: no remote copies, remote signals or barrier semaphores. Data moves between devices by JAX's collectives and lax.ppermute only.
A program may use at most 64 MiB of HBM per device.

v0:
```python
import jax
import jax.numpy as jnp
from jax import lax
from jax.sharding import PartitionSpec as P


def shifted(value, axis, by):
    size = lax.axis_size(axis)
    pairs = [(i, i + by) for i in range(size) if 0 <= i + by < size]
    return lax.ppermute(value, axis, pairs)


def normalize(inflow, gain_row):
    widened = inflow.astype(jnp.float32)
    inverse_rms = lax.rsqrt(jnp.mean(widened * widened, axis=-1, keepdims=True) + 1e-06)
    return (widened * inverse_rms * gain_row).astype(jnp.bfloat16)


def run_experts(buffer, gate_up, w_down):
    hidden_count = w_down.shape[2]
    row_block = buffer[:, :, 0].reshape(-1, buffer.shape[-1])
    projected = jnp.dot(row_block, gate_up[0, 0], preferred_element_type=jnp.float32)
    hidden = (jax.nn.silu(projected[:, :hidden_count]) * projected[:, hidden_count:]).astype(
        jnp.bfloat16
    )
    result = jnp.dot(hidden, w_down[0, 0], preferred_element_type=jnp.float32).astype(jnp.bfloat16)
    outputs = [result.reshape(buffer.shape[:2] + buffer.shape[3:])]
    return jnp.stack(outputs, axis=2)


def local(in_flight, arriving, norm_gain, gate_up, w_down, expert_ids, route_weights):
    owners = lax.axis_size("expert")
    local_count = gate_up.shape[1]
    experts_all = owners * local_count
    micro_count = in_flight.shape[1]
    tokens_mb = in_flight.shape[2]
    features = in_flight.shape[3]
    top_count = expert_ids.shape[-1]
    capacity = max(tokens_mb // 2, tokens_mb * top_count // experts_all)
    is_first = lax.axis_index("section") == 0
    gain_row = norm_gain[0][None, None, :]
    outputs = []
    inflow = in_flight[0]
    for step_number in range(expert_ids.shape[0]):
        if step_number > 0:
            incoming = shifted(outputs[-1], "section", 1)
            inflow = jnp.where(is_first, arriving[step_number - 1], incoming)
        normed = normalize(inflow, gain_row)
        step_ids = expert_ids[step_number, 0]
        flat_ids = step_ids.reshape(micro_count, tokens_mb * top_count)
        onehot = (
            flat_ids[:, :, None] == jnp.arange(experts_all, dtype=jnp.int32)[None, None, :]
        ).astype(jnp.int32)
        earlier = jnp.cumsum(onehot, axis=1) - onehot
        slot_of = jnp.sum(earlier * onehot, axis=-1)
        target = (flat_ids * capacity + slot_of).reshape(micro_count, tokens_mb, top_count)
        row_index = jnp.arange(experts_all * capacity, dtype=jnp.int32)
        picker = jnp.sum(
            (target[:, None, :, :] == row_index[None, :, None, None]).astype(jnp.int32), axis=3
        ).astype(jnp.bfloat16)
        outgoing = jnp.einsum(
            "mri,mid->mrd", picker, normed, preferred_element_type=jnp.float32
        ).astype(jnp.bfloat16)
        outgoing = outgoing.reshape(micro_count, experts_all, capacity, features)
        received = lax.all_to_all(outgoing, "expert", split_axis=1, concat_axis=1, tiled=True)
        count = received.shape[0]
        buffer = received.reshape(count, owners, local_count, capacity, features)
        served = run_experts(buffer, gate_up, w_down).reshape(
            count, experts_all, capacity, features
        )
        returned = lax.all_to_all(served, "expert", split_axis=1, concat_axis=1, tiled=True)
        picked = jnp.take_along_axis(
            returned.reshape(micro_count, experts_all * capacity, features),
            target.reshape(micro_count, tokens_mb * top_count, 1),
            axis=1,
        )
        weights_now = route_weights[step_number, 0][..., None]
        branch = jnp.sum(
            picked.reshape(micro_count, tokens_mb, top_count, features).astype(jnp.float32)
            * weights_now,
            axis=2,
        )
        outputs.append((inflow.astype(jnp.float32) + branch).astype(jnp.bfloat16))
    return jnp.stack(outputs)[:, None]


def solution(mesh):
    return jax.shard_map(
        local,
        mesh=mesh,
        in_specs=(
            P("section", None, "expert", None),
            P(None, None, "expert", None),
            P("section", None),
            P("section", "expert", None, None),
            P("section", "expert", None, None),
            P(None, "section", None, "expert", None),
            P(None, "section", None, "expert", None),
        ),
        out_specs=P(None, "section", None, "expert", None),
        check_vma=False,
    )
```

profile of v0, /device:TPU:0, one launch (start us, length us, event | category | flops | bytes accessed | tf_op | source)
XLA Modules:
  0.0 173.9 jit_solution(5850340888122731299)
XLA Ops:
  2.2 1.2 reduce-window.14
  4.0 1.4 convolution_convert_fusion.1
  5.6 32.0 %all_to_all.20 = bf16[2,16,16,1024]{3,2,0,1:T(8,128)(2,1)S(1)} all-to-all(bf16[2,16,16,1024]{3,2,0,1:T(8,128)(2,1)S(1)} %copy.46), channel_id=1, replica_groups=mesh['section'=2,'expert'=16] {'expert'}, dimensions={1} | all-to-all | bytes 2097152 | tf_op jit(solution)/shard_map/all_to_all | solution.py:65
  37.7 1.8 %fusion.2 = f32[512,1536]{1,0:T(8,128)S(1)} fusion(bf16[512,1024]{1,0:T(8,128)(2,1)S(1)} %bitcast.153, bf16[1,1,1024,1536]{3,2,1,0:T(8,128)(2,1)S(1)} %copy-done), kind=kOutput, calls=%fused_computation.4 | convolution fusion | flops 1610612736 | bytes 7340032 | tf_op jit(solution)/shard_map/dot_general | solution.py:22
  39.5 1.0 fusion.12
  40.6 1.1 copy.48
  41.7 5.0 %all-to-all-start.1 = ((bf16[2,16,16,1024]{3,2,0,1:T(8,128)(2,1)}), bf16[2,16,16,1024]{3,2,0,1:T(8,128)(2,1)}, u32[]{:S(2)}, u32[]{:S(2)}) async-start(bf16[2,16,16,1024]{3,2,0,1:T(8,128)(2,1)} %copy.48), calls=%async_computation.1 | async-start | bytes 2097152 | tf_op jit(solution)/shard_map/all_to_all | solution.py:71
  47.0 1.2 reduce-window.16
  50.7 19.1 %all-to-all-done.1 = bf16[2,16,16,1024]{3,2,0,1:T(8,128)(2,1)} async-done(((bf16[2,16,16,1024]{3,2,0,1:T(8,128)(2,1)}), bf16[2,16,16,1024]{3,2,0,1:T(8,128)(2,1)}, u32[]{:S(2)}, u32[]{:S(2)}) %all-to-all-start.1) | async-done | bytes 1048608 | tf_op jit(solution)/shard_map/all_to_all | solution.py:71
  69.7 2.4 %copy.49 = bf16[2,16,16,1024]{3,2,1,0:T(8,128)(2,1)} copy(bf16[2,16,16,1024]{3,2,0,1:T(8,128)(2,1)} %all-to-all-done.1) | data formatting | bytes 2097152 | tf_op jit(solution)/shard_map/all_to_all | solution.py:71
  72.1 10.6 %gather_fusion = bf16[512,1024]{1,0:T(8,128)(2,1)} fusion(bf16[2,256,1024]{2,1,0:T(8,128)(2,1)} %bitcast.145, s32[512]{0:T(512)S(1)} %bitcast.147), kind=kCustom, calls=%fused_computation.clone | custom fusion | bytes 2101248 | tf_op jit(solution)/shard_map/jit(take_along_axis)/gather | solution.py:72
  82.7 2.1 %fusion.5 = f32[2,32,1024]{2,1,0:T(8,128)S(1)} fusion(bf16[2,256,1024]{2,1,0:T(8,128)(2,1)} %bitcast.149, f32[2,32,8]{2,1,0:T(8,128)} %copy.50, pred[2,256]{1,0:T(4,128)(4,1)} %and_bitcast_fusion.1), kind=kLoop, calls=%fused_computation.9 | loop fusion | flops 2031616 | bytes 1313280 | tf_op jit(solution)/shard_map/reduce_sum | solution.py:78
  85.5 4.2 %collective-permute-start = (bf16[2,32,1024]{2,1,0:T(8,128)(2,1)}, bf16[2,32,1024]{2,1,0:T(8,128)(2,1)}, u32[]{:S(2)}, u32[]{:S(2)}) collective-permute-start(bf16[2,32,1024]{2,1,0:T(8,128)(2,1)} %fusion.28), channel_id=1, source_target_pairs={{0,16},{1,17},{2,18},{3,19},{4,20},{5,21},{6,22},{7,23},{8,24},{9,... | collective-permute-start | bytes 393224 | tf_op jit(solution)/shard_map/ppermute | solution.py:10
  89.7 1.4 bitcast_add_fusion
  92.8 1.0 fusion.30
  94.6 31.2 %all_to_all.21 = bf16[2,16,16,1024]{3,2,0,1:T(8,128)(2,1)S(1)} all-to-all(bf16[2,16,16,1024]{3,2,0,1:T(8,128)(2,1)S(1)} %copy.53), channel_id=1, replica_groups=mesh['section'=2,'expert'=16] {'expert'}, dimensions={1} | all-to-all | bytes 2097152 | tf_op jit(solution)/shard_map/all_to_all | solution.py:65
  125.9 1.8 %fusion = f32[512,1536]{1,0:T(8,128)S(1)} fusion(bf16[512,1024]{1,0:T(8,128)(2,1)S(1)} %bitcast.155, bf16[1,1,1024,1536]{3,2,1,0:T(8,128)(2,1)S(1)} %copy-done), kind=kOutput, calls=%fused_computation.2 | convolution fusion | flops 1610612736 | bytes 7340032 | tf_op jit(solution)/shard_map/dot_general | solution.py:22
  128.8 1.1 copy.55
  129.9 5.0 %all-to-all-start.3 = ((bf16[2,16,16,1024]{3,2,0,1:T(8,128)(2,1)}), bf16[2,16,16,1024]{3,2,0,1:T(8,128)(2,1)}, u32[]{:S(2)}, u32[]{:S(2)}) async-start(bf16[2,16,16,1024]{3,2,0,1:T(8,128)(2,1)} %copy.55), calls=%async_computation.3 | async-start | bytes 2097152 | tf_op jit(solution)/shard_map/all_to_all | solution.py:71
  135.6 1.4 broadcast_multiply_fusion
  138.6 19.4 %all-to-all-done.3 = bf16[2,16,16,1024]{3,2,0,1:T(8,128)(2,1)} async-done(((bf16[2,16,16,1024]{3,2,0,1:T(8,128)(2,1)}), bf16[2,16,16,1024]{3,2,0,1:T(8,128)(2,1)}, u32[]{:S(2)}, u32[]{:S(2)}) %all-to-all-start.3) | async-done | bytes 1048608 | tf_op jit(solution)/shard_map/all_to_all | solution.py:71
  157.9 2.4 %copy.56 = bf16[2,16,16,1024]{3,2,1,0:T(8,128)(2,1)} copy(bf16[2,16,16,1024]{3,2,0,1:T(8,128)(2,1)} %all-to-all-done.3) | data formatting | bytes 2097152 | tf_op jit(solution)/shard_map/all_to_all | solution.py:71
  160.3 10.6 %gather_fusion.1 = bf16[512,1024]{1,0:T(8,128)(2,1)} fusion(bf16[2,256,1024]{2,1,0:T(8,128)(2,1)} %bitcast.146, s32[512]{0:T(512)S(1)} %bitcast.148), kind=kCustom, calls=%fused_computation.1.clone | custom fusion | bytes 2101248 | tf_op jit(solution)/shard_map/jit(take_along_axis)/gather | solution.py:72
  171.0 2.1 %fusion.4 = f32[2,32,1024]{2,1,0:T(8,128)S(1)} fusion(bf16[2,256,1024]{2,1,0:T(8,128)(2,1)} %bitcast.150, f32[2,32,8]{2,1,0:T(8,128)S(1)} %copy-done.6, pred[2,256]{1,0:T(4,128)(4,1)S(1)} %and_bitcast_fusion), kind=kLoop, calls=%fused_computation.7 | loop fusion | flops 2031616 | bytes 1313280 | tf_op jit(solution)/shard_map/reduce_sum | solution.py:78
  (70 shorter events, 13.1 us)
Async XLA Ops:
  0.0 37.7 %copy-start = (bf16[1,1,1024,1536]{3,2,1,0:T(8,128)(2,1)S(1)}, bf16[1,1,1024,1536]{3,2,1,0:T(8,128)(2,1)}, u32[]{:S(2)}) copy-start(bf16[1,1,1024,1536]{3,2,1,0:T(8,128)(2,1)} %param.12) | copy-start | bytes 9437188
  37.7 1.8 %copy-start.9 = (bf16[1,1,768,1024]{3,2,1,0:T(8,128)(2,1)S(1)}, bf16[1,1,768,1024]{3,2,1,0:T(8,128)(2,1)}, u32[]{:S(2)}) copy-start(bf16[1,1,768,1024]{3,2,1,0:T(8,128)(2,1)} %param.13) | copy-start | bytes 4718596
  40.6 8.8 %copy-start.8 = (f32[2,1,2,32,8]{3,4,2,1,0:T(8,128)S(1)}, f32[2,1,2,32,8]{3,4,2,1,0:T(8,128)}, u32[]{:S(2)}) copy-start(f32[2,1,2,32,8]{3,4,2,1,0:T(8,128)} %param.15) | copy-start | bytes 12292
  41.7 28.0 %all-to-all-start.1 = ((bf16[2,16,16,1024]{3,2,0,1:T(8,128)(2,1)}), bf16[2,16,16,1024]{3,2,0,1:T(8,128)(2,1)}, u32[]{:S(2)}, u32[]{:S(2)}) async-start(bf16[2,16,16,1024]{3,2,0,1:T(8,128)(2,1)} %copy.48), calls=%async_computation.1 | async-start | bytes 2097152 | tf_op jit(solution)/shard_map/all_to_all | solution.py:71
  46.8 1.7 copy-start.4
  72.1 12.7 %copy-start.1 = (bf16[1,2,32,1024]{3,2,1,0:T(8,128)(2,1)S(1)}, bf16[1,2,32,1024]{3,2,1,0:T(8,128)(2,1)}, u32[]{:S(2)}) copy-start(bf16[1,2,32,1024]{3,2,1,0:T(8,128)(2,1)} %param.9) | copy-start | bytes 393220
  82.7 11.2 %copy-start.7 = (f32[1,1024]{1,0:T(1,128)S(1)}, f32[1,1024]{1,0:T(1,128)}, u32[]{:S(2)}) copy-start(f32[1,1024]{1,0:T(1,128)} %param.11) | copy-start | bytes 12292
  85.5 7.3 %collective-permute-start = (bf16[2,32,1024]{2,1,0:T(8,128)(2,1)}, bf16[2,32,1024]{2,1,0:T(8,128)(2,1)}, u32[]{:S(2)}, u32[]{:S(2)}) collective-permute-start(bf16[2,32,1024]{2,1,0:T(8,128)(2,1)} %fusion.28), channel_id=1, source_target_pairs={{0,16},{1,17},{2,18},{3,19},{4,20},{5,21},{6,22},{7,23},{8,24},{9,... | collective-permute-start | bytes 393224 | tf_op jit(solution)/shard_map/ppermute | solution.py:10
  93.8 0.7 copy-start.2
  125.9 1.8 %copy-start.10 = (bf16[1,1,768,1024]{3,2,1,0:T(8,128)(2,1)S(1)}, bf16[1,1,768,1024]{3,2,1,0:T(8,128)(2,1)}, u32[]{:S(2)}) copy-start(bf16[1,1,768,1024]{3,2,1,0:T(8,128)(2,1)} %param.13) | copy-start | bytes 4718596
  129.9 28.0 %all-to-all-start.3 = ((bf16[2,16,16,1024]{3,2,0,1:T(8,128)(2,1)}), bf16[2,16,16,1024]{3,2,0,1:T(8,128)(2,1)}, u32[]{:S(2)}, u32[]{:S(2)}) async-start(bf16[2,16,16,1024]{3,2,0,1:T(8,128)(2,1)} %copy.55), calls=%async_computation.3 | async-start | bytes 2097152 | tf_op jit(solution)/shard_map/all_to_all | solution.py:71
  160.3 10.6 %copy-start.6 = (f32[2,32,8]{2,1,0:T(8,128)S(1)}, f32[2,32,8]{2,1,0:T(8,128)}, u32[]{:S(2)}) copy-start(f32[2,32,8]{2,1,0:T(8,128)} %copy.57) | copy-start | bytes 6148
  160.3 12.8 %copy-start.3 = (bf16[2,32,1024]{2,1,0:T(8,128)(2,1)S(1)}, bf16[2,32,1024]{2,1,0:T(8,128)(2,1)}, u32[]{:S(2)}) copy-start(bf16[2,32,1024]{2,1,0:T(8,128)(2,1)} %copy-done.2) | copy-start | bytes 393220
  160.3 12.8 %copy-start.5 = (bf16[1,2,32,1024]{3,2,1,0:T(8,128)(2,1)S(1)}, bf16[1,2,32,1024]{3,2,1,0:T(8,128)(2,1)}, u32[]{:S(2)}) copy-start(bf16[1,2,32,1024]{3,2,1,0:T(8,128)(2,1)} %fusion.29) | copy-start | bytes 393220
where the time goes:
time: 177 us; the launch traced here: 174 us
  blocking collectives  63.3 us (36%)
  waiting for transfers between devices  39.2 us (22%)
  local copies, waits for them, and re-layouts  33.7 us (19%)
  other arithmetic  15.6 us (9%)
  starting transfers between devices  14.3 us (8%)
  matrix products  7.53 us (4%)
    all_to_all x2, blocking collectives, local(): lax.all_to_all(outgoing, 'expert', split_axis=1, concat_axis=1, tiled=True)  63.3 us
    all_to_all x2, waiting for transfers between devices, local(): lax.all_to_all(served, 'expert', split_axis=1, concat_axis=1, tiled=True)  38.4 us
    gather x2, local copies, waits for them, and re-layouts, local(): jnp.take_along_axis(returned.reshape(micro_count, experts_all * capacity,...  21.2 us
    all_to_all x2, starting transfers between devices, local(): lax.all_to_all(served, 'expert', split_axis=1, concat_axis=1, tiled=True)  10.1 us
    all_to_all x2, local copies, waits for them, and re-layouts, local(): lax.all_to_all(served, 'expert', split_axis=1, concat_axis=1, tiled=True)  4.74 us
    reduce_sum x2, other arithmetic, local(): jnp.sum(picked.reshape(micro_count, tokens_mb, top_count, features).astyp...  4.24 us
    ppermute x1, starting transfers between devices, shifted(): return lax.ppermute(value, axis, pairs)  4.21 us
    dot_general x2, matrix products, run_experts(): jnp.dot(row_block, gate_up[0, 0], preferred_element_type=jnp.float32)  3.6 us
  transfers between devices with their start and end apart: 3, of which 3 were waited for; matrix products, arithmetic and copies ran while one was open for 6% of the time, Pallas kernels for 0%

commit v1 on v0

v1 whole, which is shorter than its diff:
```python
import functools

import jax
import jax.numpy as jnp
from jax import lax
from jax.experimental import pallas as pl
from jax.experimental.pallas import tpu as pltpu
from jax.sharding import PartitionSpec as P

LANES = 128


def normalize(inflow, gain_row):
    widened = inflow.astype(jnp.float32)
    inverse_rms = lax.rsqrt(jnp.mean(widened * widened, axis=-1, keepdims=True) + 1e-06)
    return (widened * inverse_rms * gain_row).astype(jnp.bfloat16)


def first_kernel(
    experts_all, inflow_hbm, gain_hbm, ids_hbm, weights_hbm, *refs
):
    inflow, gain, ids, weights, sem = refs[-5:]
    payloads, later = refs[:-6], refs[-6]
    copies = [
        pltpu.make_async_copy(source, target, sem.at[number])
        for number, (source, target) in enumerate(
            ((ids_hbm, ids), (weights_hbm, weights), (inflow_hbm, inflow), (gain_hbm, gain))
        )
    ]
    for copy in copies:
        copy.start()
    for copy in copies:
        copy.wait()
    steps, micro_count, top_count, tokens = ids.shape
    features = inflow.shape[-1]
    width = later.shape[-1]
    expert = lax.broadcasted_iota(jnp.int32, (experts_all, tokens), 0)
    columns = []
    for step in range(steps):
        for micro in range(micro_count):
            dense = jnp.zeros((experts_all, tokens), jnp.float32)
            for k in range(top_count):
                named = ids[step, micro, k : k + 1, :] == expert
                dense = dense + jnp.where(named, weights[step, micro, k : k + 1, :], 0.0)
            high = dense.astype(jnp.bfloat16).astype(jnp.float32)
            empty = jnp.zeros((width - 2 * experts_all, tokens), jnp.float32)
            columns.append(jnp.concatenate([high, dense - high, empty], axis=0))
    tails = jnp.concatenate(columns, axis=1).T.astype(jnp.bfloat16)
    tails = tails.reshape(steps, micro_count, tokens, width)
    for micro, payload in enumerate(payloads):
        payload[:, :features] = normalize(inflow[micro], gain[...])
        payload[:, features:] = tails[0, micro]
    later[...] = tails[1:]


def first_payload(inflow, gain, ids, weights, experts_all):
    micro_count, tokens, features = inflow.shape
    steps = ids.shape[0]
    width = -(-2 * experts_all // LANES) * LANES
    return pl.pallas_call(
        functools.partial(first_kernel, experts_all),
        out_shape=(jax.ShapeDtypeStruct((tokens, features + width), jnp.bfloat16),) * micro_count
        + (jax.ShapeDtypeStruct((steps - 1, micro_count, tokens, width), jnp.bfloat16),),
        in_specs=[pl.BlockSpec(memory_space=pltpu.HBM)] * 4,
        out_specs=[pl.BlockSpec(memory_space=pltpu.VMEM)] * (micro_count + 1),
        scratch_shapes=[
            pltpu.VMEM(inflow.shape, inflow.dtype),
            pltpu.VMEM(gain.shape, gain.dtype),
            pltpu.VMEM(ids.shape, ids.dtype),
            pltpu.VMEM(weights.shape, weights.dtype),
            pltpu.SemaphoreType.DMA((4,)),
        ],
        compiler_params=pltpu.CompilerParams(vmem_limit_bytes=8 * 1024 * 1024),
        name="first_payload",
    )(inflow, gain, ids, weights)


def leave_kernel(step, micro, inflow, own, *refs):
    parts, (fresh, gain, tail, out, leaving, payload) = refs[:-6], refs[-6:]
    features = inflow.shape[-1]
    total = inflow[...].reshape(own.shape).astype(jnp.float32) + own[...]
    for part in parts:
        total = total + part[...].astype(jnp.float32)
    result = total.astype(jnp.bfloat16)
    out[...] = result
    is_last = lax.axis_index("section") == lax.axis_size("section") - 1
    arrived = fresh[step, micro].astype(jnp.float32)
    gone = jnp.where(is_last, arrived, result.astype(jnp.float32))
    leaving[...] = gone.astype(jnp.bfloat16)
    payload[:, :features] = normalize(gone, gain[...])
    payload[:, features:] = tail[step, micro]


def leave(step, micro, inflow, own, parts, fresh, gain, tail):
    tokens, features = own.shape
    whole = pl.BlockSpec(memory_space=pltpu.VMEM)
    rows = jax.ShapeDtypeStruct((tokens, features), jnp.bfloat16)
    return pl.pallas_call(
        functools.partial(leave_kernel, step, micro),
        out_shape=(
            rows,
            rows,
            jax.ShapeDtypeStruct((tokens, features + tail.shape[-1]), jnp.bfloat16),
        ),
        in_specs=[whole] * (5 + len(parts)),
        out_specs=[whole] * 3,
        compiler_params=pltpu.CompilerParams(vmem_limit_bytes=8 * 1024 * 1024),
        name="leave",
    )(inflow, own, *parts, fresh, gain, tail)


def swap_core(value):
    size = lax.axis_size("expert")
    return lax.ppermute(value, "expert", [(i, i ^ 1) for i in range(size)])


def swap_inner(value):
    size = lax.axis_size("expert")
    return lax.ppermute(value, "expert", [(i, i ^ 2) for i in range(size)])


def rotate_outer(value, by):
    size = lax.axis_size("expert")
    return lax.ppermute(value, "expert", [(i, (i + 4 * by) % size) for i in range(size)])


def next_section(value, by):
    sections, size = lax.axis_size("section"), lax.axis_size("expert")
    pairs = [
        (s * size + i, (s + 1) % sections * size + (i + 4 * by) % size)
        for s in range(sections)
        for i in range(size)
    ]
    return lax.ppermute(value, ("section", "expert"), pairs)


def previous_section(value):
    sections = lax.axis_size("section")
    return lax.ppermute(value, "section", [(s, (s - 1) % sections) for s in range(sections)])


def serve_kernel(
    features, hidden_count, chunk, experts_all, local_count,
    near, far, own_in, far_in, own_out, far_out,
    near_sum, far_sum, rows, hidden,
):
    blocks, tokens = near.shape[:2]
    half = blocks * tokens
    rows[pl.ds(0, half)] = near[:, :, :features].reshape(half, features)
    rows[pl.ds(half, half)] = far[:, :, :features].reshape(half, features)
    tail = jnp.concatenate(
        [part[:, :, features:].reshape(half, -1) for part in (near, far)]
    ).astype(jnp.float32)
    lane = lax.broadcasted_iota(jnp.int32, tail.shape, 1)
    me = lax.axis_index("expert")
    total = None
    for side, (w_in, w_out) in enumerate(((own_in, own_out), (far_in, far_out))):
        for own in range(local_count):
            which = (me + side * (1 - 2 * (me % 2))) * local_count + own
            chosen = (lane == which) | (lane == which + experts_all)
            weight = jnp.sum(jnp.where(chosen, tail, 0.0), axis=-1, keepdims=True)
            for at in range(0, hidden_count, chunk):
                gate = jnp.dot(
                    rows[...], w_in[own, :, pl.ds(at, chunk)], preferred_element_type=jnp.float32
                )
                up = jnp.dot(
                    rows[...],
                    w_in[own, :, pl.ds(hidden_count + at, chunk)],
                    preferred_element_type=jnp.float32,
                )
                value = gate / (1.0 + jnp.exp(-gate)) * up * weight
                hidden[:, pl.ds(at, chunk)] = value.astype(jnp.bfloat16)
            out = jnp.dot(hidden[...], w_out[own], preferred_element_type=jnp.float32)
            total = out if total is None else total + out
    near_sum[...] = total[:half].reshape(near_sum.shape)
    far_sum[...] = total[half:].astype(jnp.bfloat16).reshape(far_sum.shape)


def serve(near, far, own_in, far_in, own_out, far_out, experts_all):
    blocks, tokens, width = near.shape
    local_count, features, _ = own_in.shape
    hidden_count = own_out.shape[1]
    chunk = 256 if hidden_count % 256 == 0 else hidden_count
    rows_all = 2 * blocks * tokens
    held = 2 * (own_in.size + own_out.size) * 2
    whole = pl.BlockSpec(memory_space=pltpu.VMEM)
    return pl.pallas_call(
        functools.partial(
            serve_kernel, features, hidden_count, chunk, experts_all, local_count
        ),
        out_shape=(
            jax.ShapeDtypeStruct((blocks, tokens, features), jnp.float32),
            jax.ShapeDtypeStruct((blocks, tokens, features), jnp.bfloat16),
        ),
        in_specs=[whole] * 6,
        out_specs=[whole] * 2,
        scratch_shapes=[
            pltpu.VMEM((rows_all, features), jnp.bfloat16),
            pltpu.VMEM((rows_all, hidden_count), jnp.bfloat16),
        ],
        compiler_params=pltpu.CompilerParams(vmem_limit_bytes=held + 8 * 1024 * 1024),
        cost_estimate=pl.CostEstimate(
            flops=2 * rows_all * 2 * local_count * 3 * features * hidden_count,
            bytes_accessed=held,
            transcendentals=rows_all * 2 * local_count * hidden_count,
        ),
        name="serve",
    )(near, far, own_in, far_in, own_out, far_out)


def local(in_flight, arriving, norm_gain, gate_up, w_down, expert_ids, route_weights):
    owners = lax.axis_size("expert")
    outer = owners // 4
    local_count = gate_up.shape[1]
    experts_all = owners * local_count
    steps = expert_ids.shape[0]
    micro_count = in_flight.shape[1]
    own_in, own_out = gate_up[0], w_down[0]
    far_in, far_out = swap_core(own_in), swap_core(own_out)
    *payloads, tails = first_payload(
        in_flight[0],
        norm_gain,
        jnp.swapaxes(expert_ids[:, 0], -1, -2),
        jnp.swapaxes(route_weights[:, 0], -1, -2),
        experts_all,
    )
    later_gain = previous_section(norm_gain)
    later_tails = previous_section(tails)
    inflows = [in_flight[0, micro] for micro in range(micro_count)]
    outputs = []
    for step in range(steps):
        results = []
        for micro in range(micro_count):
            payload, inflow = payloads[micro], inflows[micro]
            if step == 0:
                near = jnp.stack([payload] + [rotate_outer(payload, by) for by in range(1, outer)])
            else:
                near = jnp.stack([next_section(payload, by) for by in range(outer)])
            far = swap_inner(near)
            near_sum, far_sum = serve(near, far, own_in, far_in, own_out, far_out, experts_all)
            served = near_sum + swap_inner(far_sum).astype(jnp.float32)
            parts = [
                rotate_outer(served[by].astype(jnp.bfloat16), -by) for by in range(1, outer)
            ]
            if step < steps - 1:
                result, leaving, payloads[micro] = leave(
                    step, micro, inflow, served[0], parts, arriving, later_gain, later_tails
                )
                inflows[micro] = next_section(leaving, 0)
            else:
                total = inflow.astype(jnp.float32) + served[0]
                for part in parts:
                    total = total + part.astype(jnp.float32)
                result = total.astype(jnp.bfloat16)
            results.append(result)
        outputs.append(jnp.stack(results))
    return jnp.stack(outputs)[:, None]


def solution(mesh):
    return jax.shard_map(
        local,
        mesh=mesh,
        in_specs=(
            P("section", None, "expert", None),
            P(None, None, "expert", None),
            P("section", None),
            P("section", "expert", None, None),
            P("section", "expert", None, None),
            P(None, "section", None, "expert", None),
            P(None, "section", None, "expert", None),
        ),
        out_specs=P(None, "section", None, "expert", None),
        check_vma=False,
    )
```

time: 177 us -> 104 us (0.59); the launches traced: 174 us -> 103 us
  blocking collectives: 63.3 us -> 0 us
  starting transfers between devices: 14.3 us -> 59.5 us
  local copies, waits for them, and re-layouts: 33.7 us -> 5.74 us
  waiting for transfers between devices: 39.2 us -> 24.5 us
  other arithmetic: 15.6 us -> 1.33 us
  Pallas kernels: 0 us -> 12.1 us
  matrix products: 7.53 us -> 0 us
    all_to_all x2 -> x0, blocking collectives: 63.3 us -> none  [local(): lax.all_to_all(outgoing, 'expert', split_axis=1, concat_axis=1, tiled=True)]
    ppermute x1 -> x40, starting transfers between devices: 4.21 us -> 59.5 us  [the longest x18 30.2 us: rotate_outer(): lax.ppermute(value, 'expert', [(i, (i + 4 * by) % size) for i in range(si...]
    all_to_all x2 -> x0, waiting for transfers between devices: 38.4 us -> none  [local(): lax.all_to_all(served, 'expert', split_axis=1, concat_axis=1, tiled=True)]
    ppermute x1 -> x40, waiting for transfers between devices: 0.73 us -> 24.5 us  [the longest x8 12.9 us: swap_inner(): return lax.ppermute(value, 'expert', [(i, i ^ 2) for i in range(size)])]
    gather x2 -> x0, local copies, waits for them, and re-layouts: 21.2 us -> none  [local(): jnp.take_along_axis(returned.reshape(micro_count, experts_all * capacity,...]
    pallas_call x0 -> x7, Pallas kernels: none -> 12.1 us  [the longest x4 10.8 us: serve(): pl.pallas_call(functools.partial(serve_kernel, features, hidden_count, ch...]
    all_to_all x2 -> x0, starting transfers between devices: 10.1 us -> none  [local(): lax.all_to_all(served, 'expert', split_axis=1, concat_axis=1, tiled=True)]
    reduce_sum x8 -> x0, other arithmetic: 7.68 us -> none  [the longest x2 4.24 us: local(): jnp.sum(picked.reshape(micro_count, tokens_mb, top_count, features).astyp...]
  transfers between devices with their start and end apart: 3 -> 40, of which waited for: 3 -> 15; matrix products, arithmetic and copies ran while one was open for 6% -> 1% of each run, Pallas kernels for 0% -> 12%
where the time goes in v1:
time: 104 us; the launch traced here: 103 us
  starting transfers between devices  59.5 us (57%)
  waiting for transfers between devices  24.5 us (24%)
  Pallas kernels  12.1 us (12%)
  local copies, waits for them, and re-layouts  5.74 us (6%)
  other arithmetic  1.33 us (1%)
    ppermute x18, starting transfers between devices, rotate_outer(): lax.ppermute(value, 'expert', [(i, (i + 4 * by) % size) for i in range(si...  30.2 us
    ppermute x10, starting transfers between devices, next_section(): return lax.ppermute(value, ('section', 'expert'), pairs)  15.3 us
    ppermute x8, waiting for transfers between devices, swap_inner(): return lax.ppermute(value, 'expert', [(i, i ^ 2) for i in range(size)])  12.9 us
    ppermute x8, starting transfers between devices, swap_inner(): return lax.ppermute(value, 'expert', [(i, i ^ 2) for i in range(size)])  11.2 us
    pallas_call x4, Pallas kernels, serve(): pl.pallas_call(functools.partial(serve_kernel, features, hidden_count, ch...  10.8 us
    ppermute x18, waiting for transfers between devices, rotate_outer(): lax.ppermute(value, 'expert', [(i, (i + 4 * by) % size) for i in range(si...  8.51 us
    unnamed x16, local copies, waits for them, and re-layouts  5.65 us
    ppermute x10, waiting for transfers between devices, next_section(): return lax.ppermute(value, ('section', 'expert'), pairs)  3.13 us
  transfers between devices with their start and end apart: 40, of which 15 were waited for; matrix products, arithmetic and copies ran while one was open for 1% of the time, Pallas kernels for 12%

profile of v1, /device:TPU:0, one launch (start us, length us, event | category | flops | bytes accessed | tf_op | source)
XLA Modules:
  0.0 103.5 jit_solution(13367791848129207411)
XLA Ops:
  4.0 5.1 %collective-permute-start.14 = (bf16[32,1152]{1,0:T(8,128)(2,1)S(1)}, bf16[32,1152]{1,0:T(8,128)(2,1)S(1)}, u32[]{:S(2)}, u32[]{:S(2)}) collective-permute-start(bf16[32,1152]{1,0:T(8,128)(2,1)S(1)} %get-tuple-element.27), channel_id=1, source_target_pairs={{0,12},{1,13},{2,14},{3,15},{4,0},{5,1},{6,2},{7,3},{8,4},{9,5},{1... | collective-permute-start | bytes 221192 | tf_op jit(solution)/shard_map/ppermute | solution.py:124
  10.1 1.7 %collective-permute-done.14 = bf16[32,1152]{1,0:T(8,128)(2,1)S(1)} collective-permute-done((bf16[32,1152]{1,0:T(8,128)(2,1)S(1)}, bf16[32,1152]{1,0:T(8,128)(2,1)S(1)}, u32[]{:S(2)}, u32[]{:S(2)}) %collective-permute-start.14) | collective-permute-done | bytes 73760 | tf_op jit(solution)/shard_map/ppermute | solution.py:124
  11.8 4.3 %collective-permute-start.2 = (bf16[32,1152]{1,0:T(8,128)(2,1)S(1)}, bf16[32,1152]{1,0:T(8,128)(2,1)S(1)}, u32[]{:S(2)}, u32[]{:S(2)}) collective-permute-start(bf16[32,1152]{1,0:T(8,128)(2,1)S(1)} %get-tuple-element.22), channel_id=1, source_target_pairs={{0,12},{1,13},{2,14},{3,15},{4,0},{5,1},{6,2},{7,3},{8,4},{9,5},{1... | collective-permute-start | bytes 221192 | tf_op jit(solution)/shard_map/ppermute | solution.py:124
  20.4 2.3 %collective-permute-done.1 = bf16[32,1152]{1,0:T(8,128)(2,1)S(1)} collective-permute-done((bf16[32,1152]{1,0:T(8,128)(2,1)S(1)}, bf16[32,1152]{1,0:T(8,128)(2,1)S(1)}, u32[]{:S(2)}, u32[]{:S(2)}) %collective-permute-start.1) | collective-permute-done | bytes 73760 | tf_op jit(solution)/shard_map/ppermute | solution.py:124
  27.2 1.9 %copy-done = bf16[1,1,1024,1536]{3,2,1,0:T(8,128)(2,1)S(1)} copy-done((bf16[1,1,1024,1536]{3,2,1,0:T(8,128)(2,1)S(1)}, bf16[1,1,1024,1536]{3,2,1,0:T(8,128)(2,1)}, u32[]{:S(2)}) %copy-start) | copy-done | bytes 3145752
  30.5 2.7 %serve.5 = (f32[4,32,1024]{2,1,0:T(8,128)S(1)}, bf16[4,32,1024]{2,1,0:T(8,128)(2,1)S(1)}) custom-call(bf16[4,32,1152]{2,1,0:T(8,128)(2,1)S(1)} %pad_maximum_fusion.1.near, bf16[4,32,1152]{2,1,0:T(8,128)(2,1)S(1)} %collective-permute-done.15.far, bf16[1,1024,1536]{2,1,0:T(8,128)(2,1)S(1)} %bitcast.100, ...), custom_call_target="tpu_custom_call" | custom-call | flops 2415919104 | bytes 9437184 | tf_op jit(solution)/shard_map/serve/pallas_call | solution.py:187
  33.7 2.7 %serve.4 = (f32[4,32,1024]{2,1,0:T(8,128)S(1)}, bf16[4,32,1024]{2,1,0:T(8,128)(2,1)S(1)}) custom-call(bf16[4,32,1152]{2,1,0:T(8,128)(2,1)S(1)} %pad_maximum_fusion.near, bf16[4,32,1152]{2,1,0:T(8,128)(2,1)S(1)} %collective-permute-done.3.far, bf16[1,1024,1536]{2,1,0:T(8,128)(2,1)S(1)} %bitcast.101, bf16[1,1024,1536]{2,1,0:T(8,128)(2,1)S(1)} %collective-permute-done.4.far_in, ...), custom_call_target="tpu_custom_call" | custom-call | flops 2415919104 | bytes 9437184 | tf_op jit(solution)/shard_map/serve/pallas_call | solution.py:187
  36.5 1.6 %collective-permute-start.6 = (bf16[4,32,1024]{2,1,0:T(8,128)(2,1)S(1)}, bf16[4,32,1024]{2,1,0:T(8,128)(2,1)S(1)}, u32[]{:S(2)}, u32[]{:S(2)}) collective-permute-start(bf16[4,32,1024]{2,1,0:T(8,128)(2,1)S(1)} %get-tuple-element.24), channel_id=1, source_target_pairs={{0,2},{1,3},{2,0},{3,1},{4,6},{5,7},{6,4},{7,5},{8,10},{9,11},{10,... | collective-permute-start | bytes 786440 | tf_op jit(solution)/shard_map/ppermute | solution.py:119
  38.1 4.3 %collective-permute-done.16 = bf16[4,32,1024]{2,1,0:T(8,128)(2,1)S(1)} collective-permute-done((bf16[4,32,1024]{2,1,0:T(8,128)(2,1)S(1)}, bf16[4,32,1024]{2,1,0:T(8,128)(2,1)S(1)}, u32[]{:S(2)}, u32[]{:S(2)}) %collective-permute-start.16) | collective-permute-done | bytes 262176 | tf_op jit(solution)/shard_map/ppermute | solution.py:119
  42.5 4.1 %collective-permute-start.17 = (bf16[32,1024]{1,0:T(8,128)(2,1)S(1)}, bf16[32,1024]{1,0:T(8,128)(2,1)S(1)}, u32[]{:S(2)}, u32[]{:S(2)}) collective-permute-start(bf16[32,1024]{1,0:T(8,128)(2,1)S(1)} %get-tuple-element.58), channel_id=1, source_target_pairs={{0,12},{1,13},{2,14},{3,15},{4,0},{5,1},{6,2},{7,3},{8,4},{9,5},{1... | collective-permute-start | bytes 196616 | tf_op jit(solution)/shard_map/ppermute | solution.py:124
  47.3 3.2 %collective-permute-start.7 = (bf16[32,1024]{1,0:T(8,128)(2,1)S(1)}, bf16[32,1024]{1,0:T(8,128)(2,1)S(1)}, u32[]{:S(2)}, u32[]{:S(2)}) collective-permute-start(bf16[32,1024]{1,0:T(8,128)(2,1)S(1)} %get-tuple-element.52), channel_id=1, source_target_pairs={{0,12},{1,13},{2,14},{3,15},{4,0},{5,1},{6,2},{7,3},{8,4},{9,5},{1... | collective-permute-start | bytes 196616 | tf_op jit(solution)/shard_map/ppermute | solution.py:124
  53.5 4.5 %collective-permute-start.34 = (bf16[32,1152]{1,0:T(8,128)(2,1)S(1)}, bf16[32,1152]{1,0:T(8,128)(2,1)S(1)}, u32[]{:S(2)}, u32[]{:S(2)}) collective-permute-start(bf16[32,1152]{1,0:T(8,128)(2,1)S(1)} %get-tuple-element.36), channel_id=1, source_target_pairs={{0,28},{1,29},{2,30},{3,31},{4,16},{5,17},{6,18},{7,19},{8,20},{9,... | collective-permute-start | bytes 221192 | tf_op jit(solution)/shard_map/ppermute | solution.py:134
  59.6 2.8 %collective-permute-start.32 = (bf16[32,1152]{1,0:T(8,128)(2,1)S(1)}, bf16[32,1152]{1,0:T(8,128)(2,1)S(1)}, u32[]{:S(2)}, u32[]{:S(2)}) collective-permute-start(bf16[32,1152]{1,0:T(8,128)(2,1)S(1)} %get-tuple-element.36), channel_id=1, source_target_pairs={{0,20},{1,21},{2,22},{3,23},{4,24},{5,25},{6,26},{7,27},{8,28},{9,... | collective-permute-start | bytes 221192 | tf_op jit(solution)/shard_map/ppermute | solution.py:134
  63.1 2.2 %collective-permute-start.24 = (bf16[32,1152]{1,0:T(8,128)(2,1)S(1)}, bf16[32,1152]{1,0:T(8,128)(2,1)S(1)}, u32[]{:S(2)}, u32[]{:S(2)}) collective-permute-start(bf16[32,1152]{1,0:T(8,128)(2,1)S(1)} %get-tuple-element.32), channel_id=1, source_target_pairs={{0,28},{1,29},{2,30},{3,31},{4,16},{5,17},{6,18},{7,19},{8,20},{9,... | collective-permute-start | bytes 221192 | tf_op jit(solution)/shard_map/ppermute | solution.py:134
  65.7 2.7 %collective-permute-start.22 = (bf16[32,1152]{1,0:T(8,128)(2,1)S(1)}, bf16[32,1152]{1,0:T(8,128)(2,1)S(1)}, u32[]{:S(2)}, u32[]{:S(2)}) collective-permute-start(bf16[32,1152]{1,0:T(8,128)(2,1)S(1)} %get-tuple-element.32), channel_id=1, source_target_pairs={{0,20},{1,21},{2,22},{3,23},{4,24},{5,25},{6,26},{7,27},{8,28},{9,... | collective-permute-start | bytes 221192 | tf_op jit(solution)/shard_map/ppermute | solution.py:134
  69.2 1.6 %collective-permute-start.35 = (bf16[4,32,1152]{2,1,0:T(8,128)(2,1)S(1)}, bf16[4,32,1152]{2,1,0:T(8,128)(2,1)S(1)}, u32[]{:S(2)}, u32[]{:S(2)}) collective-permute-start(bf16[4,32,1152]{2,1,0:T(8,128)(2,1)S(1)} %pad_maximum_fusion.3.near), channel_id=1, source_target_pairs={{0,2},{1,3},{2,0},{3,1},{4,6},{5,7},{6,4},{7,5},{8,10},{9,11},{10,... | collective-permute-start | bytes 884744 | tf_op jit(solution)/shard_map/ppermute | solution.py:119
  71.5 1.7 %collective-permute-done.23 = bf16[32,1152]{1,0:T(8,128)(2,1)S(1)} collective-permute-done((bf16[32,1152]{1,0:T(8,128)(2,1)S(1)}, bf16[32,1152]{1,0:T(8,128)(2,1)S(1)}, u32[]{:S(2)}, u32[]{:S(2)}) %collective-permute-start.23) | collective-permute-done | bytes 73760 | tf_op jit(solution)/shard_map/ppermute | solution.py:134
  74.7 3.8 %collective-permute-done.35.far = bf16[4,32,1152]{2,1,0:T(8,128)(2,1)S(1)} collective-permute-done((bf16[4,32,1152]{2,1,0:T(8,128)(2,1)S(1)}, bf16[4,32,1152]{2,1,0:T(8,128)(2,1)S(1)}, u32[]{:S(2)}, u32[]{:S(2)}) %collective-permute-start.35) | collective-permute-done | bytes 294944 | tf_op jit(solution)/shard_map/ppermute | solution.py:119
  78.6 2.7 %serve.7 = (f32[4,32,1024]{2,1,0:T(8,128)S(1)}, bf16[4,32,1024]{2,1,0:T(8,128)(2,1)S(1)}) custom-call(bf16[4,32,1152]{2,1,0:T(8,128)(2,1)S(1)} %pad_maximum_fusion.3.near, bf16[4,32,1152]{2,1,0:T(8,128)(2,1)S(1)} %collective-permute-done.35.far, bf16[1,1024,1536]{2,1,0:T(8,128)(2,1)S(1)} %bitcast.102, ...), custom_call_target="tpu_custom_call" | custom-call | flops 2415919104 | bytes 9437184 | tf_op jit(solution)/shard_map/serve/pallas_call | solution.py:187
  81.3 2.0 %collective-permute-start.36 = (bf16[4,32,1024]{2,1,0:T(8,128)(2,1)S(1)}, bf16[4,32,1024]{2,1,0:T(8,128)(2,1)S(1)}, u32[]{:S(2)}, u32[]{:S(2)}) collective-permute-start(bf16[4,32,1024]{2,1,0:T(8,128)(2,1)S(1)} %get-tuple-element.38), channel_id=1, source_target_pairs={{0,2},{1,3},{2,0},{3,1},{4,6},{5,7},{6,4},{7,5},{8,10},{9,11},{10,... | collective-permute-start | bytes 786440 | tf_op jit(solution)/shard_map/ppermute | solution.py:119
  84.8 2.7 %serve.6 = (f32[4,32,1024]{2,1,0:T(8,128)S(1)}, bf16[4,32,1024]{2,1,0:T(8,128)(2,1)S(1)}) custom-call(bf16[4,32,1152]{2,1,0:T(8,128)(2,1)S(1)} %pad_maximum_fusion.2.near, bf16[4,32,1152]{2,1,0:T(8,128)(2,1)S(1)} %collective-permute-done.25.far, bf16[1,1024,1536]{2,1,0:T(8,128)(2,1)S(1)} %bitcast.103, ...), custom_call_target="tpu_custom_call" | custom-call | flops 2415919104 | bytes 9437184 | tf_op jit(solution)/shard_map/serve/pallas_call | solution.py:187
  91.2 2.8 %collective-permute-done.26 = bf16[4,32,1024]{2,1,0:T(8,128)(2,1)S(1)} collective-permute-done((bf16[4,32,1024]{2,1,0:T(8,128)(2,1)S(1)}, bf16[4,32,1024]{2,1,0:T(8,128)(2,1)S(1)}, u32[]{:S(2)}, u32[]{:S(2)}) %collective-permute-start.26) | collective-permute-done | bytes 262176 | tf_op jit(solution)/shard_map/ppermute | solution.py:119
  96.1 1.7 %collective-permute-start.28 = (bf16[32,1024]{1,0:T(8,128)(2,1)S(1)}, bf16[32,1024]{1,0:T(8,128)(2,1)S(1)}, u32[]{:S(2)}, u32[]{:S(2)}) collective-permute-start(bf16[32,1024]{1,0:T(8,128)(2,1)S(1)} %get-tuple-element.49), channel_id=1, source_target_pairs={{0,8},{1,9},{2,10},{3,11},{4,12},{5,13},{6,14},{7,15},{8,0},{9,1},... | collective-permute-start | bytes 196616 | tf_op jit(solution)/shard_map/ppermute | solution.py:124
  97.8 2.2 %collective-permute-start.27 = (bf16[32,1024]{1,0:T(8,128)(2,1)S(1)}, bf16[32,1024]{1,0:T(8,128)(2,1)S(1)}, u32[]{:S(2)}, u32[]{:S(2)}) collective-permute-start(bf16[32,1024]{1,0:T(8,128)(2,1)S(1)} %get-tuple-element.47), channel_id=1, source_target_pairs={{0,12},{1,13},{2,14},{3,15},{4,0},{5,1},{6,2},{7,3},{8,4},{9,5},{1... | collective-permute-start | bytes 196616 | tf_op jit(solution)/shard_map/ppermute | solution.py:124
  (99 shorter events, 35.9 us)
Async XLA Ops:
  0.0 27.2 %collective-permute-start.4 = (bf16[1,1024,1536]{2,1,0:T(8,128)(2,1)}, bf16[1,1024,1536]{2,1,0:T(8,128)(2,1)S(1)}, u32[]{:S(2)}, u32[]{:S(2)}) collective-permute-start(bf16[1,1024,1536]{2,1,0:T(8,128)(2,1)} %bitcast.99), channel_id=1, source_target_pairs={{0,1},{1,0},{2,3},{3,2},{4,5},{5,4},{6,7},{7,6},{8,9},{9,8},{10,11... | collective-permute-start | bytes 9437192 | tf_op jit(solution)/shard_map/ppermute | solution.py:114
  0.5 26.7 %collective-permute-start.5 = (bf16[1,768,1024]{2,1,0:T(8,128)(2,1)}, bf16[1,768,1024]{2,1,0:T(8,128)(2,1)S(1)}, u32[]{:S(2)}, u32[]{:S(2)}) collective-permute-start(bf16[1,768,1024]{2,1,0:T(8,128)(2,1)} %bitcast.104), channel_id=1, source_target_pairs={{0,1},{1,0},{2,3},{3,2},{4,5},{5,4},{6,7},{7,6},{8,9},{9,8},{10,11... | collective-permute-start | bytes 4718600 | tf_op jit(solution)/shard_map/ppermute | solution.py:114
  4.0 7.8 %collective-permute-start.14 = (bf16[32,1152]{1,0:T(8,128)(2,1)S(1)}, bf16[32,1152]{1,0:T(8,128)(2,1)S(1)}, u32[]{:S(2)}, u32[]{:S(2)}) collective-permute-start(bf16[32,1152]{1,0:T(8,128)(2,1)S(1)} %get-tuple-element.27), channel_id=1, source_target_pairs={{0,12},{1,13},{2,14},{3,15},{4,0},{5,1},{6,2},{7,3},{8,4},{9,5},{1... | collective-permute-start | bytes 221192 | tf_op jit(solution)/shard_map/ppermute | solution.py:124
  9.1 8.3 %collective-permute-start.13 = (bf16[32,1152]{1,0:T(8,128)(2,1)S(1)}, bf16[32,1152]{1,0:T(8,128)(2,1)S(1)}, u32[]{:S(2)}, u32[]{:S(2)}) collective-permute-start(bf16[32,1152]{1,0:T(8,128)(2,1)S(1)} %get-tuple-element.27), channel_id=1, source_target_pairs={{0,8},{1,9},{2,10},{3,11},{4,12},{5,13},{6,14},{7,15},{8,0},{9,1},... | collective-permute-start | bytes 221192 | tf_op jit(solution)/shard_map/ppermute | solution.py:124
  9.1 8.3 %collective-permute-start.12 = (bf16[32,1152]{1,0:T(8,128)(2,1)S(1)}, bf16[32,1152]{1,0:T(8,128)(2,1)S(1)}, u32[]{:S(2)}, u32[]{:S(2)}) collective-permute-start(bf16[32,1152]{1,0:T(8,128)(2,1)S(1)} %get-tuple-element.27), channel_id=1, source_target_pairs={{0,4},{1,5},{2,6},{3,7},{4,8},{5,9},{6,10},{7,11},{8,12},{9,13},{1... | collective-permute-start | bytes 221192 | tf_op jit(solution)/shard_map/ppermute | solution.py:124
  22.8 24.5 %collective-permute-start.10 = (f32[1,1024]{1,0:T(1,128)}, f32[1,1024]{1,0:T(1,128)S(1)}, u32[]{:S(2)}, u32[]{:S(2)}) collective-permute-start(f32[1,1024]{1,0:T(1,128)} %gain_hbm.1), channel_id=1, source_target_pairs={{0,16},{16,0},{1,17},{17,1},{2,18},{18,2},{3,19},{19,3},{4,20},{20... | collective-permute-start | bytes 12296 | tf_op jit(solution)/shard_map/ppermute | solution.py:139
  24.3 26.3 %collective-permute-start.11 = (bf16[1,2,32,128]{3,2,1,0:T(8,128)(2,1)S(1)}, bf16[1,2,32,128]{3,2,1,0:T(8,128)(2,1)S(1)}, u32[]{:S(2)}, u32[]{:S(2)}) collective-permute-start(bf16[1,2,32,128]{3,2,1,0:T(8,128)(2,1)S(1)} %get-tuple-element.25), channel_id=1, source_target_pairs={{0,16},{16,0},{1,17},{17,1},{2,18},{18,2},{3,19},{19,3},{4,20},{20... | collective-permute-start | bytes 49160 | tf_op jit(solution)/shard_map/ppermute | solution.py:139
  25.6 8.1 %collective-permute-start.3 = (bf16[4,32,1152]{2,1,0:T(8,128)(2,1)S(1)}, bf16[4,32,1152]{2,1,0:T(8,128)(2,1)S(1)}, u32[]{:S(2)}, u32[]{:S(2)}) collective-permute-start(bf16[4,32,1152]{2,1,0:T(8,128)(2,1)S(1)} %pad_maximum_fusion.near), channel_id=1, source_target_pairs={{0,2},{1,3},{2,0},{3,1},{4,6},{5,7},{6,4},{7,5},{8,10},{9,11},{10,... | collective-permute-start | bytes 884744 | tf_op jit(solution)/shard_map/ppermute | solution.py:119
  33.1 9.2 %collective-permute-start.16 = (bf16[4,32,1024]{2,1,0:T(8,128)(2,1)S(1)}, bf16[4,32,1024]{2,1,0:T(8,128)(2,1)S(1)}, u32[]{:S(2)}, u32[]{:S(2)}) collective-permute-start(bf16[4,32,1024]{2,1,0:T(8,128)(2,1)S(1)} %get-tuple-element.29), channel_id=1, source_target_pairs={{0,2},{1,3},{2,0},{3,1},{4,6},{5,7},{6,4},{7,5},{8,10},{9,11},{10,... | collective-permute-start | bytes 786440 | tf_op jit(solution)/shard_map/ppermute | solution.py:119
  36.5 10.1 %collective-permute-start.6 = (bf16[4,32,1024]{2,1,0:T(8,128)(2,1)S(1)}, bf16[4,32,1024]{2,1,0:T(8,128)(2,1)S(1)}, u32[]{:S(2)}, u32[]{:S(2)}) collective-permute-start(bf16[4,32,1024]{2,1,0:T(8,128)(2,1)S(1)} %get-tuple-element.24), channel_id=1, source_target_pairs={{0,2},{1,3},{2,0},{3,1},{4,6},{5,7},{6,4},{7,5},{8,10},{9,11},{10,... | collective-permute-start | bytes 786440 | tf_op jit(solution)/shard_map/ppermute | solution.py:119
  42.5 9.3 %collective-permute-start.17 = (bf16[32,1024]{1,0:T(8,128)(2,1)S(1)}, bf16[32,1024]{1,0:T(8,128)(2,1)S(1)}, u32[]{:S(2)}, u32[]{:S(2)}) collective-permute-start(bf16[32,1024]{1,0:T(8,128)(2,1)S(1)} %get-tuple-element.58), channel_id=1, source_target_pairs={{0,12},{1,13},{2,14},{3,15},{4,0},{5,1},{6,2},{7,3},{8,4},{9,5},{1... | collective-permute-start | bytes 196616 | tf_op jit(solution)/shard_map/ppermute | solution.py:124
  47.3 12.2 %collective-permute-start.7 = (bf16[32,1024]{1,0:T(8,128)(2,1)S(1)}, bf16[32,1024]{1,0:T(8,128)(2,1)S(1)}, u32[]{:S(2)}, u32[]{:S(2)}) collective-permute-start(bf16[32,1024]{1,0:T(8,128)(2,1)S(1)} %get-tuple-element.52), channel_id=1, source_target_pairs={{0,12},{1,13},{2,14},{3,15},{4,0},{5,1},{6,2},{7,3},{8,4},{9,5},{1... | collective-permute-start | bytes 196616 | tf_op jit(solution)/shard_map/ppermute | solution.py:124
  50.6 11.8 %collective-permute-start.8 = (bf16[32,1024]{1,0:T(8,128)(2,1)S(1)}, bf16[32,1024]{1,0:T(8,128)(2,1)S(1)}, u32[]{:S(2)}, u32[]{:S(2)}) collective-permute-start(bf16[32,1024]{1,0:T(8,128)(2,1)S(1)} %get-tuple-element.51), channel_id=1, source_target_pairs={{0,8},{1,9},{2,10},{3,11},{4,12},{5,13},{6,14},{7,15},{8,0},{9,1},... | collective-permute-start | bytes 196616 | tf_op jit(solution)/shard_map/ppermute | solution.py:124
  51.7 11.2 %collective-permute-start.9 = (bf16[32,1024]{1,0:T(8,128)(2,1)S(1)}, bf16[32,1024]{1,0:T(8,128)(2,1)S(1)}, u32[]{:S(2)}, u32[]{:S(2)}) collective-permute-start(bf16[32,1024]{1,0:T(8,128)(2,1)S(1)} %get-tuple-element.50), channel_id=1, source_target_pairs={{0,4},{1,5},{2,6},{3,7},{4,8},{5,9},{6,10},{7,11},{8,12},{9,13},{1... | collective-permute-start | bytes 196616 | tf_op jit(solution)/shard_map/ppermute | solution.py:124
  53.5 11.8 %collective-permute-start.34 = (bf16[32,1152]{1,0:T(8,128)(2,1)S(1)}, bf16[32,1152]{1,0:T(8,128)(2,1)S(1)}, u32[]{:S(2)}, u32[]{:S(2)}) collective-permute-start(bf16[32,1152]{1,0:T(8,128)(2,1)S(1)} %get-tuple-element.36), channel_id=1, source_target_pairs={{0,28},{1,29},{2,30},{3,31},{4,16},{5,17},{6,18},{7,19},{8,20},{9,... | collective-permute-start | bytes 221192 | tf_op jit(solution)/shard_map/ppermute | solution.py:134
  58.0 7.6 %collective-permute-start.33 = (bf16[32,1152]{1,0:T(8,128)(2,1)S(1)}, bf16[32,1152]{1,0:T(8,128)(2,1)S(1)}, u32[]{:S(2)}, u32[]{:S(2)}) collective-permute-start(bf16[32,1152]{1,0:T(8,128)(2,1)S(1)} %get-tuple-element.36), channel_id=1, source_target_pairs={{0,24},{1,25},{2,26},{3,27},{4,28},{5,29},{6,30},{7,31},{8,16},{9,... | collective-permute-start | bytes 221192 | tf_op jit(solution)/shard_map/ppermute | solution.py:134
  59.6 8.8 %collective-permute-start.32 = (bf16[32,1152]{1,0:T(8,128)(2,1)S(1)}, bf16[32,1152]{1,0:T(8,128)(2,1)S(1)}, u32[]{:S(2)}, u32[]{:S(2)}) collective-permute-start(bf16[32,1152]{1,0:T(8,128)(2,1)S(1)} %get-tuple-element.36), channel_id=1, source_target_pairs={{0,20},{1,21},{2,22},{3,23},{4,24},{5,25},{6,26},{7,27},{8,28},{9,... | collective-permute-start | bytes 221192 | tf_op jit(solution)/shard_map/ppermute | solution.py:134
  63.1 7.7 %collective-permute-start.24 = (bf16[32,1152]{1,0:T(8,128)(2,1)S(1)}, bf16[32,1152]{1,0:T(8,128)(2,1)S(1)}, u32[]{:S(2)}, u32[]{:S(2)}) collective-permute-start(bf16[32,1152]{1,0:T(8,128)(2,1)S(1)} %get-tuple-element.32), channel_id=1, source_target_pairs={{0,28},{1,29},{2,30},{3,31},{4,16},{5,17},{6,18},{7,19},{8,20},{9,... | collective-permute-start | bytes 221192 | tf_op jit(solution)/shard_map/ppermute | solution.py:134
  65.3 7.8 %collective-permute-start.23 = (bf16[32,1152]{1,0:T(8,128)(2,1)S(1)}, bf16[32,1152]{1,0:T(8,128)(2,1)S(1)}, u32[]{:S(2)}, u32[]{:S(2)}) collective-permute-start(bf16[32,1152]{1,0:T(8,128)(2,1)S(1)} %get-tuple-element.32), channel_id=1, source_target_pairs={{0,24},{1,25},{2,26},{3,27},{4,28},{5,29},{6,30},{7,31},{8,16},{9,... | collective-permute-start | bytes 221192 | tf_op jit(solution)/shard_map/ppermute | solution.py:134
  69.2 9.4 %collective-permute-start.35 = (bf16[4,32,1152]{2,1,0:T(8,128)(2,1)S(1)}, bf16[4,32,1152]{2,1,0:T(8,128)(2,1)S(1)}, u32[]{:S(2)}, u32[]{:S(2)}) collective-permute-start(bf16[4,32,1152]{2,1,0:T(8,128)(2,1)S(1)} %pad_maximum_fusion.3.near), channel_id=1, source_target_pairs={{0,2},{1,3},{2,0},{3,1},{4,6},{5,7},{6,4},{7,5},{8,10},{9,11},{10,... | collective-permute-start | bytes 884744 | tf_op jit(solution)/shard_map/ppermute | solution.py:119
  70.8 24.5 %collective-permute-start.30 = (bf16[32,1024]{1,0:T(8,128)(2,1)S(1)}, bf16[32,1024]{1,0:T(8,128)(2,1)S(1)}, u32[]{:S(2)}, u32[]{:S(2)}) collective-permute-start(bf16[32,1024]{1,0:T(8,128)(2,1)S(1)} %get-tuple-element.35), channel_id=1, source_target_pairs={{0,16},{1,17},{2,18},{3,19},{4,20},{5,21},{6,22},{7,23},{8,24},{9,... | collective-permute-start | bytes 196616 | tf_op jit(solution)/shard_map/ppermute | solution.py:134
  73.2 26.9 %collective-permute-start.20 = (bf16[32,1024]{1,0:T(8,128)(2,1)S(1)}, bf16[32,1024]{1,0:T(8,128)(2,1)S(1)}, u32[]{:S(2)}, u32[]{:S(2)}) collective-permute-start(bf16[32,1024]{1,0:T(8,128)(2,1)S(1)} %get-tuple-element.31), channel_id=1, source_target_pairs={{0,16},{1,17},{2,18},{3,19},{4,20},{5,21},{6,22},{7,23},{8,24},{9,... | collective-permute-start | bytes 196616 | tf_op jit(solution)/shard_map/ppermute | solution.py:134
  73.9 10.9 %collective-permute-start.25 = (bf16[4,32,1152]{2,1,0:T(8,128)(2,1)S(1)}, bf16[4,32,1152]{2,1,0:T(8,128)(2,1)S(1)}, u32[]{:S(2)}, u32[]{:S(2)}) collective-permute-start(bf16[4,32,1152]{2,1,0:T(8,128)(2,1)S(1)} %pad_maximum_fusion.2.near), channel_id=1, source_target_pairs={{0,2},{1,3},{2,0},{3,1},{4,6},{5,7},{6,4},{7,5},{8,10},{9,11},{10,... | collective-permute-start | bytes 884744 | tf_op jit(solution)/shard_map/ppermute | solution.py:119
  81.3 7.6 %collective-permute-start.36 = (bf16[4,32,1024]{2,1,0:T(8,128)(2,1)S(1)}, bf16[4,32,1024]{2,1,0:T(8,128)(2,1)S(1)}, u32[]{:S(2)}, u32[]{:S(2)}) collective-permute-start(bf16[4,32,1024]{2,1,0:T(8,128)(2,1)S(1)} %get-tuple-element.38), channel_id=1, source_target_pairs={{0,2},{1,3},{2,0},{3,1},{4,6},{5,7},{6,4},{7,5},{8,10},{9,11},{10,... | collective-permute-start | bytes 786440 | tf_op jit(solution)/shard_map/ppermute | solution.py:119
  (24 other events, 138.8 us)

commit v2 on v1

--- a/solution.py
+++ b/solution.py
@@ -16,24 +16,8 @@
     return (widened * inverse_rms * gain_row).astype(jnp.bfloat16)
 
 
-def first_kernel(
-    experts_all, inflow_hbm, gain_hbm, ids_hbm, weights_hbm, *refs
-):
-    inflow, gain, ids, weights, sem = refs[-5:]
-    payloads, later = refs[:-6], refs[-6]
-    copies = [
-        pltpu.make_async_copy(source, target, sem.at[number])
-        for number, (source, target) in enumerate(
-            ((ids_hbm, ids), (weights_hbm, weights), (inflow_hbm, inflow), (gain_hbm, gain))
-        )
-    ]
-    for copy in copies:
-        copy.start()
-    for copy in copies:
-        copy.wait()
+def token_weights(experts_all, width, ids, weights):
     steps, micro_count, top_count, tokens = ids.shape
-    features = inflow.shape[-1]
-    width = later.shape[-1]
     expert = lax.broadcasted_iota(jnp.int32, (experts_all, tokens), 0)
     columns = []
     for step in range(steps):
@@ -46,38 +30,93 @@
             empty = jnp.zeros((width - 2 * experts_all, tokens), jnp.float32)
             columns.append(jnp.concatenate([high, dense - high, empty], axis=0))
     tails = jnp.concatenate(columns, axis=1).T.astype(jnp.bfloat16)
-    tails = tails.reshape(steps, micro_count, tokens, width)
+    return tails.reshape(steps, micro_count, tokens, width)
+
+
+def first_kernel(
+    experts_all, inflow_hbm, gain_hbm, ids_hbm, weights_hbm, *refs
+):
+    payloads, (inflow, gain, ids, weights, sem) = refs[:-5], refs[-5:]
+    copies = [
+        pltpu.make_async_copy(source, target, sem.at[number])
+        for number, (source, target) in enumerate(
+            (
+                (ids_hbm.at[pl.ds(0, 1)], ids),
+                (weights_hbm.at[pl.ds(0, 1)], weights),
+                (inflow_hbm, inflow),
+                (gain_hbm, gain),
+            )
+        )
+    ]
+    for copy in copies:
+        copy.start()
+    for copy in copies:
+        copy.wait()
+    features = inflow.shape[-1]
+    width = payloads[0].shape[-1] - features
+    tails = token_weights(experts_all, width, ids, weights)
     for micro, payload in enumerate(payloads):
         payload[:, :features] = normalize(inflow[micro], gain[...])
         payload[:, features:] = tails[0, micro]
-    later[...] = tails[1:]
-
-
-def first_payload(inflow, gain, ids, weights, experts_all):
+
+
+def first_payload(inflow, gain, ids, weights, experts_all, width):
     micro_count, tokens, features = inflow.shape
-    steps = ids.shape[0]
-    width = -(-2 * experts_all // LANES) * LANES
     return pl.pallas_call(
         functools.partial(first_kernel, experts_all),
-        out_shape=(jax.ShapeDtypeStruct((tokens, features + width), jnp.bfloat16),) * micro_count
-        + (jax.ShapeDtypeStruct((steps - 1, micro_count, tokens, width), jnp.bfloat16),),
+        out_shape=(jax.ShapeDtypeStruct((tokens, features + width), jnp.bfloat16),) * micro_count,
         in_specs=[pl.BlockSpec(memory_space=pltpu.HBM)] * 4,
-        out_specs=[pl.BlockSpec(memory_space=pltpu.VMEM)] * (micro_count + 1),
+        out_specs=[pl.BlockSpec(memory_space=pltpu.VMEM)] * micro_count,
         scratch_shapes=[
             pltpu.VMEM(inflow.shape, inflow.dtype),
             pltpu.VMEM(gain.shape, gain.dtype),
-            pltpu.VMEM(ids.shape, ids.dtype),
-            pltpu.VMEM(weights.shape, weights.dtype),
+            pltpu.VMEM((1,) + ids.shape[1:], ids.dtype),
+            pltpu.VMEM((1,) + weights.shape[1:], weights.dtype),
             pltpu.SemaphoreType.DMA((4,)),
         ],
-        compiler_params=pltpu.CompilerParams(vmem_limit_bytes=8 * 1024 * 1024),
+        compiler_params=pltpu.CompilerParams(vmem_limit_bytes=60 * 1024 * 1024),
         name="first_payload",
     )(inflow, gain, ids, weights)
 
 
+def later_kernel(experts_all, after, own_in, own_out, ids, weights, gain, later):
+    del after, own_in, own_out
+    steps, micro_count, _, tokens = ids.shape
+    made = token_weights(experts_all, later.shape[-1], ids, weights)[1:]
+    at = (steps - 1) * micro_count * tokens
+    later[:at] = made.reshape(at, later.shape[-1])
+    width = later.shape[-1]
+    pieces = gain.shape[-1] // width
+    rest = jnp.concatenate(
+        [gain[:, piece * width : (piece + 1) * width] for piece in range(pieces)], axis=0
+    )
+    for part in range(3):
+        rounded = rest.astype(jnp.bfloat16)
+        later[at + part * pieces : at + (part + 1) * pieces] = rounded
+        rest = rest - rounded.astype(jnp.float32)
+
+
+def later_rows(after, own_in, own_out, ids, weights, gain, experts_all, width):
+    steps, micro_count, _, tokens = ids.shape
+    rows = (steps - 1) * micro_count * tokens + 3 * gain.shape[-1] // width
+    whole = pl.BlockSpec(memory_space=pltpu.VMEM)
+    return pl.pallas_call(
+        functools.partial(later_kernel, experts_all),
+        out_shape=jax.ShapeDtypeStruct((rows, width), jnp.bfloat16),
+        in_specs=[pl.BlockSpec(memory_space=pl.ANY)] + [whole] * 5,
+        out_specs=whole,
+        compiler_params=pltpu.CompilerParams(
+            vmem_limit_bytes=2 * (own_in.size + own_out.size) + 8 * 1024 * 1024
+        ),
+        name="later_rows",
+    )(after, own_in, own_out, ids, weights, gain)
+
+
 def leave_kernel(step, micro, inflow, own, *refs):
-    parts, (fresh, gain, tail, out, leaving, payload) = refs[:-6], refs[-6:]
-    features = inflow.shape[-1]
+    parts, (fresh, later, out, leaving, payload) = refs[:-5], refs[-5:]
+    tokens, features = own.shape
+    width = later.shape[-1]
+    micro_count = fresh.shape[1]
     total = inflow[...].reshape(own.shape).astype(jnp.float32) + own[...]
     for part in parts:
         total = total + part[...].astype(jnp.float32)
@@ -87,11 +126,20 @@
     arrived = fresh[step, micro].astype(jnp.float32)
     gone = jnp.where(is_last, arrived, result.astype(jnp.float32))
     leaving[...] = gone.astype(jnp.bfloat16)
-    payload[:, :features] = normalize(gone, gain[...])
-    payload[:, features:] = tail[step, micro]
-
-
-def leave(step, micro, inflow, own, parts, fresh, gain, tail):
+    pieces = features // width
+    at = later.shape[0] - 3 * pieces
+    parts = [
+        later[at + part * pieces : at + (part + 1) * pieces].astype(jnp.float32)
+        for part in range(3)
+    ]
+    gain = parts[0] + parts[1] + parts[2]
+    gain = jnp.concatenate([gain[piece : piece + 1] for piece in range(pieces)], axis=1)
+    payload[:, :features] = normalize(gone, gain)
+    first = (step * micro_count + micro) * tokens
+    payload[:, features:] = later[first : first + tokens]
+
+
+def leave(step, micro, inflow, own, parts, fresh, later):
     tokens, features = own.shape
     whole = pl.BlockSpec(memory_space=pltpu.VMEM)
     rows = jax.ShapeDtypeStruct((tokens, features), jnp.bfloat16)
@@ -100,13 +148,13 @@
         out_shape=(
             rows,
             rows,
-            jax.ShapeDtypeStruct((tokens, features + tail.shape[-1]), jnp.bfloat16),
-        ),
-        in_specs=[whole] * (5 + len(parts)),
+            jax.ShapeDtypeStruct((tokens, features + later.shape[-1]), jnp.bfloat16),
+        ),
+        in_specs=[whole] * (4 + len(parts)),
         out_specs=[whole] * 3,
         compiler_params=pltpu.CompilerParams(vmem_limit_bytes=8 * 1024 * 1024),
         name="leave",
-    )(inflow, own, *parts, fresh, gain, tail)
+    )(inflow, own, *parts, fresh, later)
 
 
 def swap_core(value):
@@ -119,15 +167,15 @@
     return lax.ppermute(value, "expert", [(i, i ^ 2) for i in range(size)])
 
 
-def rotate_outer(value, by):
+def swap_outer(value, by):
     size = lax.axis_size("expert")
-    return lax.ppermute(value, "expert", [(i, (i + 4 * by) % size) for i in range(size)])
+    return lax.ppermute(value, "expert", [(i, i ^ 4 * by) for i in range(size)])
 
 
 def next_section(value, by):
     sections, size = lax.axis_size("section"), lax.axis_size("expert")
     pairs = [
-        (s * size + i, (s + 1) % sections * size + (i + 4 * by) % size)
+        (s * size + i, (s + 1) % sections * size + (i ^ 4 * by))
         for s in range(sections)
         for i in range(size)
     ]
@@ -215,17 +263,17 @@
     experts_all = owners * local_count
     steps = expert_ids.shape[0]
     micro_count = in_flight.shape[1]
+    width = -(-2 * experts_all // LANES) * LANES
+    ids = jnp.swapaxes(expert_ids[:, 0], -1, -2)
+    weights = jnp.swapaxes(route_weights[:, 0], -1, -2)
+    payloads = first_payload(in_flight[0], norm_gain, ids, weights, experts_all, width)
+    *payloads, gate_up, w_down = lax.optimization_barrier((*payloads, gate_up, w_down))
     own_in, own_out = gate_up[0], w_down[0]
     far_in, far_out = swap_core(own_in), swap_core(own_out)
-    *payloads, tails = first_payload(
-        in_flight[0],
-        norm_gain,
-        jnp.swapaxes(expert_ids[:, 0], -1, -2),
-        jnp.swapaxes(route_weights[:, 0], -1, -2),
-        experts_all,
+    later = later_rows(
+        payloads[0], own_in, own_out, ids, weights, norm_gain, experts_all, width
     )
-    later_gain = previous_section(norm_gain)
-    later_tails = previous_section(tails)
+    later = previous_section(later)
     inflows = [in_flight[0, micro] for micro in range(micro_count)]
     outputs = []
     for step in range(steps):
@@ -233,18 +281,23 @@
         for micro in range(micro_count):
             payload, inflow = payloads[micro], inflows[micro]
             if step == 0:
-                near = jnp.stack([payload] + [rotate_outer(payload, by) for by in range(1, outer)])
+                near = jnp.stack([payload] + [swap_outer(payload, by) for by in range(1, outer)])
+                if micro == micro_count - 1:
+                    near, far_in, far_out = lax.optimization_barrier((near, far_in, far_out))
             else:
                 near = jnp.stack([next_section(payload, by) for by in range(outer)])
             far = swap_inner(near)
+            if step > 0:
+                far, inflow = lax.optimization_barrier((far, inflow))
             near_sum, far_sum = serve(near, far, own_in, far_in, own_out, far_out, experts_all)
-            served = near_sum + swap_inner(far_sum).astype(jnp.float32)
-            parts = [
-                rotate_outer(served[by].astype(jnp.bfloat16), -by) for by in range(1, outer)
-            ]
+            returned = swap_inner(far_sum)
+            if step == 0 and micro == 0:
+                returned, later = lax.optimization_barrier((returned, later))
+            served = near_sum + returned.astype(jnp.float32)
+            parts = [swap_outer(served[by].astype(jnp.bfloat16), by) for by in range(1, outer)]
             if step < steps - 1:
                 result, leaving, payloads[micro] = leave(
-                    step, micro, inflow, served[0], parts, arriving, later_gain, later_tails
+                    step, micro, inflow, served[0], parts, arriving, later
                 )
                 inflows[micro] = next_section(leaving, 0)
             else:

time: 104 us -> 114 us (1.096)
  waiting for transfers between devices: 24.5 us -> 41.1 us
  starting transfers between devices: 59.5 us -> 50.9 us
    ppermute x18, waiting for transfers between devices: 8.51 us -> 21 us  [swap_outer(): return lax.ppermute(value, 'expert', [(i, i ^ 4 * by) for i in range(size)])]
    ppermute x8, starting transfers between devices: 11.2 us -> 6.87 us  [swap_inner(): return lax.ppermute(value, 'expert', [(i, i ^ 2) for i in range(size)])]
    ppermute x10, waiting for transfers between devices: 3.13 us -> 5.58 us  [next_section(): return lax.ppermute(value, ('section', 'expert'), pairs)]
    ppermute x18, starting transfers between devices: 30.2 us -> 27.8 us  [swap_outer(): return lax.ppermute(value, 'expert', [(i, i ^ 4 * by) for i in range(size)])]
    ppermute x8, waiting for transfers between devices: 12.9 us -> 14.6 us  [swap_inner(): return lax.ppermute(value, 'expert', [(i, i ^ 2) for i in range(size)])]
    ppermute x10, starting transfers between devices: 15.3 us -> 14.1 us  [next_section(): return lax.ppermute(value, ('section', 'expert'), pairs)]
    unnamed x16 -> x22, local copies, waits for them, and re-layouts: 5.65 us -> 6.32 us
  transfers between devices with their start and end apart: 40 -> 39, of which waited for: 15 -> 18; matrix products, arithmetic and copies ran while one was open for 1% -> 1% of each run, Pallas kernels for 12% -> 10%
where the time goes in v2:
time: 114 us
  starting transfers between devices  50.9 us (45%)
  waiting for transfers between devices  41.1 us (36%)
  Pallas kernels  12.8 us (11%)
  local copies, waits for them, and re-layouts  6.41 us (6%)
  other arithmetic  2.22 us (2%)
    ppermute x18, starting transfers between devices, swap_outer(): return lax.ppermute(value, 'expert', [(i, i ^ 4 * by) for i in range(size)])  27.8 us
    ppermute x18, waiting for transfers between devices, swap_outer(): return lax.ppermute(value, 'expert', [(i, i ^ 4 * by) for i in range(size)])  21 us
    ppermute x8, waiting for transfers between devices, swap_inner(): return lax.ppermute(value, 'expert', [(i, i ^ 2) for i in range(size)])  14.6 us
    ppermute x10, starting transfers between devices, next_section(): return lax.ppermute(value, ('section', 'expert'), pairs)  14.1 us
    pallas_call x4, Pallas kernels, serve(): pl.pallas_call(functools.partial(serve_kernel, features, hidden_count, ch...  10.6 us
    ppermute x8, starting transfers between devices, swap_inner(): return lax.ppermute(value, 'expert', [(i, i ^ 2) for i in range(size)])  6.87 us
    unnamed x22, local copies, waits for them, and re-layouts  6.32 us
    ppermute x10, waiting for transfers between devices, next_section(): return lax.ppermute(value, ('section', 'expert'), pairs)  5.58 us
  transfers between devices with their start and end apart: 39, of which 18 were waited for; matrix products, arithmetic and copies ran while one was open for 1% of the time, Pallas kernels for 10%

profile of v2, /device:TPU:0, one launch (start us, length us, event | category | flops | bytes accessed | tf_op | source)
XLA Modules:
  0.0 113.8 jit_solution(7705627976999816435)
XLA Ops:
  2.4 3.0 %collective-permute-start = (bf16[32,1152]{1,0:T(8,128)(2,1)}, bf16[32,1152]{1,0:T(8,128)(2,1)S(1)}, u32[]{:S(2)}, u32[]{:S(2)}) collective-permute-start(bf16[32,1152]{1,0:T(8,128)(2,1)} %get-tuple-element.36.after), channel_id=1, source_target_pairs={{0,4},{1,5},{2,6},{3,7},{4,0},{5,1},{6,2},{7,3},{8,12},{9,13},{10,... | collective-permute-start | bytes 221192 | tf_op jit(solution)/shard_map/ppermute | solution.py:172
  5.4 2.6 %collective-permute-start.1 = (bf16[32,1152]{1,0:T(8,128)(2,1)}, bf16[32,1152]{1,0:T(8,128)(2,1)S(1)}, u32[]{:S(2)}, u32[]{:S(2)}) collective-permute-start(bf16[32,1152]{1,0:T(8,128)(2,1)} %get-tuple-element.36.after), channel_id=1, source_target_pairs={{0,8},{1,9},{2,10},{3,11},{4,12},{5,13},{6,14},{7,15},{8,0},{9,1},... | collective-permute-start | bytes 221192 | tf_op jit(solution)/shard_map/ppermute | solution.py:172
  8.1 5.5 %collective-permute-done.1 = bf16[32,1152]{1,0:T(8,128)(2,1)S(1)} collective-permute-done((bf16[32,1152]{1,0:T(8,128)(2,1)}, bf16[32,1152]{1,0:T(8,128)(2,1)S(1)}, u32[]{:S(2)}, u32[]{:S(2)}) %collective-permute-start.1) | collective-permute-done | bytes 73760 | tf_op jit(solution)/shard_map/ppermute | solution.py:172
  29.5 2.7 %serve.4 = (f32[4,32,1024]{2,1,0:T(8,128)S(1)}, bf16[4,32,1024]{2,1,0:T(8,128)(2,1)S(1)}) custom-call(bf16[4,32,1152]{2,1,0:T(8,128)(2,1)S(1)} %pad_maximum_fusion.near, bf16[4,32,1152]{2,1,0:T(8,128)(2,1)S(1)} %collective-permute-done.3.far, bf16[1,1024,1536]{2,1,0:T(8,128)(2,1)S(1)} %bitcast.101, bf16[1,1024,1536]{2,1,0:T(8,128)(2,1)S(1)} %collective-permute-done.4.far_in, ...), custom_call_target="tpu_custom_call" | custom-call | flops 2415919104 | bytes 9437184 | tf_op jit(solution)/shard_map/serve/pallas_call | solution.py:235
  34.4 6.8 %collective-permute-done.6 = bf16[4,32,1024]{2,1,0:T(8,128)(2,1)S(1)} collective-permute-done((bf16[4,32,1024]{2,1,0:T(8,128)(2,1)S(1)}, bf16[4,32,1024]{2,1,0:T(8,128)(2,1)S(1)}, u32[]{:S(2)}, u32[]{:S(2)}) %collective-permute-start.6) | collective-permute-done | bytes 262176 | tf_op jit(solution)/shard_map/ppermute | solution.py:167
  43.4 2.4 %collective-permute-start.9 = (bf16[32,1024]{1,0:T(8,128)(2,1)S(1)}, bf16[32,1024]{1,0:T(8,128)(2,1)S(1)}, u32[]{:S(2)}, u32[]{:S(2)}) collective-permute-start(bf16[32,1024]{1,0:T(8,128)(2,1)S(1)} %get-tuple-element.75), channel_id=1, source_target_pairs={{0,8},{1,9},{2,10},{3,11},{4,12},{5,13},{6,14},{7,15},{8,0},{9,1},... | collective-permute-start | bytes 196616 | tf_op jit(solution)/shard_map/ppermute | solution.py:172
  45.8 2.4 %collective-permute-done.10.refs_2_ = bf16[32,1024]{1,0:T(8,128)(2,1)S(1)} collective-permute-done((bf16[32,1024]{1,0:T(8,128)(2,1)S(1)}, bf16[32,1024]{1,0:T(8,128)(2,1)S(1)}, u32[]{:S(2)}, u32[]{:S(2)}) %collective-permute-start.10) | collective-permute-done | bytes 65568 | tf_op jit(solution)/shard_map/ppermute | solution.py:172
  49.3 2.4 %collective-permute-done.9.refs_1_ = bf16[32,1024]{1,0:T(8,128)(2,1)S(1)} collective-permute-done((bf16[32,1024]{1,0:T(8,128)(2,1)S(1)}, bf16[32,1024]{1,0:T(8,128)(2,1)S(1)}, u32[]{:S(2)}, u32[]{:S(2)}) %collective-permute-start.9) | collective-permute-done | bytes 65568 | tf_op jit(solution)/shard_map/ppermute | solution.py:172
  52.8 2.8 %collective-permute-start.21 = (bf16[32,1152]{1,0:T(8,128)(2,1)S(1)}, bf16[32,1152]{1,0:T(8,128)(2,1)S(1)}, u32[]{:S(2)}, u32[]{:S(2)}) collective-permute-start(bf16[32,1152]{1,0:T(8,128)(2,1)S(1)} %get-tuple-element.51), channel_id=1, source_target_pairs={{0,24},{1,25},{2,26},{3,27},{4,28},{5,29},{6,30},{7,31},{8,16},{9,... | collective-permute-start | bytes 221192 | tf_op jit(solution)/shard_map/ppermute | solution.py:182
  55.6 3.1 %collective-permute-start.22 = (bf16[32,1152]{1,0:T(8,128)(2,1)S(1)}, bf16[32,1152]{1,0:T(8,128)(2,1)S(1)}, u32[]{:S(2)}, u32[]{:S(2)}) collective-permute-start(bf16[32,1152]{1,0:T(8,128)(2,1)S(1)} %get-tuple-element.51), channel_id=1, source_target_pairs={{0,28},{1,29},{2,30},{3,31},{4,24},{5,25},{6,26},{7,27},{8,20},{9,... | collective-permute-start | bytes 221192 | tf_op jit(solution)/shard_map/ppermute | solution.py:182
  58.7 2.6 %serve.5 = (f32[4,32,1024]{2,1,0:T(8,128)S(1)}, bf16[4,32,1024]{2,1,0:T(8,128)(2,1)S(1)}) custom-call(bf16[4,32,1152]{2,1,0:T(8,128)(2,1)S(1)} %pad_maximum_fusion.1.near, bf16[4,32,1152]{2,1,0:T(8,128)(2,1)S(1)} %collective-permute-done.14.far, bf16[1,1024,1536]{2,1,0:T(8,128)(2,1)S(1)} %bitcast.102, ...), custom_call_target="tpu_custom_call" | custom-call | flops 2415919104 | bytes 9437184 | tf_op jit(solution)/shard_map/serve/pallas_call | solution.py:235
  63.8 4.0 %collective-permute-done.15 = bf16[4,32,1024]{2,1,0:T(8,128)(2,1)S(1)} collective-permute-done((bf16[4,32,1024]{2,1,0:T(8,128)(2,1)S(1)}, bf16[4,32,1024]{2,1,0:T(8,128)(2,1)S(1)}, u32[]{:S(2)}, u32[]{:S(2)}) %collective-permute-start.15) | collective-permute-done | bytes 262176 | tf_op jit(solution)/shard_map/ppermute | solution.py:167
  68.0 2.4 %collective-permute-start.17 = (bf16[32,1024]{1,0:T(8,128)(2,1)S(1)}, bf16[32,1024]{1,0:T(8,128)(2,1)S(1)}, u32[]{:S(2)}, u32[]{:S(2)}) collective-permute-start(bf16[32,1024]{1,0:T(8,128)(2,1)S(1)} %get-tuple-element.81), channel_id=1, source_target_pairs={{0,8},{1,9},{2,10},{3,11},{4,12},{5,13},{6,14},{7,15},{8,0},{9,1},... | collective-permute-start | bytes 196616 | tf_op jit(solution)/shard_map/ppermute | solution.py:172
  70.4 2.0 %collective-permute-start.18 = (bf16[32,1024]{1,0:T(8,128)(2,1)S(1)}, bf16[32,1024]{1,0:T(8,128)(2,1)S(1)}, u32[]{:S(2)}, u32[]{:S(2)}) collective-permute-start(bf16[32,1024]{1,0:T(8,128)(2,1)S(1)} %get-tuple-element.80), channel_id=1, source_target_pairs={{0,12},{1,13},{2,14},{3,15},{4,8},{5,9},{6,10},{7,11},{8,4},{9,5},... | collective-permute-start | bytes 196616 | tf_op jit(solution)/shard_map/ppermute | solution.py:172
  77.7 2.6 %collective-permute-start.31 = (bf16[32,1152]{1,0:T(8,128)(2,1)S(1)}, bf16[32,1152]{1,0:T(8,128)(2,1)S(1)}, u32[]{:S(2)}, u32[]{:S(2)}) collective-permute-start(bf16[32,1152]{1,0:T(8,128)(2,1)S(1)} %get-tuple-element.57), channel_id=1, source_target_pairs={{0,24},{1,25},{2,26},{3,27},{4,28},{5,29},{6,30},{7,31},{8,16},{9,... | collective-permute-start | bytes 221192 | tf_op jit(solution)/shard_map/ppermute | solution.py:182
  80.3 3.1 %collective-permute-start.32 = (bf16[32,1152]{1,0:T(8,128)(2,1)S(1)}, bf16[32,1152]{1,0:T(8,128)(2,1)S(1)}, u32[]{:S(2)}, u32[]{:S(2)}) collective-permute-start(bf16[32,1152]{1,0:T(8,128)(2,1)S(1)} %get-tuple-element.57), channel_id=1, source_target_pairs={{0,28},{1,29},{2,30},{3,31},{4,24},{5,25},{6,26},{7,27},{8,20},{9,... | collective-permute-start | bytes 221192 | tf_op jit(solution)/shard_map/ppermute | solution.py:182
  83.9 4.1 %collective-permute-done.32 = bf16[32,1152]{1,0:T(8,128)(2,1)S(1)} collective-permute-done((bf16[32,1152]{1,0:T(8,128)(2,1)S(1)}, bf16[32,1152]{1,0:T(8,128)(2,1)S(1)}, u32[]{:S(2)}, u32[]{:S(2)}) %collective-permute-start.32) | collective-permute-done | bytes 73760 | tf_op jit(solution)/shard_map/ppermute | solution.py:182
  88.1 2.6 %serve.6 = (f32[4,32,1024]{2,1,0:T(8,128)S(1)}, bf16[4,32,1024]{2,1,0:T(8,128)(2,1)S(1)}) custom-call(bf16[4,32,1152]{2,1,0:T(8,128)(2,1)S(1)} %pad_maximum_fusion.2.near, bf16[4,32,1152]{2,1,0:T(8,128)(2,1)S(1)} %collective-permute-done.23.far, bf16[1,1024,1536]{2,1,0:T(8,128)(2,1)S(1)} %bitcast.103, ...), custom_call_target="tpu_custom_call" | custom-call | flops 2415919104 | bytes 9437184 | tf_op jit(solution)/shard_map/serve/pallas_call | solution.py:235
  90.8 2.1 %collective-permute-start.25 = (bf16[4,32,1024]{2,1,0:T(8,128)(2,1)S(1)}, bf16[4,32,1024]{2,1,0:T(8,128)(2,1)S(1)}, u32[]{:S(2)}, u32[]{:S(2)}) collective-permute-start(bf16[4,32,1024]{2,1,0:T(8,128)(2,1)S(1)} %get-tuple-element.56), channel_id=1, source_target_pairs={{0,2},{1,3},{2,0},{3,1},{4,6},{5,7},{6,4},{7,5},{8,10},{9,11},{10,... | collective-permute-start | bytes 786440 | tf_op jit(solution)/shard_map/ppermute | solution.py:167
  92.9 2.0 %collective-permute-done.33.far = bf16[4,32,1152]{2,1,0:T(8,128)(2,1)S(1)} collective-permute-done((bf16[4,32,1152]{2,1,0:T(8,128)(2,1)S(1)}, bf16[4,32,1152]{2,1,0:T(8,128)(2,1)S(1)}, u32[]{:S(2)}, u32[]{:S(2)}) %collective-permute-start.33) | collective-permute-done | bytes 294944 | tf_op jit(solution)/shard_map/ppermute | solution.py:167
  94.8 2.6 %serve.7 = (f32[4,32,1024]{2,1,0:T(8,128)S(1)}, bf16[4,32,1024]{2,1,0:T(8,128)(2,1)S(1)}) custom-call(bf16[4,32,1152]{2,1,0:T(8,128)(2,1)S(1)} %pad_maximum_fusion.3.near, bf16[4,32,1152]{2,1,0:T(8,128)(2,1)S(1)} %collective-permute-done.33.far, bf16[1,1024,1536]{2,1,0:T(8,128)(2,1)S(1)} %bitcast.104, ...), custom_call_target="tpu_custom_call" | custom-call | flops 2415919104 | bytes 9437184 | tf_op jit(solution)/shard_map/serve/pallas_call | solution.py:235
  97.8 2.9 %collective-permute-start.27 = (bf16[32,1024]{1,0:T(8,128)(2,1)S(1)}, bf16[32,1024]{1,0:T(8,128)(2,1)S(1)}, u32[]{:S(2)}, u32[]{:S(2)}) collective-permute-start(bf16[32,1024]{1,0:T(8,128)(2,1)S(1)} %get-tuple-element.73), channel_id=1, source_target_pairs={{0,8},{1,9},{2,10},{3,11},{4,12},{5,13},{6,14},{7,15},{8,0},{9,1},... | collective-permute-start | bytes 196616 | tf_op jit(solution)/shard_map/ppermute | solution.py:172
  104.1 2.9 %collective-permute-start.37 = (bf16[32,1024]{1,0:T(8,128)(2,1)S(1)}, bf16[32,1024]{1,0:T(8,128)(2,1)S(1)}, u32[]{:S(2)}, u32[]{:S(2)}) collective-permute-start(bf16[32,1024]{1,0:T(8,128)(2,1)S(1)} %get-tuple-element.79), channel_id=1, source_target_pairs={{0,8},{1,9},{2,10},{3,11},{4,12},{5,13},{6,14},{7,15},{8,0},{9,1},... | collective-permute-start | bytes 196616 | tf_op jit(solution)/shard_map/ppermute | solution.py:172
  109.3 3.7 %collective-permute-done.38 = bf16[32,1024]{1,0:T(8,128)(2,1)S(1)} collective-permute-done((bf16[32,1024]{1,0:T(8,128)(2,1)S(1)}, bf16[32,1024]{1,0:T(8,128)(2,1)S(1)}, u32[]{:S(2)}, u32[]{:S(2)}) %collective-permute-start.38) | collective-permute-done | bytes 65568 | tf_op jit(solution)/shard_map/ppermute | solution.py:172
  (104 shorter events, 40.1 us)
Async XLA Ops:
  1.8 27.7 %collective-permute-start.4 = (bf16[1,1024,1536]{2,1,0:T(8,128)(2,1)}, bf16[1,1024,1536]{2,1,0:T(8,128)(2,1)S(1)}, u32[]{:S(2)}, u32[]{:S(2)}) collective-permute-start(bf16[1,1024,1536]{2,1,0:T(8,128)(2,1)} %bitcast.99), channel_id=1, source_target_pairs={{0,1},{1,0},{2,3},{3,2},{4,5},{5,4},{6,7},{7,6},{8,9},{9,8},{10,11... | collective-permute-start | bytes 9437192 | tf_op jit(solution)/shard_map/ppermute | solution.py:162
  2.3 25.6 %collective-permute-start.5 = (bf16[1,768,1024]{2,1,0:T(8,128)(2,1)}, bf16[1,768,1024]{2,1,0:T(8,128)(2,1)S(1)}, u32[]{:S(2)}, u32[]{:S(2)}) collective-permute-start(bf16[1,768,1024]{2,1,0:T(8,128)(2,1)} %bitcast.105), channel_id=1, source_target_pairs={{0,1},{1,0},{2,3},{3,2},{4,5},{5,4},{6,7},{7,6},{8,9},{9,8},{10,11... | collective-permute-start | bytes 4718600 | tf_op jit(solution)/shard_map/ppermute | solution.py:162
  5.4 8.2 %collective-permute-start.1 = (bf16[32,1152]{1,0:T(8,128)(2,1)}, bf16[32,1152]{1,0:T(8,128)(2,1)S(1)}, u32[]{:S(2)}, u32[]{:S(2)}) collective-permute-start(bf16[32,1152]{1,0:T(8,128)(2,1)} %get-tuple-element.36.after), channel_id=1, source_target_pairs={{0,8},{1,9},{2,10},{3,11},{4,12},{5,13},{6,14},{7,15},{8,0},{9,1},... | collective-permute-start | bytes 221192 | tf_op jit(solution)/shard_map/ppermute | solution.py:172
  15.4 11.1 %collective-permute-start.3 = (bf16[4,32,1152]{2,1,0:T(8,128)(2,1)S(1)}, bf16[4,32,1152]{2,1,0:T(8,128)(2,1)S(1)}, u32[]{:S(2)}, u32[]{:S(2)}) collective-permute-start(bf16[4,32,1152]{2,1,0:T(8,128)(2,1)S(1)} %pad_maximum_fusion.near), channel_id=1, source_target_pairs={{0,2},{1,3},{2,0},{3,1},{4,6},{5,7},{6,4},{7,5},{8,10},{9,11},{10,... | collective-permute-start | bytes 884744 | tf_op jit(solution)/shard_map/ppermute | solution.py:167
  17.0 15.8 %collective-permute-start.11 = (bf16[32,1152]{1,0:T(8,128)(2,1)}, bf16[32,1152]{1,0:T(8,128)(2,1)S(1)}, u32[]{:S(2)}, u32[]{:S(2)}) collective-permute-start(bf16[32,1152]{1,0:T(8,128)(2,1)} %get-tuple-element.44), channel_id=1, source_target_pairs={{0,4},{1,5},{2,6},{3,7},{4,0},{5,1},{6,2},{7,3},{8,12},{9,13},{10,... | collective-permute-start | bytes 221192 | tf_op jit(solution)/shard_map/ppermute | solution.py:172
  18.4 14.4 %collective-permute-start.12 = (bf16[32,1152]{1,0:T(8,128)(2,1)}, bf16[32,1152]{1,0:T(8,128)(2,1)S(1)}, u32[]{:S(2)}, u32[]{:S(2)}) collective-permute-start(bf16[32,1152]{1,0:T(8,128)(2,1)} %get-tuple-element.44), channel_id=1, source_target_pairs={{0,8},{1,9},{2,10},{3,11},{4,12},{5,13},{6,14},{7,15},{8,0},{9,1},... | collective-permute-start | bytes 221192 | tf_op jit(solution)/shard_map/ppermute | solution.py:172
  32.2 9.1 %collective-permute-start.6 = (bf16[4,32,1024]{2,1,0:T(8,128)(2,1)S(1)}, bf16[4,32,1024]{2,1,0:T(8,128)(2,1)S(1)}, u32[]{:S(2)}, u32[]{:S(2)}) collective-permute-start(bf16[4,32,1024]{2,1,0:T(8,128)(2,1)S(1)} %get-tuple-element.40), channel_id=1, source_target_pairs={{0,2},{1,3},{2,0},{3,1},{4,6},{5,7},{6,4},{7,5},{8,10},{9,11},{10,... | collective-permute-start | bytes 786440 | tf_op jit(solution)/shard_map/ppermute | solution.py:167
  32.8 25.9 %collective-permute-start.14 = (bf16[4,32,1152]{2,1,0:T(8,128)(2,1)S(1)}, bf16[4,32,1152]{2,1,0:T(8,128)(2,1)S(1)}, u32[]{:S(2)}, u32[]{:S(2)}) collective-permute-start(bf16[4,32,1152]{2,1,0:T(8,128)(2,1)S(1)} %pad_maximum_fusion.1.near), channel_id=1, source_target_pairs={{0,2},{1,3},{2,0},{3,1},{4,6},{5,7},{6,4},{7,5},{8,10},{9,11},{10,... | collective-permute-start | bytes 884744 | tf_op jit(solution)/shard_map/ppermute | solution.py:167
  41.3 6.9 %collective-permute-start.10 = (bf16[32,1024]{1,0:T(8,128)(2,1)S(1)}, bf16[32,1024]{1,0:T(8,128)(2,1)S(1)}, u32[]{:S(2)}, u32[]{:S(2)}) collective-permute-start(bf16[32,1024]{1,0:T(8,128)(2,1)S(1)} %get-tuple-element.74), channel_id=1, source_target_pairs={{0,12},{1,13},{2,14},{3,15},{4,8},{5,9},{6,10},{7,11},{8,4},{9,5},... | collective-permute-start | bytes 196616 | tf_op jit(solution)/shard_map/ppermute | solution.py:172
  43.4 8.4 %collective-permute-start.9 = (bf16[32,1024]{1,0:T(8,128)(2,1)S(1)}, bf16[32,1024]{1,0:T(8,128)(2,1)S(1)}, u32[]{:S(2)}, u32[]{:S(2)}) collective-permute-start(bf16[32,1024]{1,0:T(8,128)(2,1)S(1)} %get-tuple-element.75), channel_id=1, source_target_pairs={{0,8},{1,9},{2,10},{3,11},{4,12},{5,13},{6,14},{7,15},{8,0},{9,1},... | collective-permute-start | bytes 196616 | tf_op jit(solution)/shard_map/ppermute | solution.py:172
  51.9 10.0 %collective-permute-start.19 = (bf16[32,1152]{1,0:T(8,128)(2,1)S(1)}, bf16[32,1152]{1,0:T(8,128)(2,1)S(1)}, u32[]{:S(2)}, u32[]{:S(2)}) collective-permute-start(bf16[32,1152]{1,0:T(8,128)(2,1)S(1)} %get-tuple-element.51), channel_id=1, source_target_pairs={{0,16},{1,17},{2,18},{3,19},{4,20},{5,21},{6,22},{7,23},{8,24},{9,... | collective-permute-start | bytes 221192 | tf_op jit(solution)/shard_map/ppermute | solution.py:182
  52.0 10.0 %collective-permute-start.20 = (bf16[32,1152]{1,0:T(8,128)(2,1)S(1)}, bf16[32,1152]{1,0:T(8,128)(2,1)S(1)}, u32[]{:S(2)}, u32[]{:S(2)}) collective-permute-start(bf16[32,1152]{1,0:T(8,128)(2,1)S(1)} %get-tuple-element.51), channel_id=1, source_target_pairs={{0,20},{1,21},{2,22},{3,23},{4,16},{5,17},{6,18},{7,19},{8,28},{9,... | collective-permute-start | bytes 221192 | tf_op jit(solution)/shard_map/ppermute | solution.py:182
  52.8 9.2 %collective-permute-start.21 = (bf16[32,1152]{1,0:T(8,128)(2,1)S(1)}, bf16[32,1152]{1,0:T(8,128)(2,1)S(1)}, u32[]{:S(2)}, u32[]{:S(2)}) collective-permute-start(bf16[32,1152]{1,0:T(8,128)(2,1)S(1)} %get-tuple-element.51), channel_id=1, source_target_pairs={{0,24},{1,25},{2,26},{3,27},{4,28},{5,29},{6,30},{7,31},{8,16},{9,... | collective-permute-start | bytes 221192 | tf_op jit(solution)/shard_map/ppermute | solution.py:182
  55.6 7.8 %collective-permute-start.22 = (bf16[32,1152]{1,0:T(8,128)(2,1)S(1)}, bf16[32,1152]{1,0:T(8,128)(2,1)S(1)}, u32[]{:S(2)}, u32[]{:S(2)}) collective-permute-start(bf16[32,1152]{1,0:T(8,128)(2,1)S(1)} %get-tuple-element.51), channel_id=1, source_target_pairs={{0,28},{1,29},{2,30},{3,31},{4,24},{5,25},{6,26},{7,27},{8,20},{9,... | collective-permute-start | bytes 221192 | tf_op jit(solution)/shard_map/ppermute | solution.py:182
  61.9 18.4 %collective-permute-start.24 = (bf16[32,1024]{1,0:T(8,128)(2,1)S(1)}, bf16[32,1024]{1,0:T(8,128)(2,1)S(1)}, u32[]{:S(2)}, u32[]{:S(2)}) collective-permute-start(bf16[32,1024]{1,0:T(8,128)(2,1)S(1)} %get-tuple-element.52), channel_id=1, source_target_pairs={{0,16},{1,17},{2,18},{3,19},{4,20},{5,21},{6,22},{7,23},{8,24},{9,... | collective-permute-start | bytes 196616 | tf_op jit(solution)/shard_map/ppermute | solution.py:182
  63.5 19.9 %collective-permute-start.23 = (bf16[4,32,1152]{2,1,0:T(8,128)(2,1)S(1)}, bf16[4,32,1152]{2,1,0:T(8,128)(2,1)S(1)}, u32[]{:S(2)}, u32[]{:S(2)}) collective-permute-start(bf16[4,32,1152]{2,1,0:T(8,128)(2,1)S(1)} %pad_maximum_fusion.2.near), channel_id=1, source_target_pairs={{0,2},{1,3},{2,0},{3,1},{4,6},{5,7},{6,4},{7,5},{8,10},{9,11},{10,... | collective-permute-start | bytes 884744 | tf_op jit(solution)/shard_map/ppermute | solution.py:167
  76.6 7.3 %collective-permute-start.29 = (bf16[32,1152]{1,0:T(8,128)(2,1)S(1)}, bf16[32,1152]{1,0:T(8,128)(2,1)S(1)}, u32[]{:S(2)}, u32[]{:S(2)}) collective-permute-start(bf16[32,1152]{1,0:T(8,128)(2,1)S(1)} %get-tuple-element.57), channel_id=1, source_target_pairs={{0,16},{1,17},{2,18},{3,19},{4,20},{5,21},{6,22},{7,23},{8,24},{9,... | collective-permute-start | bytes 221192 | tf_op jit(solution)/shard_map/ppermute | solution.py:182
  80.3 7.7 %collective-permute-start.32 = (bf16[32,1152]{1,0:T(8,128)(2,1)S(1)}, bf16[32,1152]{1,0:T(8,128)(2,1)S(1)}, u32[]{:S(2)}, u32[]{:S(2)}) collective-permute-start(bf16[32,1152]{1,0:T(8,128)(2,1)S(1)} %get-tuple-element.57), channel_id=1, source_target_pairs={{0,28},{1,29},{2,30},{3,31},{4,24},{5,25},{6,26},{7,27},{8,20},{9,... | collective-permute-start | bytes 221192 | tf_op jit(solution)/shard_map/ppermute | solution.py:182
  83.4 9.4 %collective-permute-start.34 = (bf16[32,1024]{1,0:T(8,128)(2,1)S(1)}, bf16[32,1024]{1,0:T(8,128)(2,1)S(1)}, u32[]{:S(2)}, u32[]{:S(2)}) collective-permute-start(bf16[32,1024]{1,0:T(8,128)(2,1)S(1)} %get-tuple-element.58), channel_id=1, source_target_pairs={{0,16},{1,17},{2,18},{3,19},{4,20},{5,21},{6,22},{7,23},{8,24},{9,... | collective-permute-start | bytes 196616 | tf_op jit(solution)/shard_map/ppermute | solution.py:182
  88.0 6.8 %collective-permute-start.33 = (bf16[4,32,1152]{2,1,0:T(8,128)(2,1)S(1)}, bf16[4,32,1152]{2,1,0:T(8,128)(2,1)S(1)}, u32[]{:S(2)}, u32[]{:S(2)}) collective-permute-start(bf16[4,32,1152]{2,1,0:T(8,128)(2,1)S(1)} %pad_maximum_fusion.3.near), channel_id=1, source_target_pairs={{0,2},{1,3},{2,0},{3,1},{4,6},{5,7},{6,4},{7,5},{8,10},{9,11},{10,... | collective-permute-start | bytes 884744 | tf_op jit(solution)/shard_map/ppermute | solution.py:167
  90.8 6.9 %collective-permute-start.25 = (bf16[4,32,1024]{2,1,0:T(8,128)(2,1)S(1)}, bf16[4,32,1024]{2,1,0:T(8,128)(2,1)S(1)}, u32[]{:S(2)}, u32[]{:S(2)}) collective-permute-start(bf16[4,32,1024]{2,1,0:T(8,128)(2,1)S(1)} %get-tuple-element.56), channel_id=1, source_target_pairs={{0,2},{1,3},{2,0},{3,1},{4,6},{5,7},{6,4},{7,5},{8,10},{9,11},{10,... | collective-permute-start | bytes 786440 | tf_op jit(solution)/shard_map/ppermute | solution.py:167
  97.7 9.2 %collective-permute-start.26 = (bf16[32,1024]{1,0:T(8,128)(2,1)S(1)}, bf16[32,1024]{1,0:T(8,128)(2,1)S(1)}, u32[]{:S(2)}, u32[]{:S(2)}) collective-permute-start(bf16[32,1024]{1,0:T(8,128)(2,1)S(1)} %get-tuple-element.71), channel_id=1, source_target_pairs={{0,4},{1,5},{2,6},{3,7},{4,0},{5,1},{6,2},{7,3},{8,12},{9,13},{10,... | collective-permute-start | bytes 196616 | tf_op jit(solution)/shard_map/ppermute | solution.py:172
  97.8 10.6 %collective-permute-start.27 = (bf16[32,1024]{1,0:T(8,128)(2,1)S(1)}, bf16[32,1024]{1,0:T(8,128)(2,1)S(1)}, u32[]{:S(2)}, u32[]{:S(2)}) collective-permute-start(bf16[32,1024]{1,0:T(8,128)(2,1)S(1)} %get-tuple-element.73), channel_id=1, source_target_pairs={{0,8},{1,9},{2,10},{3,11},{4,12},{5,13},{6,14},{7,15},{8,0},{9,1},... | collective-permute-start | bytes 196616 | tf_op jit(solution)/shard_map/ppermute | solution.py:172
  100.7 7.8 %collective-permute-start.28 = (bf16[32,1024]{1,0:T(8,128)(2,1)S(1)}, bf16[32,1024]{1,0:T(8,128)(2,1)S(1)}, u32[]{:S(2)}, u32[]{:S(2)}) collective-permute-start(bf16[32,1024]{1,0:T(8,128)(2,1)S(1)} %get-tuple-element.72), channel_id=1, source_target_pairs={{0,12},{1,13},{2,14},{3,15},{4,8},{5,9},{6,10},{7,11},{8,4},{9,5},... | collective-permute-start | bytes 196616 | tf_op jit(solution)/shard_map/ppermute | solution.py:172
  (26 other events, 154.2 us)

commit v3 on v1

v3 whole, which is shorter than its diff:
```python
import functools

import jax
import jax.numpy as jnp
from jax import lax
from jax.experimental import pallas as pl
from jax.experimental.pallas import tpu as pltpu
from jax.sharding import PartitionSpec as P

LANES = 128


def normalize(inflow, gain_row):
    widened = inflow.astype(jnp.float32)
    inverse_rms = lax.rsqrt(jnp.mean(widened * widened, axis=-1, keepdims=True) + 1e-06)
    return (widened * inverse_rms * gain_row).astype(jnp.bfloat16)


def token_weights(experts_all, width, ids, weights):
    steps, micro_count, top_count, tokens = ids.shape
    expert = lax.broadcasted_iota(jnp.int32, (experts_all, tokens), 0)
    columns = []
    for micro in range(micro_count):
        rows = []
        for step in range(steps):
            dense = jnp.zeros((experts_all, tokens), jnp.float32)
            for k in range(top_count):
                named = ids[step, micro, k : k + 1, :] == expert
                dense = dense + jnp.where(named, weights[step, micro, k : k + 1, :], 0.0)
            high = dense.astype(jnp.bfloat16).astype(jnp.float32)
            rows += [high, dense - high]
        empty = width - 2 * steps * experts_all
        if empty > 0:
            rows.append(jnp.zeros((empty, tokens), jnp.float32))
        columns.append(jnp.concatenate(rows, axis=0))
    return jnp.concatenate(columns, axis=1).T.astype(jnp.bfloat16).reshape(
        micro_count, tokens, width
    )


def first_kernel(experts_all, inflow_hbm, ids_hbm, weights_hbm, *refs):
    payloads, (inflow, ids, weights, sem) = refs[:-4], refs[-4:]
    copies = [
        pltpu.make_async_copy(source, target, sem.at[number])
        for number, (source, target) in enumerate(
            ((ids_hbm, ids), (weights_hbm, weights), (inflow_hbm, inflow))
        )
    ]
    for copy in copies:
        copy.start()
    for copy in copies:
        copy.wait()
    features = inflow.shape[-1]
    tails = token_weights(experts_all, payloads[0].shape[-1] - features, ids, weights)
    for micro, payload in enumerate(payloads):
        payload[:, :features] = inflow[micro]
        payload[:, features:] = tails[micro]


def first_payloads(inflow, ids, weights, experts_all):
    micro_count, tokens, features = inflow.shape
    width = -(-2 * experts_all * ids.shape[0] // LANES) * LANES
    return pl.pallas_call(
        functools.partial(first_kernel, experts_all),
        out_shape=(jax.ShapeDtypeStruct((tokens, features + width), jnp.bfloat16),) * micro_count,
        in_specs=[pl.BlockSpec(memory_space=pltpu.HBM)] * 3,
        out_specs=[pl.BlockSpec(memory_space=pltpu.VMEM)] * micro_count,
        scratch_shapes=[
            pltpu.VMEM(inflow.shape, inflow.dtype),
            pltpu.VMEM(ids.shape, ids.dtype),
            pltpu.VMEM(weights.shape, weights.dtype),
            pltpu.SemaphoreType.DMA((3,)),
        ],
        compiler_params=pltpu.CompilerParams(vmem_limit_bytes=60 * 1024 * 1024),
        name="first_payloads",
    )(inflow, ids, weights)


def hold_kernel(after, own_in, own_out, gain, kept):
    del after, own_in, own_out
    kept[...] = gain[...]


def hold(after, own_in, own_out, gain):
    whole = pl.BlockSpec(memory_space=pltpu.VMEM)
    return pl.pallas_call(
        hold_kernel,
        out_shape=jax.ShapeDtypeStruct(gain.shape, gain.dtype),
        in_specs=[pl.BlockSpec(memory_space=pl.ANY), whole, whole, whole],
        out_specs=whole,
        compiler_params=pltpu.CompilerParams(
            vmem_limit_bytes=2 * (own_in.size + own_out.size) + 8 * 1024 * 1024
        ),
        name="hold",
    )(after, own_in, own_out, gain)


def combine_kernel(near_sum, returned, own, *parts):
    own[...] = near_sum[0] + returned[0].astype(jnp.float32)
    for by, part in enumerate(parts, 1):
        part[...] = (near_sum[by] + returned[by].astype(jnp.float32)).astype(jnp.bfloat16)


def combine(near_sum, returned):
    blocks, tokens, features = near_sum.shape
    whole = pl.BlockSpec(memory_space=pltpu.VMEM)
    return pl.pallas_call(
        combine_kernel,
        out_shape=(jax.ShapeDtypeStruct((tokens, features), jnp.float32),)
        + (jax.ShapeDtypeStruct((tokens, features), jnp.bfloat16),) * (blocks - 1),
        in_specs=[whole] * 2,
        out_specs=[whole] * blocks,
        compiler_params=pltpu.CompilerParams(vmem_limit_bytes=8 * 1024 * 1024),
        name="combine",
    )(near_sum, returned)


def leave_kernel(step, micro, inflow, own, *refs):
    parts, (fresh, out, leaving) = refs[:-3], refs[-3:]
    total = inflow[...].reshape(own.shape).astype(jnp.float32) + own[...]
    for part in parts:
        total = total + part[...].astype(jnp.float32)
    result = total.astype(jnp.bfloat16)
    out[...] = result
    is_last = lax.axis_index("section") == lax.axis_size("section") - 1
    arrived = fresh[step, micro].astype(jnp.float32)
    leaving[...] = jnp.where(is_last, arrived, result.astype(jnp.float32)).astype(jnp.bfloat16)


def leave(step, micro, inflow, own, parts, fresh):
    whole = pl.BlockSpec(memory_space=pltpu.VMEM)
    return pl.pallas_call(
        functools.partial(leave_kernel, step, micro),
        out_shape=(jax.ShapeDtypeStruct(own.shape, jnp.bfloat16),) * 2,
        in_specs=[whole] * (3 + len(parts)),
        out_specs=[whole] * 2,
        compiler_params=pltpu.CompilerParams(vmem_limit_bytes=8 * 1024 * 1024),
        name="leave",
    )(inflow, own, *parts, fresh)


def swap_core(value):
    size = lax.axis_size("expert")
    return lax.ppermute(value, "expert", [(i, i ^ 1) for i in range(size)])


def swap_inner(value):
    size = lax.axis_size("expert")
    return lax.ppermute(value, "expert", [(i, i ^ 2) for i in range(size)])


def swap_outer(value, by):
    size = lax.axis_size("expert")
    return lax.ppermute(value, "expert", [(i, i ^ 4 * by) for i in range(size)])


def next_section(value, by):
    sections, size = lax.axis_size("section"), lax.axis_size("expert")
    pairs = [
        (s * size + i, (s + 1) % sections * size + (i ^ 4 * by))
        for s in range(sections)
        for i in range(size)
    ]
    return lax.ppermute(value, ("section", "expert"), pairs)


def previous_section(value):
    sections = lax.axis_size("section")
    return lax.ppermute(value, "section", [(s, (s - 1) % sections) for s in range(sections)])


def serve_kernel(
    features, hidden_count, chunk, experts_all, local_count, step,
    near, far, near_tail, far_tail, gain, own_in, far_in, own_out, far_out,
    near_sum, far_sum, rows, hidden,
):
    blocks, tokens = near.shape[:2]
    half = blocks * tokens
    for start, part in ((0, near), (half, far)):
        for block in range(blocks):
            at = start + block * tokens
            rows[at : at + tokens] = normalize(part[block, :, :features], gain[...])
    tail = jnp.concatenate(
        [part[:, :, features:].reshape(half, -1) for part in (near_tail, far_tail)]
    ).astype(jnp.float32)
    lane = lax.broadcasted_iota(jnp.int32, tail.shape, 1) - 2 * experts_all * step
    me = lax.axis_index("expert")
    total = None
    for side, (w_in, w_out) in enumerate(((own_in, own_out), (far_in, far_out))):
        for own in range(local_count):
            which = (me + side * (1 - 2 * (me % 2))) * local_count + own
            chosen = (lane == which) | (lane == which + experts_all)
            weight = jnp.sum(jnp.where(chosen, tail, 0.0), axis=-1, keepdims=True)
            for at in range(0, hidden_count, chunk):
                gate = jnp.dot(
                    rows[...], w_in[own, :, pl.ds(at, chunk)], preferred_element_type=jnp.float32
                )
                up = jnp.dot(
                    rows[...],
                    w_in[own, :, pl.ds(hidden_count + at, chunk)],
                    preferred_element_type=jnp.float32,
                )
                value = gate / (1.0 + jnp.exp(-gate)) * up * weight
                hidden[:, pl.ds(at, chunk)] = value.astype(jnp.bfloat16)
            out = jnp.dot(hidden[...], w_out[own], preferred_element_type=jnp.float32)
            total = out if total is None else total + out
    near_sum[...] = total[:half].reshape(near_sum.shape)
    far_sum[...] = total[half:].astype(jnp.bfloat16).reshape(far_sum.shape)


def serve(step, near, far, near_tail, far_tail, gain, own_in, far_in, own_out, far_out, experts_all):
    blocks, tokens, _ = near.shape
    local_count, features, _ = own_in.shape
    hidden_count = own_out.shape[1]
    chunk = 256 if hidden_count % 256 == 0 else hidden_count
    rows_all = 2 * blocks * tokens
    held = 2 * (own_in.size + own_out.size) * 2
    whole = pl.BlockSpec(memory_space=pltpu.VMEM)
    return pl.pallas_call(
        functools.partial(
            serve_kernel, features, hidden_count, chunk, experts_all, local_count, step
        ),
        out_shape=(
            jax.ShapeDtypeStruct((blocks, tokens, features), jnp.float32),
            jax.ShapeDtypeStruct((blocks, tokens, features), jnp.bfloat16),
        ),
        in_specs=[whole] * 9,
        out_specs=[whole] * 2,
        scratch_shapes=[
            pltpu.VMEM((rows_all, features), jnp.bfloat16),
            pltpu.VMEM((rows_all, hidden_count), jnp.bfloat16),
        ],
        compiler_params=pltpu.CompilerParams(vmem_limit_bytes=held + 10 * 1024 * 1024),
        cost_estimate=pl.CostEstimate(
            flops=2 * rows_all * 2 * local_count * 3 * features * hidden_count,
            bytes_accessed=held,
            transcendentals=rows_all * 2 * local_count * hidden_count,
        ),
        name="serve",
    )(near, far, near_tail, far_tail, gain, own_in, far_in, own_out, far_out)


def tied(*values):
    return lax.optimization_barrier(values)


def local(in_flight, arriving, norm_gain, gate_up, w_down, expert_ids, route_weights):
    owners = lax.axis_size("expert")
    outer = owners // 4
    local_count = gate_up.shape[1]
    experts_all = owners * local_count
    steps = expert_ids.shape[0]
    micro_count = in_flight.shape[1]
    micros = range(micro_count)
    payloads = first_payloads(
        in_flight[0],
        jnp.swapaxes(expert_ids[:, 0], -1, -2),
        jnp.swapaxes(route_weights[:, 0], -1, -2),
        experts_all,
    )
    *payloads, gate_up, w_down = tied(*payloads, gate_up, w_down)
    own_in, own_out = gate_up[0], w_down[0]
    far_in, far_out = swap_core(own_in), swap_core(own_out)
    gain = norm_gain
    inflows = [in_flight[0, micro] for micro in micros]
    outputs = []
    for step in range(steps):
        near, far, own, parts, results = [], [], [], [], []
        for micro in micros:
            payload = payloads[micro]
            if step == 0:
                blocks = [swap_outer(payload, by) for by in range(outer - 1, 0, -1)] + [payload]
            else:
                blocks = [next_section(payload, by) for by in range(outer - 1, -1, -1)]
                inflows[micro] = blocks[-1]
            near.append(jnp.stack(blocks[::-1]))
            if step == 0 and micro == 0:
                gain = hold(near[0], own_in, own_out, gain)
            far.append(swap_inner(near[micro]))
        if step == 0:
            near_tail, far_tail = near, far
        returned = []
        for micro in micros:
            near_sum, far_sum = serve(
                step, near[micro], far[micro], near_tail[micro], far_tail[micro], gain,
                own_in, far_in, own_out, far_out, experts_all,
            )
            own.append(near_sum)
            returned.append(swap_inner(far_sum))
        for micro in micros:
            own[micro], *blocks = combine(own[micro], returned[micro])
            parts.append([swap_outer(blocks[by - 1], by) for by in range(outer - 1, 0, -1)])
        for micro in micros:
            if step < steps - 1:
                if micro < micro_count - 1:
                    parts[micro][0], own[micro + 1] = tied(parts[micro][0], own[micro + 1])
                result, payloads[micro] = leave(
                    step, micro, inflows[micro], own[micro], parts[micro], arriving
                )
            else:
                total = inflows[micro].astype(jnp.float32) + own[micro]
                for part in parts[micro]:
                    total = total + part.astype(jnp.float32)
                result = total.astype(jnp.bfloat16)
            results.append(result)
        outputs.append(jnp.stack(results))
    return jnp.stack(outputs)[:, None]


def solution(mesh):
    return jax.shard_map(
        local,
        mesh=mesh,
        in_specs=(
            P("section", None, "expert", None),
            P(None, None, "expert", None),
            P("section", None),
            P("section", "expert", None, None),
            P("section", "expert", None, None),
            P(None, "section", None, "expert", None),
            P(None, "section", None, "expert", None),
        ),
        out_specs=P(None, "section", None, "expert", None),
        check_vma=False,
    )
```

time: 104 us -> 104 us (level)
  starting transfers between devices: 59.5 us -> 56.6 us
  other arithmetic: 1.33 us -> 2.78 us
  Pallas kernels: 12.1 us -> 13.5 us
    ppermute x8, waiting for transfers between devices: 12.9 us -> 5.26 us  [swap_inner(): return lax.ppermute(value, 'expert', [(i, i ^ 2) for i in range(size)])]
    ppermute x20 -> x18, waiting for transfers between devices: 8.52 us -> 12.7 us  [swap_outer(): return lax.ppermute(value, 'expert', [(i, i ^ 4 * by) for i in range(size)])]
    ppermute x20 -> x18, starting transfers between devices: 32.5 us -> 28.6 us  [swap_outer(): return lax.ppermute(value, 'expert', [(i, i ^ 4 * by) for i in range(size)])]
    ppermute x10 -> x8, waiting for transfers between devices: 3.13 us -> 6.66 us  [next_section(): return lax.ppermute(value, ('section', 'expert'), pairs)]
    ppermute x8, starting transfers between devices: 11.2 us -> 13.7 us  [swap_inner(): return lax.ppermute(value, 'expert', [(i, i ^ 2) for i in range(size)])]
    ppermute x10 -> x8, starting transfers between devices: 15.3 us -> 13.6 us  [next_section(): return lax.ppermute(value, ('section', 'expert'), pairs)]
    another operation x8 -> x4, other arithmetic: 0.49 us -> 1.93 us  [local(): near.append(jnp.stack(blocks[::-1]))]
    pallas_call x3 -> x8, Pallas kernels: 1.39 us -> 2.1 us  [the longest x1 1.77 us: first_payloads(): pl.pallas_call(functools.partial(first_kernel, experts_all), out_shape=(j...]
  transfers between devices with their start and end apart: 40 -> 36, of which waited for: 15 -> 15; matrix products, arithmetic and copies ran while one was open for 1% -> 2% of each run, Pallas kernels for 12% -> 11%
where the time goes in v3:
time: 104 us; the launch traced here: 103 us
  starting transfers between devices  56.6 us (54%)
  waiting for transfers between devices  24.6 us (24%)
  Pallas kernels  13.5 us (13%)
  local copies, waits for them, and re-layouts  5.81 us (6%)
  other arithmetic  2.78 us (3%)
    ppermute x18, starting transfers between devices, swap_outer(): return lax.ppermute(value, 'expert', [(i, i ^ 4 * by) for i in range(size)])  28.6 us
    ppermute x8, starting transfers between devices, swap_inner(): return lax.ppermute(value, 'expert', [(i, i ^ 2) for i in range(size)])  13.7 us
    ppermute x8, starting transfers between devices, next_section(): return lax.ppermute(value, ('section', 'expert'), pairs)  13.6 us
    ppermute x18, waiting for transfers between devices, swap_outer(): return lax.ppermute(value, 'expert', [(i, i ^ 4 * by) for i in range(size)])  12.7 us
    pallas_call x4, Pallas kernels, serve(): pl.pallas_call(functools.partial(serve_kernel, features, hidden_count, ch...  11.4 us
    ppermute x8, waiting for transfers between devices, next_section(): return lax.ppermute(value, ('section', 'expert'), pairs)  6.66 us
    unnamed x14, local copies, waits for them, and re-layouts  5.8 us
    ppermute x8, waiting for transfers between devices, swap_inner(): return lax.ppermute(value, 'expert', [(i, i ^ 2) for i in range(size)])  5.26 us
  transfers between devices with their start and end apart: 36, of which 15 were waited for; matrix products, arithmetic and copies ran while one was open for 2% of the time, Pallas kernels for 11%

profile of v3, /device:TPU:0, one launch (start us, length us, event | category | flops | bytes accessed | tf_op | source)
XLA Modules:
  0.0 103.4 jit_solution(6191148045144973723)
XLA Ops:
  2.4 3.0 %collective-permute-start = (bf16[32,1152]{1,0:T(8,128)(2,1)}, bf16[32,1152]{1,0:T(8,128)(2,1)S(1)}, u32[]{:S(2)}, u32[]{:S(2)}) collective-permute-start(bf16[32,1152]{1,0:T(8,128)(2,1)} %get-tuple-element.43), channel_id=1, source_target_pairs={{0,4},{1,5},{2,6},{3,7},{4,0},{5,1},{6,2},{7,3},{8,12},{9,13},{10,... | collective-permute-start | bytes 221192 | tf_op jit(solution)/shard_map/ppermute | solution.py:154
  5.4 2.6 %collective-permute-start.1 = (bf16[32,1152]{1,0:T(8,128)(2,1)}, bf16[32,1152]{1,0:T(8,128)(2,1)S(1)}, u32[]{:S(2)}, u32[]{:S(2)}) collective-permute-start(bf16[32,1152]{1,0:T(8,128)(2,1)} %get-tuple-element.43), channel_id=1, source_target_pairs={{0,8},{1,9},{2,10},{3,11},{4,12},{5,13},{6,14},{7,15},{8,0},{9,1},... | collective-permute-start | bytes 221192 | tf_op jit(solution)/shard_map/ppermute | solution.py:154
  9.9 3.7 %collective-permute-done.1 = bf16[32,1152]{1,0:T(8,128)(2,1)S(1)} collective-permute-done((bf16[32,1152]{1,0:T(8,128)(2,1)}, bf16[32,1152]{1,0:T(8,128)(2,1)S(1)}, u32[]{:S(2)}, u32[]{:S(2)}) %collective-permute-start.1) | collective-permute-done | bytes 73760 | tf_op jit(solution)/shard_map/ppermute | solution.py:154
  14.6 2.9 %collective-permute-start.10 = (bf16[32,1152]{1,0:T(8,128)(2,1)}, bf16[32,1152]{1,0:T(8,128)(2,1)S(1)}, u32[]{:S(2)}, u32[]{:S(2)}) collective-permute-start(bf16[32,1152]{1,0:T(8,128)(2,1)} %get-tuple-element.50), channel_id=1, source_target_pairs={{0,12},{1,13},{2,14},{3,15},{4,8},{5,9},{6,10},{7,11},{8,4},{9,5},... | collective-permute-start | bytes 221192 | tf_op jit(solution)/shard_map/ppermute | solution.py:154
  23.5 1.9 %copy-done = bf16[1,1,1024,1536]{3,2,1,0:T(8,128)(2,1)S(1)} copy-done((bf16[1,1,1024,1536]{3,2,1,0:T(8,128)(2,1)S(1)}, bf16[1,1,1024,1536]{3,2,1,0:T(8,128)(2,1)}, u32[]{:S(2)}) %copy-start) | copy-done | bytes 3145752
  29.8 2.8 %serve.4 = (f32[4,32,1024]{2,1,0:T(8,128)S(1)}, bf16[4,32,1024]{2,1,0:T(8,128)(2,1)S(1)}) custom-call(bf16[4,32,1152]{2,1,0:T(8,128)(2,1)S(1)} %pad_maximum_fusion.after.near.near_tail, bf16[4,32,1152]{2,1,0:T(8,128)(2,1)S(1)} %collective-permute-done.3.far.far_tail, bf16[4,32,1152]{2,1,0:T(8,128)(2,1)S(1)} %pad_maximum_fusion.after.near.near_tail, ...), custom_call_target="tpu_custom_call" | custom-call | flops 2415919104 | bytes 9437184 | tf_op jit(solution)/shard_map/serve/pallas_call | solution.py:219
  33.3 2.8 %serve.5 = (f32[4,32,1024]{2,1,0:T(8,128)S(1)}, bf16[4,32,1024]{2,1,0:T(8,128)(2,1)S(1)}) custom-call(bf16[4,32,1152]{2,1,0:T(8,128)(2,1)S(1)} %pad_maximum_fusion.1.near.near_tail, bf16[4,32,1152]{2,1,0:T(8,128)(2,1)S(1)} %collective-permute-done.11.far.far_tail, bf16[4,32,1152]{2,1,0:T(8,128)(2,1)S(1)} %pad_maximum_fusion.1.near.near_tail, ...), custom_call_target="tpu_custom_call" | custom-call | flops 2415919104 | bytes 9437184 | tf_op jit(solution)/shard_map/serve/pallas_call | solution.py:219
  37.7 3.3 %collective-permute-done.6.returned = bf16[4,32,1024]{2,1,0:T(8,128)(2,1)S(1)} collective-permute-done((bf16[4,32,1024]{2,1,0:T(8,128)(2,1)S(1)}, bf16[4,32,1024]{2,1,0:T(8,128)(2,1)S(1)}, u32[]{:S(2)}, u32[]{:S(2)}) %collective-permute-start.6) | collective-permute-done | bytes 262176 | tf_op jit(solution)/shard_map/ppermute | solution.py:149
  43.6 1.9 %collective-permute-start.14 = (bf16[32,1024]{1,0:T(8,128)(2,1)S(1)}, bf16[32,1024]{1,0:T(8,128)(2,1)S(1)}, u32[]{:S(2)}, u32[]{:S(2)}) collective-permute-start(bf16[32,1024]{1,0:T(8,128)(2,1)S(1)} %get-tuple-element.56), channel_id=1, source_target_pairs={{0,4},{1,5},{2,6},{3,7},{4,0},{5,1},{6,2},{7,3},{8,12},{9,13},{10,... | collective-permute-start | bytes 196616 | tf_op jit(solution)/shard_map/ppermute | solution.py:154
  45.6 2.0 %collective-permute-done.7.refs_0_ = bf16[32,1024]{1,0:T(8,128)(2,1)S(1)} collective-permute-done((bf16[32,1024]{1,0:T(8,128)(2,1)S(1)}, bf16[32,1024]{1,0:T(8,128)(2,1)S(1)}, u32[]{:S(2)}, u32[]{:S(2)}) %collective-permute-start.7) | collective-permute-done | bytes 65568 | tf_op jit(solution)/shard_map/ppermute | solution.py:154
  47.6 2.4 %collective-permute-done.13.refs_1_ = bf16[32,1024]{1,0:T(8,128)(2,1)S(1)} collective-permute-done((bf16[32,1024]{1,0:T(8,128)(2,1)S(1)}, bf16[32,1024]{1,0:T(8,128)(2,1)S(1)}, u32[]{:S(2)}, u32[]{:S(2)}) %collective-permute-start.13) | collective-permute-done | bytes 65568 | tf_op jit(solution)/shard_map/ppermute | solution.py:154
  51.9 4.5 %collective-permute-start.20 = (bf16[32,1024]{1,0:T(8,128)(2,1)S(1)}, bf16[32,1024]{1,0:T(8,128)(2,1)S(1)}, u32[]{:S(2)}, u32[]{:S(2)}) collective-permute-start(bf16[32,1024]{1,0:T(8,128)(2,1)S(1)} %get-tuple-element.63), channel_id=1, source_target_pairs={{0,24},{1,25},{2,26},{3,27},{4,28},{5,29},{6,30},{7,31},{8,16},{9,... | collective-permute-start | bytes 196616 | tf_op jit(solution)/shard_map/ppermute | solution.py:164
  56.9 2.8 %collective-permute-start.15 = (bf16[32,1024]{1,0:T(8,128)(2,1)S(1)}, bf16[32,1024]{1,0:T(8,128)(2,1)S(1)}, u32[]{:S(2)}, u32[]{:S(2)}) collective-permute-start(bf16[32,1024]{1,0:T(8,128)(2,1)S(1)} %get-tuple-element.59), channel_id=1, source_target_pairs={{0,12},{1,13},{2,14},{3,15},{4,8},{5,9},{6,10},{7,11},{8,4},{9,5},... | collective-permute-start | bytes 196616 | tf_op jit(solution)/shard_map/ppermute | solution.py:154
  61.3 2.1 %collective-permute-done.21 = bf16[32,1024]{1,0:T(8,128)(2,1)S(1)} collective-permute-done((bf16[32,1024]{1,0:T(8,128)(2,1)S(1)}, bf16[32,1024]{1,0:T(8,128)(2,1)S(1)}, u32[]{:S(2)}, u32[]{:S(2)}) %collective-permute-start.21) | collective-permute-done | bytes 65568 | tf_op jit(solution)/shard_map/ppermute | solution.py:164
  63.5 3.4 %collective-permute-start.22 = (bf16[4,32,1024]{2,1,0:T(8,128)(2,1)S(1)}, bf16[4,32,1024]{2,1,0:T(8,128)(2,1)S(1)}, u32[]{:S(2)}, u32[]{:S(2)}) collective-permute-start(bf16[4,32,1024]{2,1,0:T(8,128)(2,1)S(1)} %pad_maximum_fusion.2.near), channel_id=1, source_target_pairs={{0,2},{1,3},{2,0},{3,1},{4,6},{5,7},{6,4},{7,5},{8,10},{9,11},{10,... | collective-permute-start | bytes 786440 | tf_op jit(solution)/shard_map/ppermute | solution.py:149
  69.3 2.1 %collective-permute-start.29 = (bf16[32,1024]{1,0:T(8,128)(2,1)S(1)}, bf16[32,1024]{1,0:T(8,128)(2,1)S(1)}, u32[]{:S(2)}, u32[]{:S(2)}) collective-permute-start(bf16[32,1024]{1,0:T(8,128)(2,1)S(1)} %get-tuple-element.70), channel_id=1, source_target_pairs={{0,24},{1,25},{2,26},{3,27},{4,28},{5,29},{6,30},{7,31},{8,16},{9,... | collective-permute-start | bytes 196616 | tf_op jit(solution)/shard_map/ppermute | solution.py:164
  71.4 2.4 %collective-permute-start.30 = (bf16[32,1024]{1,0:T(8,128)(2,1)S(1)}, bf16[32,1024]{1,0:T(8,128)(2,1)S(1)}, u32[]{:S(2)}, u32[]{:S(2)}) collective-permute-start(bf16[32,1024]{1,0:T(8,128)(2,1)S(1)} %get-tuple-element.70), channel_id=1, source_target_pairs={{0,28},{1,29},{2,30},{3,31},{4,24},{5,25},{6,26},{7,27},{8,20},{9,... | collective-permute-start | bytes 196616 | tf_op jit(solution)/shard_map/ppermute | solution.py:164
  75.4 3.0 %collective-permute-done.30 = bf16[32,1024]{1,0:T(8,128)(2,1)S(1)} collective-permute-done((bf16[32,1024]{1,0:T(8,128)(2,1)S(1)}, bf16[32,1024]{1,0:T(8,128)(2,1)S(1)}, u32[]{:S(2)}, u32[]{:S(2)}) %collective-permute-start.30) | collective-permute-done | bytes 65568 | tf_op jit(solution)/shard_map/ppermute | solution.py:164
  78.4 2.8 %collective-permute-start.31 = (bf16[4,32,1024]{2,1,0:T(8,128)(2,1)S(1)}, bf16[4,32,1024]{2,1,0:T(8,128)(2,1)S(1)}, u32[]{:S(2)}, u32[]{:S(2)}) collective-permute-start(bf16[4,32,1024]{2,1,0:T(8,128)(2,1)S(1)} %pad_maximum_fusion.3.near), channel_id=1, source_target_pairs={{0,2},{1,3},{2,0},{3,1},{4,6},{5,7},{6,4},{7,5},{8,10},{9,11},{10,... | collective-permute-start | bytes 786440 | tf_op jit(solution)/shard_map/ppermute | solution.py:149
  81.2 2.8 %serve.6 = (f32[4,32,1024]{2,1,0:T(8,128)S(1)}, bf16[4,32,1024]{2,1,0:T(8,128)(2,1)S(1)}) custom-call(bf16[4,32,1024]{2,1,0:T(8,128)(2,1)S(1)} %pad_maximum_fusion.2.near, bf16[4,32,1024]{2,1,0:T(8,128)(2,1)S(1)} %collective-permute-done.22.far, bf16[4,32,1152]{2,1,0:T(8,128)(2,1)S(1)} %pad_maximum_fusion.after.near.near_tail, ...), custom_call_target="tpu_custom_call" | custom-call | flops 2415919104 | bytes 9437184 | tf_op jit(solution)/shard_map/serve/pallas_call | solution.py:219
  85.5 2.8 %serve.7 = (f32[4,32,1024]{2,1,0:T(8,128)S(1)}, bf16[4,32,1024]{2,1,0:T(8,128)(2,1)S(1)}) custom-call(bf16[4,32,1024]{2,1,0:T(8,128)(2,1)S(1)} %pad_maximum_fusion.3.near, bf16[4,32,1024]{2,1,0:T(8,128)(2,1)S(1)} %collective-permute-done.31.far, bf16[4,32,1152]{2,1,0:T(8,128)(2,1)S(1)} %pad_maximum_fusion.1.near.near_tail, ...), custom_call_target="tpu_custom_call" | custom-call | flops 2415919104 | bytes 9437184 | tf_op jit(solution)/shard_map/serve/pallas_call | solution.py:219
  88.4 2.1 %collective-permute-start.32 = (bf16[4,32,1024]{2,1,0:T(8,128)(2,1)S(1)}, bf16[4,32,1024]{2,1,0:T(8,128)(2,1)S(1)}, u32[]{:S(2)}, u32[]{:S(2)}) collective-permute-start(bf16[4,32,1024]{2,1,0:T(8,128)(2,1)S(1)} %get-tuple-element.72), channel_id=1, source_target_pairs={{0,2},{1,3},{2,0},{3,1},{4,6},{5,7},{6,4},{7,5},{8,10},{9,11},{10,... | collective-permute-start | bytes 786440 | tf_op jit(solution)/shard_map/ppermute | solution.py:149
  91.9 3.0 %collective-permute-start.26 = (bf16[32,1024]{1,0:T(8,128)(2,1)S(1)}, bf16[32,1024]{1,0:T(8,128)(2,1)S(1)}, u32[]{:S(2)}, u32[]{:S(2)}) collective-permute-start(bf16[32,1024]{1,0:T(8,128)(2,1)S(1)} %get-tuple-element.69), channel_id=1, source_target_pairs={{0,4},{1,5},{2,6},{3,7},{4,0},{5,1},{6,2},{7,3},{8,12},{9,13},{10,... | collective-permute-start | bytes 196616 | tf_op jit(solution)/shard_map/ppermute | solution.py:154
  96.7 2.8 %collective-permute-start.35 = (bf16[32,1024]{1,0:T(8,128)(2,1)S(1)}, bf16[32,1024]{1,0:T(8,128)(2,1)S(1)}, u32[]{:S(2)}, u32[]{:S(2)}) collective-permute-start(bf16[32,1024]{1,0:T(8,128)(2,1)S(1)} %get-tuple-element.76), channel_id=1, source_target_pairs={{0,4},{1,5},{2,6},{3,7},{4,0},{5,1},{6,2},{7,3},{8,12},{9,13},{10,... | collective-permute-start | bytes 196616 | tf_op jit(solution)/shard_map/ppermute | solution.py:154
  (84 shorter events, 37.1 us)
Async XLA Ops:
  1.8 26.3 %collective-permute-start.4 = (bf16[1,1024,1536]{2,1,0:T(8,128)(2,1)}, bf16[1,1024,1536]{2,1,0:T(8,128)(2,1)S(1)}, u32[]{:S(2)}, u32[]{:S(2)}) collective-permute-start(bf16[1,1024,1536]{2,1,0:T(8,128)(2,1)} %bitcast.43), channel_id=1, source_target_pairs={{0,1},{1,0},{2,3},{3,2},{4,5},{5,4},{6,7},{7,6},{8,9},{9,8},{10,11... | collective-permute-start | bytes 9437192 | tf_op jit(solution)/shard_map/ppermute | solution.py:144
  2.3 25.7 %collective-permute-start.5 = (bf16[1,768,1024]{2,1,0:T(8,128)(2,1)}, bf16[1,768,1024]{2,1,0:T(8,128)(2,1)S(1)}, u32[]{:S(2)}, u32[]{:S(2)}) collective-permute-start(bf16[1,768,1024]{2,1,0:T(8,128)(2,1)} %bitcast.49), channel_id=1, source_target_pairs={{0,1},{1,0},{2,3},{3,2},{4,5},{5,4},{6,7},{7,6},{8,9},{9,8},{10,11... | collective-permute-start | bytes 4718600 | tf_op jit(solution)/shard_map/ppermute | solution.py:144
  5.4 8.3 %collective-permute-start.1 = (bf16[32,1152]{1,0:T(8,128)(2,1)}, bf16[32,1152]{1,0:T(8,128)(2,1)S(1)}, u32[]{:S(2)}, u32[]{:S(2)}) collective-permute-start(bf16[32,1152]{1,0:T(8,128)(2,1)} %get-tuple-element.43), channel_id=1, source_target_pairs={{0,8},{1,9},{2,10},{3,11},{4,12},{5,13},{6,14},{7,15},{8,0},{9,1},... | collective-permute-start | bytes 221192 | tf_op jit(solution)/shard_map/ppermute | solution.py:154
  8.0 6.6 %collective-permute-start.2 = (bf16[32,1152]{1,0:T(8,128)(2,1)}, bf16[32,1152]{1,0:T(8,128)(2,1)S(1)}, u32[]{:S(2)}, u32[]{:S(2)}) collective-permute-start(bf16[32,1152]{1,0:T(8,128)(2,1)} %get-tuple-element.43), channel_id=1, source_target_pairs={{0,12},{1,13},{2,14},{3,15},{4,8},{5,9},{6,10},{7,11},{8,4},{9,5},... | collective-permute-start | bytes 221192 | tf_op jit(solution)/shard_map/ppermute | solution.py:154
  8.1 10.4 %collective-permute-start.8 = (bf16[32,1152]{1,0:T(8,128)(2,1)}, bf16[32,1152]{1,0:T(8,128)(2,1)S(1)}, u32[]{:S(2)}, u32[]{:S(2)}) collective-permute-start(bf16[32,1152]{1,0:T(8,128)(2,1)} %get-tuple-element.50), channel_id=1, source_target_pairs={{0,4},{1,5},{2,6},{3,7},{4,0},{5,1},{6,2},{7,3},{8,12},{9,13},{10,... | collective-permute-start | bytes 221192 | tf_op jit(solution)/shard_map/ppermute | solution.py:154
  18.5 9.5 %collective-permute-start.3 = (bf16[4,32,1152]{2,1,0:T(8,128)(2,1)S(1)}, bf16[4,32,1152]{2,1,0:T(8,128)(2,1)S(1)}, u32[]{:S(2)}, u32[]{:S(2)}) collective-permute-start(bf16[4,32,1152]{2,1,0:T(8,128)(2,1)S(1)} %pad_maximum_fusion.after.near.near_tail), channel_id=1, source_target_pairs={{0,2},{1,3},{2,0},{3,1},{4,6},{5,7},{6,4},{7,5},{8,10},{9,11},{10,... | collective-permute-start | bytes 884744 | tf_op jit(solution)/shard_map/ppermute | solution.py:149
  21.9 11.4 %collective-permute-start.11 = (bf16[4,32,1152]{2,1,0:T(8,128)(2,1)S(1)}, bf16[4,32,1152]{2,1,0:T(8,128)(2,1)S(1)}, u32[]{:S(2)}, u32[]{:S(2)}) collective-permute-start(bf16[4,32,1152]{2,1,0:T(8,128)(2,1)S(1)} %pad_maximum_fusion.1.near.near_tail), channel_id=1, source_target_pairs={{0,2},{1,3},{2,0},{3,1},{4,6},{5,7},{6,4},{7,5},{8,10},{9,11},{10,... | collective-permute-start | bytes 884744 | tf_op jit(solution)/shard_map/ppermute | solution.py:149
  32.7 8.3 %collective-permute-start.6 = (bf16[4,32,1024]{2,1,0:T(8,128)(2,1)S(1)}, bf16[4,32,1024]{2,1,0:T(8,128)(2,1)S(1)}, u32[]{:S(2)}, u32[]{:S(2)}) collective-permute-start(bf16[4,32,1024]{2,1,0:T(8,128)(2,1)S(1)} %get-tuple-element.47), channel_id=1, source_target_pairs={{0,2},{1,3},{2,0},{3,1},{4,6},{5,7},{6,4},{7,5},{8,10},{9,11},{10,... | collective-permute-start | bytes 786440 | tf_op jit(solution)/shard_map/ppermute | solution.py:149
  36.1 9.4 %collective-permute-start.12 = (bf16[4,32,1024]{2,1,0:T(8,128)(2,1)S(1)}, bf16[4,32,1024]{2,1,0:T(8,128)(2,1)S(1)}, u32[]{:S(2)}, u32[]{:S(2)}) collective-permute-start(bf16[4,32,1024]{2,1,0:T(8,128)(2,1)S(1)} %get-tuple-element.52), channel_id=1, source_target_pairs={{0,2},{1,3},{2,0},{3,1},{4,6},{5,7},{6,4},{7,5},{8,10},{9,11},{10,... | collective-permute-start | bytes 786440 | tf_op jit(solution)/shard_map/ppermute | solution.py:149
  42.6 7.4 %collective-permute-start.13 = (bf16[32,1024]{1,0:T(8,128)(2,1)S(1)}, bf16[32,1024]{1,0:T(8,128)(2,1)S(1)}, u32[]{:S(2)}, u32[]{:S(2)}) collective-permute-start(bf16[32,1024]{1,0:T(8,128)(2,1)S(1)} %get-tuple-element.55), channel_id=1, source_target_pairs={{0,8},{1,9},{2,10},{3,11},{4,12},{5,13},{6,14},{7,15},{8,0},{9,1},... | collective-permute-start | bytes 196616 | tf_op jit(solution)/shard_map/ppermute | solution.py:154
  50.1 9.6 %collective-permute-start.18 = (bf16[32,1024]{1,0:T(8,128)(2,1)S(1)}, bf16[32,1024]{1,0:T(8,128)(2,1)S(1)}, u32[]{:S(2)}, u32[]{:S(2)}) collective-permute-start(bf16[32,1024]{1,0:T(8,128)(2,1)S(1)} %get-tuple-element.63), channel_id=1, source_target_pairs={{0,16},{1,17},{2,18},{3,19},{4,20},{5,21},{6,22},{7,23},{8,24},{9,... | collective-permute-start | bytes 196616 | tf_op jit(solution)/shard_map/ppermute | solution.py:164
  51.9 7.9 %collective-permute-start.19 = (bf16[32,1024]{1,0:T(8,128)(2,1)S(1)}, bf16[32,1024]{1,0:T(8,128)(2,1)S(1)}, u32[]{:S(2)}, u32[]{:S(2)}) collective-permute-start(bf16[32,1024]{1,0:T(8,128)(2,1)S(1)} %get-tuple-element.63), channel_id=1, source_target_pairs={{0,20},{1,21},{2,22},{3,23},{4,16},{5,17},{6,18},{7,19},{8,28},{9,... | collective-permute-start | bytes 196616 | tf_op jit(solution)/shard_map/ppermute | solution.py:164
  51.9 9.5 %collective-permute-start.20 = (bf16[32,1024]{1,0:T(8,128)(2,1)S(1)}, bf16[32,1024]{1,0:T(8,128)(2,1)S(1)}, u32[]{:S(2)}, u32[]{:S(2)}) collective-permute-start(bf16[32,1024]{1,0:T(8,128)(2,1)S(1)} %get-tuple-element.63), channel_id=1, source_target_pairs={{0,24},{1,25},{2,26},{3,27},{4,28},{5,29},{6,30},{7,31},{8,16},{9,... | collective-permute-start | bytes 196616 | tf_op jit(solution)/shard_map/ppermute | solution.py:164
  56.4 7.1 %collective-permute-start.21 = (bf16[32,1024]{1,0:T(8,128)(2,1)S(1)}, bf16[32,1024]{1,0:T(8,128)(2,1)S(1)}, u32[]{:S(2)}, u32[]{:S(2)}) collective-permute-start(bf16[32,1024]{1,0:T(8,128)(2,1)S(1)} %get-tuple-element.63), channel_id=1, source_target_pairs={{0,28},{1,29},{2,30},{3,31},{4,24},{5,25},{6,26},{7,27},{8,20},{9,... | collective-permute-start | bytes 196616 | tf_op jit(solution)/shard_map/ppermute | solution.py:164
  56.9 10.0 %collective-permute-start.15 = (bf16[32,1024]{1,0:T(8,128)(2,1)S(1)}, bf16[32,1024]{1,0:T(8,128)(2,1)S(1)}, u32[]{:S(2)}, u32[]{:S(2)}) collective-permute-start(bf16[32,1024]{1,0:T(8,128)(2,1)S(1)} %get-tuple-element.59), channel_id=1, source_target_pairs={{0,12},{1,13},{2,14},{3,15},{4,8},{5,9},{6,10},{7,11},{8,4},{9,5},... | collective-permute-start | bytes 196616 | tf_op jit(solution)/shard_map/ppermute | solution.py:154
  59.7 7.2 %collective-permute-start.16 = (bf16[32,1024]{1,0:T(8,128)(2,1)S(1)}, bf16[32,1024]{1,0:T(8,128)(2,1)S(1)}, u32[]{:S(2)}, u32[]{:S(2)}) collective-permute-start(bf16[32,1024]{1,0:T(8,128)(2,1)S(1)} %get-tuple-element.60), channel_id=1, source_target_pairs={{0,8},{1,9},{2,10},{3,11},{4,12},{5,13},{6,14},{7,15},{8,0},{9,1},... | collective-permute-start | bytes 196616 | tf_op jit(solution)/shard_map/ppermute | solution.py:154
  59.8 7.2 %collective-permute-start.17 = (bf16[32,1024]{1,0:T(8,128)(2,1)S(1)}, bf16[32,1024]{1,0:T(8,128)(2,1)S(1)}, u32[]{:S(2)}, u32[]{:S(2)}) collective-permute-start(bf16[32,1024]{1,0:T(8,128)(2,1)S(1)} %get-tuple-element.61), channel_id=1, source_target_pairs={{0,4},{1,5},{2,6},{3,7},{4,0},{5,1},{6,2},{7,3},{8,12},{9,13},{10,... | collective-permute-start | bytes 196616 | tf_op jit(solution)/shard_map/ppermute | solution.py:154
  63.5 17.7 %collective-permute-start.22 = (bf16[4,32,1024]{2,1,0:T(8,128)(2,1)S(1)}, bf16[4,32,1024]{2,1,0:T(8,128)(2,1)S(1)}, u32[]{:S(2)}, u32[]{:S(2)}) collective-permute-start(bf16[4,32,1024]{2,1,0:T(8,128)(2,1)S(1)} %pad_maximum_fusion.2.near), channel_id=1, source_target_pairs={{0,2},{1,3},{2,0},{3,1},{4,6},{5,7},{6,4},{7,5},{8,10},{9,11},{10,... | collective-permute-start | bytes 786440 | tf_op jit(solution)/shard_map/ppermute | solution.py:149
  67.0 6.8 %collective-permute-start.27 = (bf16[32,1024]{1,0:T(8,128)(2,1)S(1)}, bf16[32,1024]{1,0:T(8,128)(2,1)S(1)}, u32[]{:S(2)}, u32[]{:S(2)}) collective-permute-start(bf16[32,1024]{1,0:T(8,128)(2,1)S(1)} %get-tuple-element.70), channel_id=1, source_target_pairs={{0,16},{1,17},{2,18},{3,19},{4,20},{5,21},{6,22},{7,23},{8,24},{9,... | collective-permute-start | bytes 196616 | tf_op jit(solution)/shard_map/ppermute | solution.py:164
  71.4 7.0 %collective-permute-start.30 = (bf16[32,1024]{1,0:T(8,128)(2,1)S(1)}, bf16[32,1024]{1,0:T(8,128)(2,1)S(1)}, u32[]{:S(2)}, u32[]{:S(2)}) collective-permute-start(bf16[32,1024]{1,0:T(8,128)(2,1)S(1)} %get-tuple-element.70), channel_id=1, source_target_pairs={{0,28},{1,29},{2,30},{3,31},{4,24},{5,25},{6,26},{7,27},{8,20},{9,... | collective-permute-start | bytes 196616 | tf_op jit(solution)/shard_map/ppermute | solution.py:164
  78.4 7.2 %collective-permute-start.31 = (bf16[4,32,1024]{2,1,0:T(8,128)(2,1)S(1)}, bf16[4,32,1024]{2,1,0:T(8,128)(2,1)S(1)}, u32[]{:S(2)}, u32[]{:S(2)}) collective-permute-start(bf16[4,32,1024]{2,1,0:T(8,128)(2,1)S(1)} %pad_maximum_fusion.3.near), channel_id=1, source_target_pairs={{0,2},{1,3},{2,0},{3,1},{4,6},{5,7},{6,4},{7,5},{8,10},{9,11},{10,... | collective-permute-start | bytes 786440 | tf_op jit(solution)/shard_map/ppermute | solution.py:149
  88.4 6.6 %collective-permute-start.32 = (bf16[4,32,1024]{2,1,0:T(8,128)(2,1)S(1)}, bf16[4,32,1024]{2,1,0:T(8,128)(2,1)S(1)}, u32[]{:S(2)}, u32[]{:S(2)}) collective-permute-start(bf16[4,32,1024]{2,1,0:T(8,128)(2,1)S(1)} %get-tuple-element.72), channel_id=1, source_target_pairs={{0,2},{1,3},{2,0},{3,1},{4,6},{5,7},{6,4},{7,5},{8,10},{9,11},{10,... | collective-permute-start | bytes 786440 | tf_op jit(solution)/shard_map/ppermute | solution.py:149
  91.9 7.6 %collective-permute-start.25 = (bf16[32,1024]{1,0:T(8,128)(2,1)S(1)}, bf16[32,1024]{1,0:T(8,128)(2,1)S(1)}, u32[]{:S(2)}, u32[]{:S(2)}) collective-permute-start(bf16[32,1024]{1,0:T(8,128)(2,1)S(1)} %get-tuple-element.68), channel_id=1, source_target_pairs={{0,8},{1,9},{2,10},{3,11},{4,12},{5,13},{6,14},{7,15},{8,0},{9,1},... | collective-permute-start | bytes 196616 | tf_op jit(solution)/shard_map/ppermute | solution.py:154
  91.9 7.6 %collective-permute-start.26 = (bf16[32,1024]{1,0:T(8,128)(2,1)S(1)}, bf16[32,1024]{1,0:T(8,128)(2,1)S(1)}, u32[]{:S(2)}, u32[]{:S(2)}) collective-permute-start(bf16[32,1024]{1,0:T(8,128)(2,1)S(1)} %get-tuple-element.69), channel_id=1, source_target_pairs={{0,4},{1,5},{2,6},{3,7},{4,0},{5,1},{6,2},{7,3},{8,12},{9,13},{10,... | collective-permute-start | bytes 196616 | tf_op jit(solution)/shard_map/ppermute | solution.py:154
  (19 other events, 113.0 us)

commit v4 on v3

--- a/solution.py
+++ b/solution.py
@@ -115,28 +115,40 @@
     )(near_sum, returned)
 
 
-def leave_kernel(step, micro, inflow, own, *refs):
-    parts, (fresh, out, leaving) = refs[:-3], refs[-3:]
-    total = inflow[...].reshape(own.shape).astype(jnp.float32) + own[...]
-    for part in parts:
-        total = total + part[...].astype(jnp.float32)
-    result = total.astype(jnp.bfloat16)
-    out[...] = result
+def leave_kernel(step, micro_count, *refs):
+    fresh, leaving = refs[-2 - micro_count], refs[-1]
+    results = refs[-1 - micro_count : -1]
+    each = (len(refs) - 2 - micro_count) // micro_count
     is_last = lax.axis_index("section") == lax.axis_size("section") - 1
-    arrived = fresh[step, micro].astype(jnp.float32)
-    leaving[...] = jnp.where(is_last, arrived, result.astype(jnp.float32)).astype(jnp.bfloat16)
-
-
-def leave(step, micro, inflow, own, parts, fresh):
+    for micro, out in enumerate(results):
+        inflow, own, *parts = refs[micro * each : (micro + 1) * each]
+        total = inflow[...].astype(jnp.float32) + own[...]
+        for part in parts:
+            total = total + part[...].astype(jnp.float32)
+        result = total.astype(jnp.bfloat16)
+        out[...] = result
+        arrived = fresh[step, micro].astype(jnp.float32)
+        gone = jnp.where(is_last, arrived, result.astype(jnp.float32))
+        leaving[micro] = gone.astype(jnp.bfloat16)
+
+
+def leave(step, inflows, own, parts, fresh):
+    micro_count = len(own)
+    rows = jax.ShapeDtypeStruct(own[0].shape, jnp.bfloat16)
+    operands = []
+    for micro in range(micro_count):
+        operands += [inflows[micro], own[micro], *parts[micro]]
+    operands.append(fresh)
     whole = pl.BlockSpec(memory_space=pltpu.VMEM)
     return pl.pallas_call(
-        functools.partial(leave_kernel, step, micro),
-        out_shape=(jax.ShapeDtypeStruct(own.shape, jnp.bfloat16),) * 2,
-        in_specs=[whole] * (3 + len(parts)),
-        out_specs=[whole] * 2,
+        functools.partial(leave_kernel, step, micro_count),
+        out_shape=(rows,) * micro_count
+        + (jax.ShapeDtypeStruct((micro_count,) + rows.shape, rows.dtype),),
+        in_specs=[whole] * len(operands),
+        out_specs=[whole] * (micro_count + 1),
         compiler_params=pltpu.CompilerParams(vmem_limit_bytes=8 * 1024 * 1024),
         name="leave",
-    )(inflow, own, *parts, fresh)
+    )(*operands)
 
 
 def swap_core(value):
@@ -266,16 +278,19 @@
     outputs = []
     for step in range(steps):
         near, far, own, parts, results = [], [], [], [], []
+        if step > 0:
+            hopped = [next_section(leaving, by) for by in range(outer - 1, -1, -1)]
         for micro in micros:
-            payload = payloads[micro]
             if step == 0:
+                payload = payloads[micro]
                 blocks = [swap_outer(payload, by) for by in range(outer - 1, 0, -1)] + [payload]
             else:
-                blocks = [next_section(payload, by) for by in range(outer - 1, -1, -1)]
+                blocks = [block[micro] for block in hopped]
                 inflows[micro] = blocks[-1]
             near.append(jnp.stack(blocks[::-1]))
             if step == 0 and micro == 0:
-                gain = hold(near[0], own_in, own_out, gain)
+                gain = hold(payload, own_in, own_out, gain)
+                near[0], gain = tied(near[0], gain)
             far.append(swap_inner(near[micro]))
         if step == 0:
             near_tail, far_tail = near, far
@@ -290,19 +305,14 @@
         for micro in micros:
             own[micro], *blocks = combine(own[micro], returned[micro])
             parts.append([swap_outer(blocks[by - 1], by) for by in range(outer - 1, 0, -1)])
-        for micro in micros:
-            if step < steps - 1:
-                if micro < micro_count - 1:
-                    parts[micro][0], own[micro + 1] = tied(parts[micro][0], own[micro + 1])
-                result, payloads[micro] = leave(
-                    step, micro, inflows[micro], own[micro], parts[micro], arriving
-                )
-            else:
+        if step < steps - 1:
+            *results, leaving = leave(step, inflows, own, parts, arriving)
+        else:
+            for micro in micros:
                 total = inflows[micro].astype(jnp.float32) + own[micro]
                 for part in parts[micro]:
                     total = total + part.astype(jnp.float32)
-                result = total.astype(jnp.bfloat16)
-            results.append(result)
+                results.append(total.astype(jnp.bfloat16))
         outputs.append(jnp.stack(results))
     return jnp.stack(outputs)[:, None]
 

time: 104 us -> 99.9 us (0.961)
  starting transfers between devices: 56.6 us -> 48.1 us
  waiting for transfers between devices: 24.6 us -> 32.2 us
  other arithmetic: 2.78 us -> 1.01 us
    ppermute x8, waiting for transfers between devices: 5.26 us -> 15 us  [swap_inner(): return lax.ppermute(value, 'expert', [(i, i ^ 2) for i in range(size)])]
    ppermute x8 -> x4, starting transfers between devices: 13.6 us -> 7.42 us  [next_section(): return lax.ppermute(value, ('section', 'expert'), pairs)]
    ppermute x8, starting transfers between devices: 13.7 us -> 11.3 us  [swap_inner(): return lax.ppermute(value, 'expert', [(i, i ^ 2) for i in range(size)])]
    another operation x4, other arithmetic: 1.93 us -> 0.17 us  [local(): near.append(jnp.stack(blocks[::-1]))]
    ppermute x8 -> x4, waiting for transfers between devices: 6.66 us -> 5.09 us  [next_section(): return lax.ppermute(value, ('section', 'expert'), pairs)]
    unnamed x14 -> x18, local copies, waits for them, and re-layouts: 5.8 us -> 4.89 us
  transfers between devices with their start and end apart: 36 -> 32, of which waited for: 15 -> 20; matrix products, arithmetic and copies ran while one was open for 2% -> 0% of each run, Pallas kernels for 11% -> 11%
where the time goes in v4:
time: 99.9 us; the launch traced here: 99.6 us
  starting transfers between devices  48.1 us (48%)
  waiting for transfers between devices  32.2 us (32%)
  Pallas kernels  13.2 us (13%)
  local copies, waits for them, and re-layouts  4.94 us (5%)
  other arithmetic  1.01 us (1%)
    ppermute x18, starting transfers between devices, swap_outer(): return lax.ppermute(value, 'expert', [(i, i ^ 4 * by) for i in range(size)])  28.8 us
    ppermute x8, waiting for transfers between devices, swap_inner(): return lax.ppermute(value, 'expert', [(i, i ^ 2) for i in range(size)])  15 us
    ppermute x18, waiting for transfers between devices, swap_outer(): return lax.ppermute(value, 'expert', [(i, i ^ 4 * by) for i in range(size)])  12.1 us
    ppermute x8, starting transfers between devices, swap_inner(): return lax.ppermute(value, 'expert', [(i, i ^ 2) for i in range(size)])  11.3 us
    pallas_call x4, Pallas kernels, serve(): pl.pallas_call(functools.partial(serve_kernel, features, hidden_count, ch...  11.1 us
    ppermute x4, starting transfers between devices, next_section(): return lax.ppermute(value, ('section', 'expert'), pairs)  7.42 us
    ppermute x4, waiting for transfers between devices, next_section(): return lax.ppermute(value, ('section', 'expert'), pairs)  5.09 us
    unnamed x18, local copies, waits for them, and re-layouts  4.89 us
  transfers between devices with their start and end apart: 32, of which 20 were waited for; matrix products, arithmetic and copies ran while one was open for 0% of the time, Pallas kernels for 11%

profile of v4, /device:TPU:0, one launch (start us, length us, event | category | flops | bytes accessed | tf_op | source)
XLA Modules:
  0.0 99.6 jit_solution(8838677825914716882)
XLA Ops:
  0.0 1.8 %first_payloads.1 = (bf16[32,1152]{1,0:T(8,128)(2,1)}, bf16[32,1152]{1,0:T(8,128)(2,1)}) custom-call(bf16[2,32,1024]{2,1,0:T(8,128)(2,1)} %bitcast.56, s32[2,2,8,32]{3,2,1,0:T(8,128)} %bitcast.64, f32[2,2,8,32]{3,2,1,0:T(8,128)} %bitcast.65), custom_call_target="tpu_custom_call" | custom-call | tf_op jit(solution)/shard_map/first_payloads/pallas_call | solution.py:63
  2.4 5.0 %collective-permute-start.12 = (bf16[32,1152]{1,0:T(8,128)(2,1)}, bf16[32,1152]{1,0:T(8,128)(2,1)S(1)}, u32[]{:S(2)}, u32[]{:S(2)}) collective-permute-start(bf16[32,1152]{1,0:T(8,128)(2,1)} %get-tuple-element.53), channel_id=1, source_target_pairs={{0,12},{1,13},{2,14},{3,15},{4,8},{5,9},{6,10},{7,11},{8,4},{9,5},... | collective-permute-start | bytes 221192 | tf_op jit(solution)/shard_map/ppermute | solution.py:166
  8.0 1.9 %copy-done = bf16[1,1,1024,1536]{3,2,1,0:T(8,128)(2,1)S(1)} copy-done((bf16[1,1,1024,1536]{3,2,1,0:T(8,128)(2,1)S(1)}, bf16[1,1,1024,1536]{3,2,1,0:T(8,128)(2,1)}, u32[]{:S(2)}) %copy-start) | copy-done | bytes 3145752
  12.9 3.9 %collective-permute-start.2 = (bf16[32,1152]{1,0:T(8,128)(2,1)S(1)}, bf16[32,1152]{1,0:T(8,128)(2,1)S(1)}, u32[]{:S(2)}, u32[]{:S(2)}) collective-permute-start(bf16[32,1152]{1,0:T(8,128)(2,1)S(1)} %copy-done.4), channel_id=1, source_target_pairs={{0,12},{1,13},{2,14},{3,15},{4,8},{5,9},{6,10},{7,11},{8,4},{9,5},... | collective-permute-start | bytes 221192 | tf_op jit(solution)/shard_map/ppermute | solution.py:166
  17.5 2.3 %collective-permute-done.2 = bf16[32,1152]{1,0:T(8,128)(2,1)S(1)} collective-permute-done((bf16[32,1152]{1,0:T(8,128)(2,1)S(1)}, bf16[32,1152]{1,0:T(8,128)(2,1)S(1)}, u32[]{:S(2)}, u32[]{:S(2)}) %collective-permute-start.2) | collective-permute-done | bytes 73760 | tf_op jit(solution)/shard_map/ppermute | solution.py:166
  22.8 1.6 %collective-permute-start.3 = (bf16[4,32,1152]{2,1,0:T(8,128)(2,1)S(1)}, bf16[4,32,1152]{2,1,0:T(8,128)(2,1)S(1)}, u32[]{:S(2)}, u32[]{:S(2)}) collective-permute-start(bf16[4,32,1152]{2,1,0:T(8,128)(2,1)S(1)} %pad_maximum_fusion.near.near_tail), channel_id=1, source_target_pairs={{0,2},{1,3},{2,0},{3,1},{4,6},{5,7},{6,4},{7,5},{8,10},{9,11},{10,... | collective-permute-start | bytes 884744 | tf_op jit(solution)/shard_map/ppermute | solution.py:161
  24.4 3.8 %collective-permute-done.13.far.far_tail = bf16[4,32,1152]{2,1,0:T(8,128)(2,1)S(1)} collective-permute-done((bf16[4,32,1152]{2,1,0:T(8,128)(2,1)S(1)}, bf16[4,32,1152]{2,1,0:T(8,128)(2,1)S(1)}, u32[]{:S(2)}, u32[]{:S(2)}) %collective-permute-start.13) | collective-permute-done | bytes 294944 | tf_op jit(solution)/shard_map/ppermute | solution.py:161
  28.2 2.8 %serve.5 = (f32[4,32,1024]{2,1,0:T(8,128)S(1)}, bf16[4,32,1024]{2,1,0:T(8,128)(2,1)S(1)}) custom-call(bf16[4,32,1152]{2,1,0:T(8,128)(2,1)S(1)} %pad_maximum_fusion.1.near.near_tail, bf16[4,32,1152]{2,1,0:T(8,128)(2,1)S(1)} %collective-permute-done.13.far.far_tail, bf16[4,32,1152]{2,1,0:T(8,128)(2,1)S(1)} %pad_maximum_fusion.1.near.near_tail, ...), custom_call_target="tpu_custom_call" | custom-call | flops 2415919104 | bytes 9437184 | tf_op jit(solution)/shard_map/serve/pallas_call | solution.py:231
  32.5 2.0 %collective-permute-done.3.far.far_tail = bf16[4,32,1152]{2,1,0:T(8,128)(2,1)S(1)} collective-permute-done((bf16[4,32,1152]{2,1,0:T(8,128)(2,1)S(1)}, bf16[4,32,1152]{2,1,0:T(8,128)(2,1)S(1)}, u32[]{:S(2)}, u32[]{:S(2)}) %collective-permute-start.3) | collective-permute-done | bytes 294944 | tf_op jit(solution)/shard_map/ppermute | solution.py:161
  34.5 2.8 %serve.4 = (f32[4,32,1024]{2,1,0:T(8,128)S(1)}, bf16[4,32,1024]{2,1,0:T(8,128)(2,1)S(1)}) custom-call(bf16[4,32,1152]{2,1,0:T(8,128)(2,1)S(1)} %pad_maximum_fusion.near.near_tail, bf16[4,32,1152]{2,1,0:T(8,128)(2,1)S(1)} %collective-permute-done.3.far.far_tail, bf16[4,32,1152]{2,1,0:T(8,128)(2,1)S(1)} %pad_maximum_fusion.near.near_tail, ...), custom_call_target="tpu_custom_call" | custom-call | flops 2415919104 | bytes 9437184 | tf_op jit(solution)/shard_map/serve/pallas_call | solution.py:231
  40.2 4.7 %collective-permute-start.15 = (bf16[32,1024]{1,0:T(8,128)(2,1)S(1)}, bf16[32,1024]{1,0:T(8,128)(2,1)S(1)}, u32[]{:S(2)}, u32[]{:S(2)}) collective-permute-start(bf16[32,1024]{1,0:T(8,128)(2,1)S(1)} %get-tuple-element.57), channel_id=1, source_target_pairs={{0,12},{1,13},{2,14},{3,15},{4,8},{5,9},{6,10},{7,11},{8,4},{9,5},... | collective-permute-start | bytes 196616 | tf_op jit(solution)/shard_map/ppermute | solution.py:166
  45.6 3.8 %collective-permute-start.7 = (bf16[32,1024]{1,0:T(8,128)(2,1)S(1)}, bf16[32,1024]{1,0:T(8,128)(2,1)S(1)}, u32[]{:S(2)}, u32[]{:S(2)}) collective-permute-start(bf16[32,1024]{1,0:T(8,128)(2,1)S(1)} %get-tuple-element.50), channel_id=1, source_target_pairs={{0,12},{1,13},{2,14},{3,15},{4,8},{5,9},{6,10},{7,11},{8,4},{9,5},... | collective-permute-start | bytes 196616 | tf_op jit(solution)/shard_map/ppermute | solution.py:166
  50.6 1.7 %collective-permute-done.7.refs_2_ = bf16[32,1024]{1,0:T(8,128)(2,1)S(1)} collective-permute-done((bf16[32,1024]{1,0:T(8,128)(2,1)S(1)}, bf16[32,1024]{1,0:T(8,128)(2,1)S(1)}, u32[]{:S(2)}, u32[]{:S(2)}) %collective-permute-start.7) | collective-permute-done | bytes 65568 | tf_op jit(solution)/shard_map/ppermute | solution.py:166
  52.3 3.0 %collective-permute-done.8.refs_3_ = bf16[32,1024]{1,0:T(8,128)(2,1)S(1)} collective-permute-done((bf16[32,1024]{1,0:T(8,128)(2,1)S(1)}, bf16[32,1024]{1,0:T(8,128)(2,1)S(1)}, u32[]{:S(2)}, u32[]{:S(2)}) %collective-permute-start.8) | collective-permute-done | bytes 65568 | tf_op jit(solution)/shard_map/ppermute | solution.py:166
  55.4 2.5 %collective-permute-start.21 = (bf16[2,32,1024]{2,1,0:T(8,128)(2,1)S(1)}, bf16[2,32,1024]{2,1,0:T(8,128)(2,1)S(1)}, u32[]{:S(2)}, u32[]{:S(2)}) collective-permute-start(bf16[2,32,1024]{2,1,0:T(8,128)(2,1)S(1)} %get-tuple-element.62), channel_id=1, source_target_pairs={{0,28},{1,29},{2,30},{3,31},{4,24},{5,25},{6,26},{7,27},{8,20},{9,... | collective-permute-start | bytes 393224 | tf_op jit(solution)/shard_map/ppermute | solution.py:176
  58.5 4.3 %collective-permute-start.19 = (bf16[2,32,1024]{2,1,0:T(8,128)(2,1)S(1)}, bf16[2,32,1024]{2,1,0:T(8,128)(2,1)S(1)}, u32[]{:S(2)}, u32[]{:S(2)}) collective-permute-start(bf16[2,32,1024]{2,1,0:T(8,128)(2,1)S(1)} %get-tuple-element.62), channel_id=1, source_target_pairs={{0,20},{1,21},{2,22},{3,23},{4,16},{5,17},{6,18},{7,19},{8,28},{9,... | collective-permute-start | bytes 393224 | tf_op jit(solution)/shard_map/ppermute | solution.py:176
  63.2 3.0 %collective-permute-done.20 = bf16[2,32,1024]{2,1,0:T(8,128)(2,1)S(1)} collective-permute-done((bf16[2,32,1024]{2,1,0:T(8,128)(2,1)S(1)}, bf16[2,32,1024]{2,1,0:T(8,128)(2,1)S(1)}, u32[]{:S(2)}, u32[]{:S(2)}) %collective-permute-start.20) | collective-permute-done | bytes 131104 | tf_op jit(solution)/shard_map/ppermute | solution.py:176
  68.0 1.6 %collective-permute-start.27 = (bf16[4,32,1024]{2,1,0:T(8,128)(2,1)S(1)}, bf16[4,32,1024]{2,1,0:T(8,128)(2,1)S(1)}, u32[]{:S(2)}, u32[]{:S(2)}) collective-permute-start(bf16[4,32,1024]{2,1,0:T(8,128)(2,1)S(1)} %pad_maximum_fusion.3.near), channel_id=1, source_target_pairs={{0,2},{1,3},{2,0},{3,1},{4,6},{5,7},{6,4},{7,5},{8,10},{9,11},{10,... | collective-permute-start | bytes 786440 | tf_op jit(solution)/shard_map/ppermute | solution.py:161
  70.2 6.2 %collective-permute-done.27.far = bf16[4,32,1024]{2,1,0:T(8,128)(2,1)S(1)} collective-permute-done((bf16[4,32,1024]{2,1,0:T(8,128)(2,1)S(1)}, bf16[4,32,1024]{2,1,0:T(8,128)(2,1)S(1)}, u32[]{:S(2)}, u32[]{:S(2)}) %collective-permute-start.27) | collective-permute-done | bytes 262176 | tf_op jit(solution)/shard_map/ppermute | solution.py:161
  76.3 2.8 %serve.7 = (f32[4,32,1024]{2,1,0:T(8,128)S(1)}, bf16[4,32,1024]{2,1,0:T(8,128)(2,1)S(1)}) custom-call(bf16[4,32,1024]{2,1,0:T(8,128)(2,1)S(1)} %pad_maximum_fusion.3.near, bf16[4,32,1024]{2,1,0:T(8,128)(2,1)S(1)} %collective-permute-done.27.far, bf16[4,32,1152]{2,1,0:T(8,128)(2,1)S(1)} %pad_maximum_fusion.1.near.near_tail, ...), custom_call_target="tpu_custom_call" | custom-call | flops 2415919104 | bytes 9437184 | tf_op jit(solution)/shard_map/serve/pallas_call | solution.py:231
  82.0 2.8 %serve.6 = (f32[4,32,1024]{2,1,0:T(8,128)S(1)}, bf16[4,32,1024]{2,1,0:T(8,128)(2,1)S(1)}) custom-call(bf16[4,32,1024]{2,1,0:T(8,128)(2,1)S(1)} %pad_maximum_fusion.2.near, bf16[4,32,1024]{2,1,0:T(8,128)(2,1)S(1)} %collective-permute-done.22.far, bf16[4,32,1152]{2,1,0:T(8,128)(2,1)S(1)} %pad_maximum_fusion.near.near_tail, ...), custom_call_target="tpu_custom_call" | custom-call | flops 2415919104 | bytes 9437184 | tf_op jit(solution)/shard_map/serve/pallas_call | solution.py:231
  88.0 2.9 %collective-permute-start.31 = (bf16[32,1024]{1,0:T(8,128)(2,1)S(1)}, bf16[32,1024]{1,0:T(8,128)(2,1)S(1)}, u32[]{:S(2)}, u32[]{:S(2)}) collective-permute-start(bf16[32,1024]{1,0:T(8,128)(2,1)S(1)} %get-tuple-element.74), channel_id=1, source_target_pairs={{0,4},{1,5},{2,6},{3,7},{4,0},{5,1},{6,2},{7,3},{8,12},{9,13},{10,... | collective-permute-start | bytes 196616 | tf_op jit(solution)/shard_map/ppermute | solution.py:166
  92.6 3.2 %collective-permute-start.26 = (bf16[32,1024]{1,0:T(8,128)(2,1)S(1)}, bf16[32,1024]{1,0:T(8,128)(2,1)S(1)}, u32[]{:S(2)}, u32[]{:S(2)}) collective-permute-start(bf16[32,1024]{1,0:T(8,128)(2,1)S(1)} %get-tuple-element.68), channel_id=1, source_target_pairs={{0,4},{1,5},{2,6},{3,7},{4,0},{5,1},{6,2},{7,3},{8,12},{9,13},{10,... | collective-permute-start | bytes 196616 | tf_op jit(solution)/shard_map/ppermute | solution.py:166
  95.8 1.7 %collective-permute-done.24 = bf16[32,1024]{1,0:T(8,128)(2,1)S(1)} collective-permute-done((bf16[32,1024]{1,0:T(8,128)(2,1)S(1)}, bf16[32,1024]{1,0:T(8,128)(2,1)S(1)}, u32[]{:S(2)}, u32[]{:S(2)}) %collective-permute-start.24) | collective-permute-done | bytes 65568 | tf_op jit(solution)/shard_map/ppermute | solution.py:166
  (82 shorter events, 27.5 us)
Async XLA Ops:
  1.8 26.4 %collective-permute-start.4 = (bf16[1,1024,1536]{2,1,0:T(8,128)(2,1)}, bf16[1,1024,1536]{2,1,0:T(8,128)(2,1)S(1)}, u32[]{:S(2)}, u32[]{:S(2)}) collective-permute-start(bf16[1,1024,1536]{2,1,0:T(8,128)(2,1)} %bitcast.41), channel_id=1, source_target_pairs={{0,1},{1,0},{2,3},{3,2},{4,5},{5,4},{6,7},{7,6},{8,9},{9,8},{10,11... | collective-permute-start | bytes 9437192 | tf_op jit(solution)/shard_map/ppermute | solution.py:156
  2.3 25.9 %collective-permute-start.5 = (bf16[1,768,1024]{2,1,0:T(8,128)(2,1)}, bf16[1,768,1024]{2,1,0:T(8,128)(2,1)S(1)}, u32[]{:S(2)}, u32[]{:S(2)}) collective-permute-start(bf16[1,768,1024]{2,1,0:T(8,128)(2,1)} %bitcast.47), channel_id=1, source_target_pairs={{0,1},{1,0},{2,3},{3,2},{4,5},{5,4},{6,7},{7,6},{8,9},{9,8},{10,11... | collective-permute-start | bytes 4718600 | tf_op jit(solution)/shard_map/ppermute | solution.py:156
  2.4 10.5 %collective-permute-start.12 = (bf16[32,1152]{1,0:T(8,128)(2,1)}, bf16[32,1152]{1,0:T(8,128)(2,1)S(1)}, u32[]{:S(2)}, u32[]{:S(2)}) collective-permute-start(bf16[32,1152]{1,0:T(8,128)(2,1)} %get-tuple-element.53), channel_id=1, source_target_pairs={{0,12},{1,13},{2,14},{3,15},{4,8},{5,9},{6,10},{7,11},{8,4},{9,5},... | collective-permute-start | bytes 221192 | tf_op jit(solution)/shard_map/ppermute | solution.py:166
  7.4 9.3 %collective-permute-start.11 = (bf16[32,1152]{1,0:T(8,128)(2,1)}, bf16[32,1152]{1,0:T(8,128)(2,1)S(1)}, u32[]{:S(2)}, u32[]{:S(2)}) collective-permute-start(bf16[32,1152]{1,0:T(8,128)(2,1)} %get-tuple-element.53), channel_id=1, source_target_pairs={{0,8},{1,9},{2,10},{3,11},{4,12},{5,13},{6,14},{7,15},{8,0},{9,1},... | collective-permute-start | bytes 221192 | tf_op jit(solution)/shard_map/ppermute | solution.py:166
  7.4 9.4 %collective-permute-start.10 = (bf16[32,1152]{1,0:T(8,128)(2,1)}, bf16[32,1152]{1,0:T(8,128)(2,1)S(1)}, u32[]{:S(2)}, u32[]{:S(2)}) collective-permute-start(bf16[32,1152]{1,0:T(8,128)(2,1)} %get-tuple-element.53), channel_id=1, source_target_pairs={{0,4},{1,5},{2,6},{3,7},{4,0},{5,1},{6,2},{7,3},{8,12},{9,13},{10,... | collective-permute-start | bytes 221192 | tf_op jit(solution)/shard_map/ppermute | solution.py:166
  12.9 6.9 %collective-permute-start.2 = (bf16[32,1152]{1,0:T(8,128)(2,1)S(1)}, bf16[32,1152]{1,0:T(8,128)(2,1)S(1)}, u32[]{:S(2)}, u32[]{:S(2)}) collective-permute-start(bf16[32,1152]{1,0:T(8,128)(2,1)S(1)} %copy-done.4), channel_id=1, source_target_pairs={{0,12},{1,13},{2,14},{3,15},{4,8},{5,9},{6,10},{7,11},{8,4},{9,5},... | collective-permute-start | bytes 221192 | tf_op jit(solution)/shard_map/ppermute | solution.py:166
  19.8 8.5 %collective-permute-start.13 = (bf16[4,32,1152]{2,1,0:T(8,128)(2,1)S(1)}, bf16[4,32,1152]{2,1,0:T(8,128)(2,1)S(1)}, u32[]{:S(2)}, u32[]{:S(2)}) collective-permute-start(bf16[4,32,1152]{2,1,0:T(8,128)(2,1)S(1)} %pad_maximum_fusion.1.near.near_tail), channel_id=1, source_target_pairs={{0,2},{1,3},{2,0},{3,1},{4,6},{5,7},{6,4},{7,5},{8,10},{9,11},{10,... | collective-permute-start | bytes 884744 | tf_op jit(solution)/shard_map/ppermute | solution.py:161
  22.8 11.7 %collective-permute-start.3 = (bf16[4,32,1152]{2,1,0:T(8,128)(2,1)S(1)}, bf16[4,32,1152]{2,1,0:T(8,128)(2,1)S(1)}, u32[]{:S(2)}, u32[]{:S(2)}) collective-permute-start(bf16[4,32,1152]{2,1,0:T(8,128)(2,1)S(1)} %pad_maximum_fusion.near.near_tail), channel_id=1, source_target_pairs={{0,2},{1,3},{2,0},{3,1},{4,6},{5,7},{6,4},{7,5},{8,10},{9,11},{10,... | collective-permute-start | bytes 884744 | tf_op jit(solution)/shard_map/ppermute | solution.py:161
  31.1 9.1 %collective-permute-start.14 = (bf16[4,32,1024]{2,1,0:T(8,128)(2,1)S(1)}, bf16[4,32,1024]{2,1,0:T(8,128)(2,1)S(1)}, u32[]{:S(2)}, u32[]{:S(2)}) collective-permute-start(bf16[4,32,1024]{2,1,0:T(8,128)(2,1)S(1)} %get-tuple-element.55), channel_id=1, source_target_pairs={{0,2},{1,3},{2,0},{3,1},{4,6},{5,7},{6,4},{7,5},{8,10},{9,11},{10,... | collective-permute-start | bytes 786440 | tf_op jit(solution)/shard_map/ppermute | solution.py:161
  37.3 8.2 %collective-permute-start.6 = (bf16[4,32,1024]{2,1,0:T(8,128)(2,1)S(1)}, bf16[4,32,1024]{2,1,0:T(8,128)(2,1)S(1)}, u32[]{:S(2)}, u32[]{:S(2)}) collective-permute-start(bf16[4,32,1024]{2,1,0:T(8,128)(2,1)S(1)} %get-tuple-element.48), channel_id=1, source_target_pairs={{0,2},{1,3},{2,0},{3,1},{4,6},{5,7},{6,4},{7,5},{8,10},{9,11},{10,... | collective-permute-start | bytes 786440 | tf_op jit(solution)/shard_map/ppermute | solution.py:161
  40.2 9.3 %collective-permute-start.15 = (bf16[32,1024]{1,0:T(8,128)(2,1)S(1)}, bf16[32,1024]{1,0:T(8,128)(2,1)S(1)}, u32[]{:S(2)}, u32[]{:S(2)}) collective-permute-start(bf16[32,1024]{1,0:T(8,128)(2,1)S(1)} %get-tuple-element.57), channel_id=1, source_target_pairs={{0,12},{1,13},{2,14},{3,15},{4,8},{5,9},{6,10},{7,11},{8,4},{9,5},... | collective-permute-start | bytes 196616 | tf_op jit(solution)/shard_map/ppermute | solution.py:166
  45.6 6.6 %collective-permute-start.7 = (bf16[32,1024]{1,0:T(8,128)(2,1)S(1)}, bf16[32,1024]{1,0:T(8,128)(2,1)S(1)}, u32[]{:S(2)}, u32[]{:S(2)}) collective-permute-start(bf16[32,1024]{1,0:T(8,128)(2,1)S(1)} %get-tuple-element.50), channel_id=1, source_target_pairs={{0,12},{1,13},{2,14},{3,15},{4,8},{5,9},{6,10},{7,11},{8,4},{9,5},... | collective-permute-start | bytes 196616 | tf_op jit(solution)/shard_map/ppermute | solution.py:166
  55.4 7.8 %collective-permute-start.21 = (bf16[2,32,1024]{2,1,0:T(8,128)(2,1)S(1)}, bf16[2,32,1024]{2,1,0:T(8,128)(2,1)S(1)}, u32[]{:S(2)}, u32[]{:S(2)}) collective-permute-start(bf16[2,32,1024]{2,1,0:T(8,128)(2,1)S(1)} %get-tuple-element.62), channel_id=1, source_target_pairs={{0,28},{1,29},{2,30},{3,31},{4,24},{5,25},{6,26},{7,27},{8,20},{9,... | collective-permute-start | bytes 393224 | tf_op jit(solution)/shard_map/ppermute | solution.py:176
  57.9 8.3 %collective-permute-start.20 = (bf16[2,32,1024]{2,1,0:T(8,128)(2,1)S(1)}, bf16[2,32,1024]{2,1,0:T(8,128)(2,1)S(1)}, u32[]{:S(2)}, u32[]{:S(2)}) collective-permute-start(bf16[2,32,1024]{2,1,0:T(8,128)(2,1)S(1)} %get-tuple-element.62), channel_id=1, source_target_pairs={{0,24},{1,25},{2,26},{3,27},{4,28},{5,29},{6,30},{7,31},{8,16},{9,... | collective-permute-start | bytes 393224 | tf_op jit(solution)/shard_map/ppermute | solution.py:176
  58.5 8.0 %collective-permute-start.19 = (bf16[2,32,1024]{2,1,0:T(8,128)(2,1)S(1)}, bf16[2,32,1024]{2,1,0:T(8,128)(2,1)S(1)}, u32[]{:S(2)}, u32[]{:S(2)}) collective-permute-start(bf16[2,32,1024]{2,1,0:T(8,128)(2,1)S(1)} %get-tuple-element.62), channel_id=1, source_target_pairs={{0,20},{1,21},{2,22},{3,23},{4,16},{5,17},{6,18},{7,19},{8,28},{9,... | collective-permute-start | bytes 393224 | tf_op jit(solution)/shard_map/ppermute | solution.py:176
  68.0 8.4 %collective-permute-start.27 = (bf16[4,32,1024]{2,1,0:T(8,128)(2,1)S(1)}, bf16[4,32,1024]{2,1,0:T(8,128)(2,1)S(1)}, u32[]{:S(2)}, u32[]{:S(2)}) collective-permute-start(bf16[4,32,1024]{2,1,0:T(8,128)(2,1)S(1)} %pad_maximum_fusion.3.near), channel_id=1, source_target_pairs={{0,2},{1,3},{2,0},{3,1},{4,6},{5,7},{6,4},{7,5},{8,10},{9,11},{10,... | collective-permute-start | bytes 786440 | tf_op jit(solution)/shard_map/ppermute | solution.py:161
  69.6 12.3 %collective-permute-start.22 = (bf16[4,32,1024]{2,1,0:T(8,128)(2,1)S(1)}, bf16[4,32,1024]{2,1,0:T(8,128)(2,1)S(1)}, u32[]{:S(2)}, u32[]{:S(2)}) collective-permute-start(bf16[4,32,1024]{2,1,0:T(8,128)(2,1)S(1)} %pad_maximum_fusion.2.near), channel_id=1, source_target_pairs={{0,2},{1,3},{2,0},{3,1},{4,6},{5,7},{6,4},{7,5},{8,10},{9,11},{10,... | collective-permute-start | bytes 786440 | tf_op jit(solution)/shard_map/ppermute | solution.py:161
  79.1 7.2 %collective-permute-start.28 = (bf16[4,32,1024]{2,1,0:T(8,128)(2,1)S(1)}, bf16[4,32,1024]{2,1,0:T(8,128)(2,1)S(1)}, u32[]{:S(2)}, u32[]{:S(2)}) collective-permute-start(bf16[4,32,1024]{2,1,0:T(8,128)(2,1)S(1)} %get-tuple-element.70), channel_id=1, source_target_pairs={{0,2},{1,3},{2,0},{3,1},{4,6},{5,7},{6,4},{7,5},{8,10},{9,11},{10,... | collective-permute-start | bytes 786440 | tf_op jit(solution)/shard_map/ppermute | solution.py:161
  84.8 6.4 %collective-permute-start.23 = (bf16[4,32,1024]{2,1,0:T(8,128)(2,1)S(1)}, bf16[4,32,1024]{2,1,0:T(8,128)(2,1)S(1)}, u32[]{:S(2)}, u32[]{:S(2)}) collective-permute-start(bf16[4,32,1024]{2,1,0:T(8,128)(2,1)S(1)} %get-tuple-element.64), channel_id=1, source_target_pairs={{0,2},{1,3},{2,0},{3,1},{4,6},{5,7},{6,4},{7,5},{8,10},{9,11},{10,... | collective-permute-start | bytes 786440 | tf_op jit(solution)/shard_map/ppermute | solution.py:161
  87.9 7.9 %collective-permute-start.30 = (bf16[32,1024]{1,0:T(8,128)(2,1)S(1)}, bf16[32,1024]{1,0:T(8,128)(2,1)S(1)}, u32[]{:S(2)}, u32[]{:S(2)}) collective-permute-start(bf16[32,1024]{1,0:T(8,128)(2,1)S(1)} %get-tuple-element.73), channel_id=1, source_target_pairs={{0,8},{1,9},{2,10},{3,11},{4,12},{5,13},{6,14},{7,15},{8,0},{9,1},... | collective-permute-start | bytes 196616 | tf_op jit(solution)/shard_map/ppermute | solution.py:166
  88.0 7.8 %collective-permute-start.31 = (bf16[32,1024]{1,0:T(8,128)(2,1)S(1)}, bf16[32,1024]{1,0:T(8,128)(2,1)S(1)}, u32[]{:S(2)}, u32[]{:S(2)}) collective-permute-start(bf16[32,1024]{1,0:T(8,128)(2,1)S(1)} %get-tuple-element.74), channel_id=1, source_target_pairs={{0,4},{1,5},{2,6},{3,7},{4,0},{5,1},{6,2},{7,3},{8,12},{9,13},{10,... | collective-permute-start | bytes 196616 | tf_op jit(solution)/shard_map/ppermute | solution.py:166
  91.3 6.2 %collective-permute-start.24 = (bf16[32,1024]{1,0:T(8,128)(2,1)S(1)}, bf16[32,1024]{1,0:T(8,128)(2,1)S(1)}, u32[]{:S(2)}, u32[]{:S(2)}) collective-permute-start(bf16[32,1024]{1,0:T(8,128)(2,1)S(1)} %get-tuple-element.66), channel_id=1, source_target_pairs={{0,12},{1,13},{2,14},{3,15},{4,8},{5,9},{6,10},{7,11},{8,4},{9,5},... | collective-permute-start | bytes 196616 | tf_op jit(solution)/shard_map/ppermute | solution.py:166
  92.4 6.4 %collective-permute-start.25 = (bf16[32,1024]{1,0:T(8,128)(2,1)S(1)}, bf16[32,1024]{1,0:T(8,128)(2,1)S(1)}, u32[]{:S(2)}, u32[]{:S(2)}) collective-permute-start(bf16[32,1024]{1,0:T(8,128)(2,1)S(1)} %get-tuple-element.67), channel_id=1, source_target_pairs={{0,8},{1,9},{2,10},{3,11},{4,12},{5,13},{6,14},{7,15},{8,0},{9,1},... | collective-permute-start | bytes 196616 | tf_op jit(solution)/shard_map/ppermute | solution.py:166
  92.6 6.2 %collective-permute-start.26 = (bf16[32,1024]{1,0:T(8,128)(2,1)S(1)}, bf16[32,1024]{1,0:T(8,128)(2,1)S(1)}, u32[]{:S(2)}, u32[]{:S(2)}) collective-permute-start(bf16[32,1024]{1,0:T(8,128)(2,1)S(1)} %get-tuple-element.68), channel_id=1, source_target_pairs={{0,4},{1,5},{2,6},{3,7},{4,0},{5,1},{6,2},{7,3},{8,12},{9,13},{10,... | collective-permute-start | bytes 196616 | tf_op jit(solution)/shard_map/ppermute | solution.py:166
  (17 other events, 129.3 us)

commit v5 on v4

--- a/solution.py
+++ b/solution.py
@@ -39,7 +39,7 @@
 
 
 def first_kernel(experts_all, inflow_hbm, ids_hbm, weights_hbm, *refs):
-    payloads, (inflow, ids, weights, sem) = refs[:-4], refs[-4:]
+    both, first, inflow, ids, weights, sem = refs
     copies = [
         pltpu.make_async_copy(source, target, sem.at[number])
         for number, (source, target) in enumerate(
@@ -51,10 +51,11 @@
     for copy in copies:
         copy.wait()
     features = inflow.shape[-1]
-    tails = token_weights(experts_all, payloads[0].shape[-1] - features, ids, weights)
-    for micro, payload in enumerate(payloads):
-        payload[:, :features] = inflow[micro]
-        payload[:, features:] = tails[micro]
+    tails = token_weights(experts_all, both.shape[-1] - features, ids, weights)
+    both[:, :, :features] = inflow[...]
+    both[:, :, features:] = tails
+    first[:, :features] = inflow[0]
+    first[:, features:] = tails[0]
 
 
 def first_payloads(inflow, ids, weights, experts_all):
@@ -62,9 +63,12 @@
     width = -(-2 * experts_all * ids.shape[0] // LANES) * LANES
     return pl.pallas_call(
         functools.partial(first_kernel, experts_all),
-        out_shape=(jax.ShapeDtypeStruct((tokens, features + width), jnp.bfloat16),) * micro_count,
+        out_shape=(
+            jax.ShapeDtypeStruct((micro_count, tokens, features + width), jnp.bfloat16),
+            jax.ShapeDtypeStruct((tokens, features + width), jnp.bfloat16),
+        ),
         in_specs=[pl.BlockSpec(memory_space=pltpu.HBM)] * 3,
-        out_specs=[pl.BlockSpec(memory_space=pltpu.VMEM)] * micro_count,
+        out_specs=[pl.BlockSpec(memory_space=pltpu.VMEM)] * 2,
         scratch_shapes=[
             pltpu.VMEM(inflow.shape, inflow.dtype),
             pltpu.VMEM(ids.shape, ids.dtype),
@@ -115,55 +119,70 @@
     )(near_sum, returned)
 
 
-def leave_kernel(step, micro_count, *refs):
-    fresh, leaving = refs[-2 - micro_count], refs[-1]
-    results = refs[-1 - micro_count : -1]
-    each = (len(refs) - 2 - micro_count) // micro_count
+def halve_kernel(kept, received, own, out):
+    half = own.shape[0]
+    own[...] = kept[:half] + received[:half].astype(jnp.float32)
+    out[...] = (kept[half:] + received[half:].astype(jnp.float32)).astype(jnp.bfloat16)
+
+
+def halve(kept, received):
+    blocks, tokens, features = kept.shape
+    whole = pl.BlockSpec(memory_space=pltpu.VMEM)
+    return pl.pallas_call(
+        halve_kernel,
+        out_shape=(
+            jax.ShapeDtypeStruct((blocks // 2, tokens, features), jnp.float32),
+            jax.ShapeDtypeStruct((blocks // 2, tokens, features), jnp.bfloat16),
+        ),
+        in_specs=[whole] * 2,
+        out_specs=[whole] * 2,
+        compiler_params=pltpu.CompilerParams(vmem_limit_bytes=8 * 1024 * 1024),
+        name="halve",
+    )(kept, received)
+
+
+def leave_kernel(step, counts, *refs):
+    outs = len(counts) + 2
+    fresh, results, both, first = refs[-outs - 1], refs[-outs:-2], refs[-2], refs[-1]
     is_last = lax.axis_index("section") == lax.axis_size("section") - 1
+    at = 0
     for micro, out in enumerate(results):
-        inflow, own, *parts = refs[micro * each : (micro + 1) * each]
-        total = inflow[...].astype(jnp.float32) + own[...]
+        inflow, *parts = refs[at : at + counts[micro]]
+        at += counts[micro]
+        total = inflow[...].astype(jnp.float32)
         for part in parts:
-            total = total + part[...].astype(jnp.float32)
+            total = total + part[...].reshape(out.shape).astype(jnp.float32)
         result = total.astype(jnp.bfloat16)
         out[...] = result
         arrived = fresh[step, micro].astype(jnp.float32)
-        gone = jnp.where(is_last, arrived, result.astype(jnp.float32))
-        leaving[micro] = gone.astype(jnp.bfloat16)
-
-
-def leave(step, inflows, own, parts, fresh):
-    micro_count = len(own)
-    rows = jax.ShapeDtypeStruct(own[0].shape, jnp.bfloat16)
-    operands = []
-    for micro in range(micro_count):
-        operands += [inflows[micro], own[micro], *parts[micro]]
+        gone = jnp.where(is_last, arrived, result.astype(jnp.float32)).astype(jnp.bfloat16)
+        both[micro] = gone
+        if micro == 0:
+            first[...] = gone
+
+
+def leave(step, inflows, parts, fresh):
+    rows = jax.ShapeDtypeStruct(inflows[0].shape, jnp.bfloat16)
+    operands, counts = [], []
+    for inflow, some in zip(inflows, parts):
+        operands += [inflow, *some]
+        counts.append(1 + len(some))
     operands.append(fresh)
     whole = pl.BlockSpec(memory_space=pltpu.VMEM)
     return pl.pallas_call(
-        functools.partial(leave_kernel, step, micro_count),
-        out_shape=(rows,) * micro_count
-        + (jax.ShapeDtypeStruct((micro_count,) + rows.shape, rows.dtype),),
+        functools.partial(leave_kernel, step, counts),
+        out_shape=(rows,) * len(inflows)
+        + (jax.ShapeDtypeStruct((len(inflows),) + rows.shape, rows.dtype), rows),
         in_specs=[whole] * len(operands),
-        out_specs=[whole] * (micro_count + 1),
+        out_specs=[whole] * (len(inflows) + 2),
         compiler_params=pltpu.CompilerParams(vmem_limit_bytes=8 * 1024 * 1024),
         name="leave",
     )(*operands)
 
 
-def swap_core(value):
+def swapped(value, mask):
     size = lax.axis_size("expert")
-    return lax.ppermute(value, "expert", [(i, i ^ 1) for i in range(size)])
-
-
-def swap_inner(value):
-    size = lax.axis_size("expert")
-    return lax.ppermute(value, "expert", [(i, i ^ 2) for i in range(size)])
-
-
-def swap_outer(value, by):
-    size = lax.axis_size("expert")
-    return lax.ppermute(value, "expert", [(i, i ^ 4 * by) for i in range(size)])
+    return lax.ppermute(value, "expert", [(i, i ^ mask) for i in range(size)])
 
 
 def next_section(value, by):
@@ -264,54 +283,81 @@
     steps = expert_ids.shape[0]
     micro_count = in_flight.shape[1]
     micros = range(micro_count)
-    payloads = first_payloads(
+    both, first = first_payloads(
         in_flight[0],
         jnp.swapaxes(expert_ids[:, 0], -1, -2),
         jnp.swapaxes(route_weights[:, 0], -1, -2),
         experts_all,
     )
-    *payloads, gate_up, w_down = tied(*payloads, gate_up, w_down)
+    both, first, gate_up, w_down = tied(both, first, gate_up, w_down)
     own_in, own_out = gate_up[0], w_down[0]
-    far_in, far_out = swap_core(own_in), swap_core(own_out)
-    gain = norm_gain
+    far_in, far_out = swapped(own_in, 1), swapped(own_out, 1)
+    gain = hold(first, own_in, own_out, norm_gain)
     inflows = [in_flight[0, micro] for micro in micros]
+    top = outer // 2
+    masks = [4 * bit for bit in (1 << place for place in range(outer.bit_length())) if bit < outer]
+    masks = masks[-2:0:-1] + [2] + masks[:1] * (len(masks) > 1)
+    tails = [None] * micro_count
     outputs = []
     for step in range(steps):
-        near, far, own, parts, results = [], [], [], [], []
-        if step > 0:
-            hopped = [next_section(leaving, by) for by in range(outer - 1, -1, -1)]
+        if step == 0:
+            here = both
+            there = swapped(both, 4 * top)
+            blocks = {by: swapped(first, 4 * by) for by in range(outer - 1, 0, -1) if by != top}
+        else:
+            there = next_section(both, top)
+            blocks = {by: next_section(first, by) for by in range(outer - 1, 0, -1) if by != top}
+            here = next_section(both, 0)
+            inflows = [here[micro] for micro in micros]
+        near, far = [], []
+        here, there, *others = tied(here, there, *blocks.values())
+        blocks = dict(zip(blocks, others))
+        if step == 0:
+            there, gain = tied(there, gain)
         for micro in micros:
-            if step == 0:
-                payload = payloads[micro]
-                blocks = [swap_outer(payload, by) for by in range(outer - 1, 0, -1)] + [payload]
+            if micro == 0:
+                blocks[0], blocks[top] = here[0], there[0]
+                value = jnp.stack([blocks[by] for by in range(outer)])
+                last = 2
             else:
-                blocks = [block[micro] for block in hopped]
-                inflows[micro] = blocks[-1]
-            near.append(jnp.stack(blocks[::-1]))
-            if step == 0 and micro == 0:
-                gain = hold(payload, own_in, own_out, gain)
-                near[0], gain = tied(near[0], gain)
-            far.append(swap_inner(near[micro]))
+                value = jnp.stack([here[micro], there[micro]])
+                for mask in masks[:-1]:
+                    value = jnp.concatenate([value, swapped(value, mask)])
+                last = masks[-1]
+            near.append(value)
+            far.append(swapped(value, last))
         if step == 0:
-            near_tail, far_tail = near, far
-        returned = []
+            tails = list(zip(near, far))
+        sums, sent = [], []
         for micro in micros:
-            near_sum, far_sum = serve(
-                step, near[micro], far[micro], near_tail[micro], far_tail[micro], gain,
+            if micro > 0:
+                far[micro], sums[micro - 1] = tied(far[micro], sums[micro - 1])
+            one_sum, one_sent = serve(
+                step, near[micro], far[micro], *tails[micro], gain,
                 own_in, far_in, own_out, far_out, experts_all,
             )
-            own.append(near_sum)
-            returned.append(swap_inner(far_sum))
+            sums.append(one_sum)
+            sent.append(one_sent)
+        parts = []
         for micro in micros:
-            own[micro], *blocks = combine(own[micro], returned[micro])
-            parts.append([swap_outer(blocks[by - 1], by) for by in range(outer - 1, 0, -1)])
+            if micro == 0:
+                own, *sends = combine(sums[0], swapped(sent[0], 2))
+                returned = [swapped(sends[by - 1], 4 * by) for by in range(outer - 1, 0, -1)]
+            else:
+                own, received = sums[micro], swapped(sent[micro], masks[-1])
+                for mask in ([4 * top] + masks[:-1])[::-1]:
+                    own, rest = halve(own, received)
+                    received = swapped(rest, mask)
+                returned = [received]
+            parts.append([own, *returned])
         if step < steps - 1:
-            *results, leaving = leave(step, inflows, own, parts, arriving)
+            *results, both, first = leave(step, inflows, parts, arriving)
         else:
+            results = []
             for micro in micros:
-                total = inflows[micro].astype(jnp.float32) + own[micro]
+                total = inflows[micro].astype(jnp.float32)
                 for part in parts[micro]:
-                    total = total + part.astype(jnp.float32)
+                    total = total + part.reshape(total.shape).astype(jnp.float32)
                 results.append(total.astype(jnp.bfloat16))
         outputs.append(jnp.stack(results))
     return jnp.stack(outputs)[:, None]

time: 99.9 us -> 104 us (1.041)
  waiting for transfers between devices: 32.2 us -> 42.9 us
  starting transfers between devices: 48.1 us -> 39.9 us
    ppermute x28 -> x25, waiting for transfers between devices: 27.1 us -> 37.8 us  [swapped(): return lax.ppermute(value, 'expert', [(i, i ^ mask) for i in range(size)])]
    ppermute x28 -> x25, starting transfers between devices: 40.6 us -> 34 us  [swapped(): return lax.ppermute(value, 'expert', [(i, i ^ mask) for i in range(size)])]
    ppermute x4, starting transfers between devices: 7.42 us -> 5.91 us  [next_section(): return lax.ppermute(value, ('section', 'expert'), pairs)]
    unnamed x18 -> x16, local copies, waits for them, and re-layouts: 4.89 us -> 4.88 us
  transfers between devices with their start and end apart: 32 -> 29, of which waited for: 20 -> 21; matrix products, arithmetic and copies ran while one was open for 0% -> 1% of each run, Pallas kernels for 11% -> 6%
where the time goes in v5:
time: 104 us; the launch traced here: 103 us
  waiting for transfers between devices  42.9 us (41%)
  starting transfers between devices  39.9 us (38%)
  Pallas kernels  13.3 us (13%)
  local copies, waits for them, and re-layouts  5.86 us (6%)
    ppermute x25, waiting for transfers between devices, swapped(): return lax.ppermute(value, 'expert', [(i, i ^ mask) for i in range(size)])  37.8 us
    ppermute x25, starting transfers between devices, swapped(): return lax.ppermute(value, 'expert', [(i, i ^ mask) for i in range(size)])  34 us
    pallas_call x4, Pallas kernels, serve(): pl.pallas_call(functools.partial(serve_kernel, features, hidden_count, ch...  11.2 us
    ppermute x4, starting transfers between devices, next_section(): return lax.ppermute(value, ('section', 'expert'), pairs)  5.91 us
    ppermute x4, waiting for transfers between devices, next_section(): return lax.ppermute(value, ('section', 'expert'), pairs)  5.09 us
    unnamed x16, local copies, waits for them, and re-layouts  4.88 us
  transfers between devices with their start and end apart: 29, of which 21 were waited for; matrix products, arithmetic and copies ran while one was open for 1% of the time, Pallas kernels for 6%

profile of v5, /device:TPU:0, one launch (start us, length us, event | category | flops | bytes accessed | tf_op | source)
XLA Modules:
  0.0 103.2 jit_solution(11957166771595455702)
XLA Ops:
  0.0 1.8 %first_payloads.1 = (bf16[2,32,1152]{2,1,0:T(8,128)(2,1)}, bf16[32,1152]{1,0:T(8,128)(2,1)}) custom-call(bf16[2,32,1024]{2,1,0:T(8,128)(2,1)} %bitcast.48, s32[2,2,8,32]{3,2,1,0:T(8,128)} %bitcast.53, f32[2,2,8,32]{3,2,1,0:T(8,128)} %bitcast.54), custom_call_target="tpu_custom_call" | custom-call | tf_op jit(solution)/shard_map/first_payloads/pallas_call | solution.py:64
  2.4 4.0 %collective-permute-start = (bf16[2,32,1152]{2,1,0:T(8,128)(2,1)}, bf16[2,32,1152]{2,1,0:T(8,128)(2,1)S(1)}, u32[]{:S(2)}, u32[]{:S(2)}) collective-permute-start(bf16[2,32,1152]{2,1,0:T(8,128)(2,1)} %get-tuple-element.57), channel_id=1, source_target_pairs={{0,8},{1,9},{2,10},{3,11},{4,12},{5,13},{6,14},{7,15},{8,0},{9,1},... | collective-permute-start | bytes 442376 | tf_op jit(solution)/shard_map/ppermute | solution.py:185
  8.0 1.9 %copy-done = bf16[1,1,1024,1536]{3,2,1,0:T(8,128)(2,1)S(1)} copy-done((bf16[1,1,1024,1536]{3,2,1,0:T(8,128)(2,1)S(1)}, bf16[1,1,1024,1536]{3,2,1,0:T(8,128)(2,1)}, u32[]{:S(2)}) %copy-start) | copy-done | bytes 3145752
  17.0 1.9 %collective-permute-start.3 = (bf16[2,32,1152]{2,1,0:T(8,128)(2,1)S(1)}, bf16[2,32,1152]{2,1,0:T(8,128)(2,1)S(1)}, u32[]{:S(2)}, u32[]{:S(2)}) collective-permute-start(bf16[2,32,1152]{2,1,0:T(8,128)(2,1)S(1)} %pad_maximum_fusion.4), channel_id=1, source_target_pairs={{0,2},{1,3},{2,0},{3,1},{4,6},{5,7},{6,4},{7,5},{8,10},{9,11},{10,... | collective-permute-start | bytes 442376 | tf_op jit(solution)/shard_map/ppermute | solution.py:185
  19.3 4.6 %collective-permute-done.3 = bf16[2,32,1152]{2,1,0:T(8,128)(2,1)S(1)} collective-permute-done((bf16[2,32,1152]{2,1,0:T(8,128)(2,1)S(1)}, bf16[2,32,1152]{2,1,0:T(8,128)(2,1)S(1)}, u32[]{:S(2)}, u32[]{:S(2)}) %collective-permute-start.3) | collective-permute-done | bytes 147488 | tf_op jit(solution)/shard_map/ppermute | solution.py:185
  23.9 1.8 %collective-permute-start.4 = (bf16[4,32,1152]{2,1,0:T(8,128)(2,1)S(1)}, bf16[4,32,1152]{2,1,0:T(8,128)(2,1)S(1)}, u32[]{:S(2)}, u32[]{:S(2)}) collective-permute-start(bf16[4,32,1152]{2,1,0:T(8,128)(2,1)S(1)} %pad_maximum_fusion.near.near_tail), channel_id=1, source_target_pairs={{0,4},{1,5},{2,6},{3,7},{4,0},{5,1},{6,2},{7,3},{8,12},{9,13},{10,... | collective-permute-start | bytes 884744 | tf_op jit(solution)/shard_map/ppermute | solution.py:185
  25.8 2.4 %collective-permute-done.5.far.far_tail = bf16[4,32,1152]{2,1,0:T(8,128)(2,1)S(1)} collective-permute-done((bf16[4,32,1152]{2,1,0:T(8,128)(2,1)S(1)}, bf16[4,32,1152]{2,1,0:T(8,128)(2,1)S(1)}, u32[]{:S(2)}, u32[]{:S(2)}) %collective-permute-start.5) | collective-permute-done | bytes 294944 | tf_op jit(solution)/shard_map/ppermute | solution.py:185
  28.2 2.8 %serve.4 = (f32[4,32,1024]{2,1,0:T(8,128)S(1)}, bf16[4,32,1024]{2,1,0:T(8,128)(2,1)S(1)}) custom-call(bf16[4,32,1152]{2,1,0:T(8,128)(2,1)S(1)} %pad_maximum_fusion.1.near.near_tail, bf16[4,32,1152]{2,1,0:T(8,128)(2,1)S(1)} %collective-permute-done.5.far.far_tail, bf16[4,32,1152]{2,1,0:T(8,128)(2,1)S(1)} %pad_maximum_fusion.1.near.near_tail, ...), custom_call_target="tpu_custom_call" | custom-call | flops 2415919104 | bytes 9437184 | tf_op jit(solution)/shard_map/serve/pallas_call | solution.py:250
  31.2 2.8 %serve.5 = (f32[4,32,1024]{2,1,0:T(8,128)S(1)}, bf16[4,32,1024]{2,1,0:T(8,128)(2,1)S(1)}) custom-call(bf16[4,32,1152]{2,1,0:T(8,128)(2,1)S(1)} %pad_maximum_fusion.near.near_tail, bf16[4,32,1152]{2,1,0:T(8,128)(2,1)S(1)} %collective-permute-done.4.far.far_tail, bf16[4,32,1152]{2,1,0:T(8,128)(2,1)S(1)} %pad_maximum_fusion.near.near_tail, ...), custom_call_target="tpu_custom_call" | custom-call | flops 2415919104 | bytes 9437184 | tf_op jit(solution)/shard_map/serve/pallas_call | solution.py:250
  34.0 2.8 %collective-permute-start.12 = (bf16[4,32,1024]{2,1,0:T(8,128)(2,1)S(1)}, bf16[4,32,1024]{2,1,0:T(8,128)(2,1)S(1)}, u32[]{:S(2)}, u32[]{:S(2)}) collective-permute-start(bf16[4,32,1024]{2,1,0:T(8,128)(2,1)S(1)} %get-tuple-element.74), channel_id=1, source_target_pairs={{0,4},{1,5},{2,6},{3,7},{4,0},{5,1},{6,2},{7,3},{8,12},{9,13},{10,... | collective-permute-start | bytes 786440 | tf_op jit(solution)/shard_map/ppermute | solution.py:185
  38.3 4.1 %collective-permute-done.12.received = bf16[4,32,1024]{2,1,0:T(8,128)(2,1)S(1)} collective-permute-done((bf16[4,32,1024]{2,1,0:T(8,128)(2,1)S(1)}, bf16[4,32,1024]{2,1,0:T(8,128)(2,1)S(1)}, u32[]{:S(2)}, u32[]{:S(2)}) %collective-permute-start.12) | collective-permute-done | bytes 262176 | tf_op jit(solution)/shard_map/ppermute | solution.py:185
  44.1 3.6 %collective-permute-start.10 = (bf16[32,1024]{1,0:T(8,128)(2,1)S(1)}, bf16[32,1024]{1,0:T(8,128)(2,1)S(1)}, u32[]{:S(2)}, u32[]{:S(2)}) collective-permute-start(bf16[32,1024]{1,0:T(8,128)(2,1)S(1)} %get-tuple-element.70), channel_id=1, source_target_pairs={{0,8},{1,9},{2,10},{3,11},{4,12},{5,13},{6,14},{7,15},{8,0},{9,1},... | collective-permute-start | bytes 196616 | tf_op jit(solution)/shard_map/ppermute | solution.py:185
  49.3 2.0 %collective-permute-start.14 = (bf16[1,32,1024]{2,1,0:T(8,128)(2,1)S(1)}, bf16[1,32,1024]{2,1,0:T(8,128)(2,1)S(1)}, u32[]{:S(2)}, u32[]{:S(2)}) collective-permute-start(bf16[1,32,1024]{2,1,0:T(8,128)(2,1)S(1)} %get-tuple-element.78), channel_id=1, source_target_pairs={{0,8},{1,9},{2,10},{3,11},{4,12},{5,13},{6,14},{7,15},{8,0},{9,1},... | collective-permute-start | bytes 196616 | tf_op jit(solution)/shard_map/ppermute | solution.py:185
  54.2 2.0 %collective-permute-done.14.refs_7_ = bf16[1,32,1024]{2,1,0:T(8,128)(2,1)S(1)} collective-permute-done((bf16[1,32,1024]{2,1,0:T(8,128)(2,1)S(1)}, bf16[1,32,1024]{2,1,0:T(8,128)(2,1)S(1)}, u32[]{:S(2)}, u32[]{:S(2)}) %collective-permute-start.14) | collective-permute-done | bytes 65568 | tf_op jit(solution)/shard_map/ppermute | solution.py:185
  58.2 2.8 %collective-permute-start.17 = (bf16[32,1024]{1,0:T(8,128)(2,1)S(1)}, bf16[32,1024]{1,0:T(8,128)(2,1)S(1)}, u32[]{:S(2)}, u32[]{:S(2)}) collective-permute-start(bf16[32,1024]{1,0:T(8,128)(2,1)S(1)} %get-tuple-element.82), channel_id=1, source_target_pairs={{0,28},{1,29},{2,30},{3,31},{4,24},{5,25},{6,26},{7,27},{8,20},{9,... | collective-permute-start | bytes 196616 | tf_op jit(solution)/shard_map/ppermute | solution.py:195
  62.2 3.2 %collective-permute-done.17 = bf16[32,1024]{1,0:T(8,128)(2,1)S(1)} collective-permute-done((bf16[32,1024]{1,0:T(8,128)(2,1)S(1)}, bf16[32,1024]{1,0:T(8,128)(2,1)S(1)}, u32[]{:S(2)}, u32[]{:S(2)}) %collective-permute-start.17) | collective-permute-done | bytes 65568 | tf_op jit(solution)/shard_map/ppermute | solution.py:195
  69.6 4.3 %collective-permute-done.19 = bf16[2,32,1024]{2,1,0:T(8,128)(2,1)S(1)} collective-permute-done((bf16[2,32,1024]{2,1,0:T(8,128)(2,1)S(1)}, bf16[2,32,1024]{2,1,0:T(8,128)(2,1)S(1)}, u32[]{:S(2)}, u32[]{:S(2)}) %collective-permute-start.19) | collective-permute-done | bytes 131104 | tf_op jit(solution)/shard_map/ppermute | solution.py:185
  76.7 2.8 %serve.6 = (f32[4,32,1024]{2,1,0:T(8,128)S(1)}, bf16[4,32,1024]{2,1,0:T(8,128)(2,1)S(1)}) custom-call(bf16[4,32,1024]{2,1,0:T(8,128)(2,1)S(1)} %pad_maximum_fusion.3.near, bf16[4,32,1024]{2,1,0:T(8,128)(2,1)S(1)} %collective-permute-done.21.far, bf16[4,32,1152]{2,1,0:T(8,128)(2,1)S(1)} %pad_maximum_fusion.1.near.near_tail, ...), custom_call_target="tpu_custom_call" | custom-call | flops 2415919104 | bytes 9437184 | tf_op jit(solution)/shard_map/serve/pallas_call | solution.py:250
  80.4 2.8 %serve.7 = (f32[4,32,1024]{2,1,0:T(8,128)S(1)}, bf16[4,32,1024]{2,1,0:T(8,128)(2,1)S(1)}) custom-call(bf16[4,32,1024]{2,1,0:T(8,128)(2,1)S(1)} %pad_maximum_fusion.2.near, bf16[4,32,1024]{2,1,0:T(8,128)(2,1)S(1)} %collective-permute-done.20.far, bf16[4,32,1152]{2,1,0:T(8,128)(2,1)S(1)} %pad_maximum_fusion.near.near_tail, ...), custom_call_target="tpu_custom_call" | custom-call | flops 2415919104 | bytes 9437184 | tf_op jit(solution)/shard_map/serve/pallas_call | solution.py:250
  84.9 4.7 %collective-permute-done.26.received = bf16[4,32,1024]{2,1,0:T(8,128)(2,1)S(1)} collective-permute-done((bf16[4,32,1024]{2,1,0:T(8,128)(2,1)S(1)}, bf16[4,32,1024]{2,1,0:T(8,128)(2,1)S(1)}, u32[]{:S(2)}, u32[]{:S(2)}) %collective-permute-start.26) | collective-permute-done | bytes 262176 | tf_op jit(solution)/shard_map/ppermute | solution.py:185
  90.2 2.1 %collective-permute-done.22.returned = bf16[4,32,1024]{2,1,0:T(8,128)(2,1)S(1)} collective-permute-done((bf16[4,32,1024]{2,1,0:T(8,128)(2,1)S(1)}, bf16[4,32,1024]{2,1,0:T(8,128)(2,1)S(1)}, u32[]{:S(2)}, u32[]{:S(2)}) %collective-permute-start.22) | collective-permute-done | bytes 262176 | tf_op jit(solution)/shard_map/ppermute | solution.py:185
  92.3 2.1 %collective-permute-start.23 = (bf16[32,1024]{1,0:T(8,128)(2,1)S(1)}, bf16[32,1024]{1,0:T(8,128)(2,1)S(1)}, u32[]{:S(2)}, u32[]{:S(2)}) collective-permute-start(bf16[32,1024]{1,0:T(8,128)(2,1)S(1)} %get-tuple-element.91), channel_id=1, source_target_pairs={{0,12},{1,13},{2,14},{3,15},{4,8},{5,9},{6,10},{7,11},{8,4},{9,5},... | collective-permute-start | bytes 196616 | tf_op jit(solution)/shard_map/ppermute | solution.py:185
  94.4 2.4 %collective-permute-start.25 = (bf16[32,1024]{1,0:T(8,128)(2,1)S(1)}, bf16[32,1024]{1,0:T(8,128)(2,1)S(1)}, u32[]{:S(2)}, u32[]{:S(2)}) collective-permute-start(bf16[32,1024]{1,0:T(8,128)(2,1)S(1)} %get-tuple-element.93), channel_id=1, source_target_pairs={{0,4},{1,5},{2,6},{3,7},{4,0},{5,1},{6,2},{7,3},{8,12},{9,13},{10,... | collective-permute-start | bytes 196616 | tf_op jit(solution)/shard_map/ppermute | solution.py:185
  99.9 2.5 %collective-permute-done.28 = bf16[1,32,1024]{2,1,0:T(8,128)(2,1)S(1)} collective-permute-done((bf16[1,32,1024]{2,1,0:T(8,128)(2,1)S(1)}, bf16[1,32,1024]{2,1,0:T(8,128)(2,1)S(1)}, u32[]{:S(2)}, u32[]{:S(2)}) %collective-permute-start.28) | collective-permute-done | bytes 65568 | tf_op jit(solution)/shard_map/ppermute | solution.py:185
  (78 shorter events, 34.8 us)
Async XLA Ops:
  1.8 26.4 %collective-permute-start.6 = (bf16[1,1024,1536]{2,1,0:T(8,128)(2,1)}, bf16[1,1024,1536]{2,1,0:T(8,128)(2,1)S(1)}, u32[]{:S(2)}, u32[]{:S(2)}) collective-permute-start(bf16[1,1024,1536]{2,1,0:T(8,128)(2,1)} %bitcast.34), channel_id=1, source_target_pairs={{0,1},{1,0},{2,3},{3,2},{4,5},{5,4},{6,7},{7,6},{8,9},{9,8},{10,11... | collective-permute-start | bytes 9437192 | tf_op jit(solution)/shard_map/ppermute | solution.py:185
  2.3 25.9 %collective-permute-start.7 = (bf16[1,768,1024]{2,1,0:T(8,128)(2,1)}, bf16[1,768,1024]{2,1,0:T(8,128)(2,1)S(1)}, u32[]{:S(2)}, u32[]{:S(2)}) collective-permute-start(bf16[1,768,1024]{2,1,0:T(8,128)(2,1)} %bitcast.40), channel_id=1, source_target_pairs={{0,1},{1,0},{2,3},{3,2},{4,5},{5,4},{6,7},{7,6},{8,9},{9,8},{10,11... | collective-permute-start | bytes 4718600 | tf_op jit(solution)/shard_map/ppermute | solution.py:185
  2.4 13.7 %collective-permute-start = (bf16[2,32,1152]{2,1,0:T(8,128)(2,1)}, bf16[2,32,1152]{2,1,0:T(8,128)(2,1)S(1)}, u32[]{:S(2)}, u32[]{:S(2)}) collective-permute-start(bf16[2,32,1152]{2,1,0:T(8,128)(2,1)} %get-tuple-element.57), channel_id=1, source_target_pairs={{0,8},{1,9},{2,10},{3,11},{4,12},{5,13},{6,14},{7,15},{8,0},{9,1},... | collective-permute-start | bytes 442376 | tf_op jit(solution)/shard_map/ppermute | solution.py:185
  6.4 7.8 %collective-permute-start.1 = (bf16[32,1152]{1,0:T(8,128)(2,1)}, bf16[32,1152]{1,0:T(8,128)(2,1)S(1)}, u32[]{:S(2)}, u32[]{:S(2)}) collective-permute-start(bf16[32,1152]{1,0:T(8,128)(2,1)} %get-tuple-element.56.after), channel_id=1, source_target_pairs={{0,12},{1,13},{2,14},{3,15},{4,8},{5,9},{6,10},{7,11},{8,4},{9,5},... | collective-permute-start | bytes 221192 | tf_op jit(solution)/shard_map/ppermute | solution.py:185
  7.8 7.4 %collective-permute-start.2 = (bf16[32,1152]{1,0:T(8,128)(2,1)}, bf16[32,1152]{1,0:T(8,128)(2,1)S(1)}, u32[]{:S(2)}, u32[]{:S(2)}) collective-permute-start(bf16[32,1152]{1,0:T(8,128)(2,1)} %get-tuple-element.56.after), channel_id=1, source_target_pairs={{0,4},{1,5},{2,6},{3,7},{4,0},{5,1},{6,2},{7,3},{8,12},{9,13},{10,... | collective-permute-start | bytes 221192 | tf_op jit(solution)/shard_map/ppermute | solution.py:185
  17.0 6.8 %collective-permute-start.3 = (bf16[2,32,1152]{2,1,0:T(8,128)(2,1)S(1)}, bf16[2,32,1152]{2,1,0:T(8,128)(2,1)S(1)}, u32[]{:S(2)}, u32[]{:S(2)}) collective-permute-start(bf16[2,32,1152]{2,1,0:T(8,128)(2,1)S(1)} %pad_maximum_fusion.4), channel_id=1, source_target_pairs={{0,2},{1,3},{2,0},{3,1},{4,6},{5,7},{6,4},{7,5},{8,10},{9,11},{10,... | collective-permute-start | bytes 442376 | tf_op jit(solution)/shard_map/ppermute | solution.py:185
  19.0 9.2 %collective-permute-start.5 = (bf16[4,32,1152]{2,1,0:T(8,128)(2,1)S(1)}, bf16[4,32,1152]{2,1,0:T(8,128)(2,1)S(1)}, u32[]{:S(2)}, u32[]{:S(2)}) collective-permute-start(bf16[4,32,1152]{2,1,0:T(8,128)(2,1)S(1)} %pad_maximum_fusion.1.near.near_tail), channel_id=1, source_target_pairs={{0,2},{1,3},{2,0},{3,1},{4,6},{5,7},{6,4},{7,5},{8,10},{9,11},{10,... | collective-permute-start | bytes 884744 | tf_op jit(solution)/shard_map/ppermute | solution.py:185
  23.9 7.3 %collective-permute-start.4 = (bf16[4,32,1152]{2,1,0:T(8,128)(2,1)S(1)}, bf16[4,32,1152]{2,1,0:T(8,128)(2,1)S(1)}, u32[]{:S(2)}, u32[]{:S(2)}) collective-permute-start(bf16[4,32,1152]{2,1,0:T(8,128)(2,1)S(1)} %pad_maximum_fusion.near.near_tail), channel_id=1, source_target_pairs={{0,4},{1,5},{2,6},{3,7},{4,0},{5,1},{6,2},{7,3},{8,12},{9,13},{10,... | collective-permute-start | bytes 884744 | tf_op jit(solution)/shard_map/ppermute | solution.py:185
  34.0 8.4 %collective-permute-start.12 = (bf16[4,32,1024]{2,1,0:T(8,128)(2,1)S(1)}, bf16[4,32,1024]{2,1,0:T(8,128)(2,1)S(1)}, u32[]{:S(2)}, u32[]{:S(2)}) collective-permute-start(bf16[4,32,1024]{2,1,0:T(8,128)(2,1)S(1)} %get-tuple-element.74), channel_id=1, source_target_pairs={{0,4},{1,5},{2,6},{3,7},{4,0},{5,1},{6,2},{7,3},{8,12},{9,13},{10,... | collective-permute-start | bytes 786440 | tf_op jit(solution)/shard_map/ppermute | solution.py:185
  36.8 7.3 %collective-permute-start.8 = (bf16[4,32,1024]{2,1,0:T(8,128)(2,1)S(1)}, bf16[4,32,1024]{2,1,0:T(8,128)(2,1)S(1)}, u32[]{:S(2)}, u32[]{:S(2)}) collective-permute-start(bf16[4,32,1024]{2,1,0:T(8,128)(2,1)S(1)} %get-tuple-element.67), channel_id=1, source_target_pairs={{0,2},{1,3},{2,0},{3,1},{4,6},{5,7},{6,4},{7,5},{8,10},{9,11},{10,... | collective-permute-start | bytes 786440 | tf_op jit(solution)/shard_map/ppermute | solution.py:185
  42.5 6.8 %collective-permute-start.13 = (bf16[2,32,1024]{2,1,0:T(8,128)(2,1)S(1)}, bf16[2,32,1024]{2,1,0:T(8,128)(2,1)S(1)}, u32[]{:S(2)}, u32[]{:S(2)}) collective-permute-start(bf16[2,32,1024]{2,1,0:T(8,128)(2,1)S(1)} %get-tuple-element.76), channel_id=1, source_target_pairs={{0,2},{1,3},{2,0},{3,1},{4,6},{5,7},{6,4},{7,5},{8,10},{9,11},{10,... | collective-permute-start | bytes 393224 | tf_op jit(solution)/shard_map/ppermute | solution.py:185
  44.1 8.7 %collective-permute-start.10 = (bf16[32,1024]{1,0:T(8,128)(2,1)S(1)}, bf16[32,1024]{1,0:T(8,128)(2,1)S(1)}, u32[]{:S(2)}, u32[]{:S(2)}) collective-permute-start(bf16[32,1024]{1,0:T(8,128)(2,1)S(1)} %get-tuple-element.70), channel_id=1, source_target_pairs={{0,8},{1,9},{2,10},{3,11},{4,12},{5,13},{6,14},{7,15},{8,0},{9,1},... | collective-permute-start | bytes 196616 | tf_op jit(solution)/shard_map/ppermute | solution.py:185
  48.0 6.2 %collective-permute-start.9 = (bf16[32,1024]{1,0:T(8,128)(2,1)S(1)}, bf16[32,1024]{1,0:T(8,128)(2,1)S(1)}, u32[]{:S(2)}, u32[]{:S(2)}) collective-permute-start(bf16[32,1024]{1,0:T(8,128)(2,1)S(1)} %get-tuple-element.69), channel_id=1, source_target_pairs={{0,12},{1,13},{2,14},{3,15},{4,8},{5,9},{6,10},{7,11},{8,4},{9,5},... | collective-permute-start | bytes 196616 | tf_op jit(solution)/shard_map/ppermute | solution.py:185
  49.3 6.9 %collective-permute-start.14 = (bf16[1,32,1024]{2,1,0:T(8,128)(2,1)S(1)}, bf16[1,32,1024]{2,1,0:T(8,128)(2,1)S(1)}, u32[]{:S(2)}, u32[]{:S(2)}) collective-permute-start(bf16[1,32,1024]{2,1,0:T(8,128)(2,1)S(1)} %get-tuple-element.78), channel_id=1, source_target_pairs={{0,8},{1,9},{2,10},{3,11},{4,12},{5,13},{6,14},{7,15},{8,0},{9,1},... | collective-permute-start | bytes 196616 | tf_op jit(solution)/shard_map/ppermute | solution.py:185
  56.3 10.5 %collective-permute-start.15 = (bf16[2,32,1024]{2,1,0:T(8,128)(2,1)S(1)}, bf16[2,32,1024]{2,1,0:T(8,128)(2,1)S(1)}, u32[]{:S(2)}, u32[]{:S(2)}) collective-permute-start(bf16[2,32,1024]{2,1,0:T(8,128)(2,1)S(1)} %get-tuple-element.81), channel_id=1, source_target_pairs={{0,16},{1,17},{2,18},{3,19},{4,20},{5,21},{6,22},{7,23},{8,24},{9,... | collective-permute-start | bytes 393224 | tf_op jit(solution)/shard_map/ppermute | solution.py:195
  57.9 9.5 %collective-permute-start.16 = (bf16[2,32,1024]{2,1,0:T(8,128)(2,1)S(1)}, bf16[2,32,1024]{2,1,0:T(8,128)(2,1)S(1)}, u32[]{:S(2)}, u32[]{:S(2)}) collective-permute-start(bf16[2,32,1024]{2,1,0:T(8,128)(2,1)S(1)} %get-tuple-element.81), channel_id=1, source_target_pairs={{0,24},{1,25},{2,26},{3,27},{4,28},{5,29},{6,30},{7,31},{8,16},{9,... | collective-permute-start | bytes 393224 | tf_op jit(solution)/shard_map/ppermute | solution.py:195
  58.2 7.2 %collective-permute-start.17 = (bf16[32,1024]{1,0:T(8,128)(2,1)S(1)}, bf16[32,1024]{1,0:T(8,128)(2,1)S(1)}, u32[]{:S(2)}, u32[]{:S(2)}) collective-permute-start(bf16[32,1024]{1,0:T(8,128)(2,1)S(1)} %get-tuple-element.82), channel_id=1, source_target_pairs={{0,28},{1,29},{2,30},{3,31},{4,24},{5,25},{6,26},{7,27},{8,20},{9,... | collective-permute-start | bytes 196616 | tf_op jit(solution)/shard_map/ppermute | solution.py:195
  67.4 6.5 %collective-permute-start.19 = (bf16[2,32,1024]{2,1,0:T(8,128)(2,1)S(1)}, bf16[2,32,1024]{2,1,0:T(8,128)(2,1)S(1)}, u32[]{:S(2)}, u32[]{:S(2)}) collective-permute-start(bf16[2,32,1024]{2,1,0:T(8,128)(2,1)S(1)} %pad_maximum_fusion.5), channel_id=1, source_target_pairs={{0,2},{1,3},{2,0},{3,1},{4,6},{5,7},{6,4},{7,5},{8,10},{9,11},{10,... | collective-permute-start | bytes 393224 | tf_op jit(solution)/shard_map/ppermute | solution.py:185
  68.2 8.5 %collective-permute-start.21 = (bf16[4,32,1024]{2,1,0:T(8,128)(2,1)S(1)}, bf16[4,32,1024]{2,1,0:T(8,128)(2,1)S(1)}, u32[]{:S(2)}, u32[]{:S(2)}) collective-permute-start(bf16[4,32,1024]{2,1,0:T(8,128)(2,1)S(1)} %pad_maximum_fusion.3.near), channel_id=1, source_target_pairs={{0,2},{1,3},{2,0},{3,1},{4,6},{5,7},{6,4},{7,5},{8,10},{9,11},{10,... | collective-permute-start | bytes 786440 | tf_op jit(solution)/shard_map/ppermute | solution.py:185
  73.9 6.4 %collective-permute-start.20 = (bf16[4,32,1024]{2,1,0:T(8,128)(2,1)S(1)}, bf16[4,32,1024]{2,1,0:T(8,128)(2,1)S(1)}, u32[]{:S(2)}, u32[]{:S(2)}) collective-permute-start(bf16[4,32,1024]{2,1,0:T(8,128)(2,1)S(1)} %pad_maximum_fusion.2.near), channel_id=1, source_target_pairs={{0,4},{1,5},{2,6},{3,7},{4,0},{5,1},{6,2},{7,3},{8,12},{9,13},{10,... | collective-permute-start | bytes 786440 | tf_op jit(solution)/shard_map/ppermute | solution.py:185
  83.2 6.4 %collective-permute-start.26 = (bf16[4,32,1024]{2,1,0:T(8,128)(2,1)S(1)}, bf16[4,32,1024]{2,1,0:T(8,128)(2,1)S(1)}, u32[]{:S(2)}, u32[]{:S(2)}) collective-permute-start(bf16[4,32,1024]{2,1,0:T(8,128)(2,1)S(1)} %get-tuple-element.96), channel_id=1, source_target_pairs={{0,4},{1,5},{2,6},{3,7},{4,0},{5,1},{6,2},{7,3},{8,12},{9,13},{10,... | collective-permute-start | bytes 786440 | tf_op jit(solution)/shard_map/ppermute | solution.py:185
  84.5 7.8 %collective-permute-start.22 = (bf16[4,32,1024]{2,1,0:T(8,128)(2,1)S(1)}, bf16[4,32,1024]{2,1,0:T(8,128)(2,1)S(1)}, u32[]{:S(2)}, u32[]{:S(2)}) collective-permute-start(bf16[4,32,1024]{2,1,0:T(8,128)(2,1)S(1)} %get-tuple-element.89), channel_id=1, source_target_pairs={{0,2},{1,3},{2,0},{3,1},{4,6},{5,7},{6,4},{7,5},{8,10},{9,11},{10,... | collective-permute-start | bytes 786440 | tf_op jit(solution)/shard_map/ppermute | solution.py:185
  89.7 7.2 %collective-permute-start.27 = (bf16[2,32,1024]{2,1,0:T(8,128)(2,1)S(1)}, bf16[2,32,1024]{2,1,0:T(8,128)(2,1)S(1)}, u32[]{:S(2)}, u32[]{:S(2)}) collective-permute-start(bf16[2,32,1024]{2,1,0:T(8,128)(2,1)S(1)} %get-tuple-element.98), channel_id=1, source_target_pairs={{0,2},{1,3},{2,0},{3,1},{4,6},{5,7},{6,4},{7,5},{8,10},{9,11},{10,... | collective-permute-start | bytes 393224 | tf_op jit(solution)/shard_map/ppermute | solution.py:185
  92.3 6.1 %collective-permute-start.23 = (bf16[32,1024]{1,0:T(8,128)(2,1)S(1)}, bf16[32,1024]{1,0:T(8,128)(2,1)S(1)}, u32[]{:S(2)}, u32[]{:S(2)}) collective-permute-start(bf16[32,1024]{1,0:T(8,128)(2,1)S(1)} %get-tuple-element.91), channel_id=1, source_target_pairs={{0,12},{1,13},{2,14},{3,15},{4,8},{5,9},{6,10},{7,11},{8,4},{9,5},... | collective-permute-start | bytes 196616 | tf_op jit(solution)/shard_map/ppermute | solution.py:185
  (13 other events, 108.1 us)

commit v6 on v5

--- a/solution.py
+++ b/solution.py
@@ -117,28 +117,6 @@
         compiler_params=pltpu.CompilerParams(vmem_limit_bytes=8 * 1024 * 1024),
         name="combine",
     )(near_sum, returned)
-
-
-def halve_kernel(kept, received, own, out):
-    half = own.shape[0]
-    own[...] = kept[:half] + received[:half].astype(jnp.float32)
-    out[...] = (kept[half:] + received[half:].astype(jnp.float32)).astype(jnp.bfloat16)
-
-
-def halve(kept, received):
-    blocks, tokens, features = kept.shape
-    whole = pl.BlockSpec(memory_space=pltpu.VMEM)
-    return pl.pallas_call(
-        halve_kernel,
-        out_shape=(
-            jax.ShapeDtypeStruct((blocks // 2, tokens, features), jnp.float32),
-            jax.ShapeDtypeStruct((blocks // 2, tokens, features), jnp.bfloat16),
-        ),
-        in_specs=[whole] * 2,
-        out_specs=[whole] * 2,
-        compiler_params=pltpu.CompilerParams(vmem_limit_bytes=8 * 1024 * 1024),
-        name="halve",
-    )(kept, received)
 
 
 def leave_kernel(step, counts, *refs):
@@ -340,15 +318,16 @@
             sent.append(one_sent)
         parts = []
         for micro in micros:
-            if micro == 0:
-                own, *sends = combine(sums[0], swapped(sent[0], 2))
-                returned = [swapped(sends[by - 1], 4 * by) for by in range(outer - 1, 0, -1)]
-            else:
-                own, received = sums[micro], swapped(sent[micro], masks[-1])
-                for mask in ([4 * top] + masks[:-1])[::-1]:
-                    own, rest = halve(own, received)
-                    received = swapped(rest, mask)
-                returned = [received]
+            own, *sends = combine(sums[micro], swapped(sent[micro], 2 if micro == 0 else masks[-1]))
+            returned = []
+            for number in range(len(sends), 0, -1):
+                if micro == 0:
+                    mask = 4 * number
+                else:
+                    mask = 0
+                    for place, step_mask in enumerate([4 * top] + masks[:-1]):
+                        mask ^= step_mask * (number >> place & 1)
+                returned.append(swapped(sends[number - 1], mask))
             parts.append([own, *returned])
         if step < steps - 1:
             *results, both, first = leave(step, inflows, parts, arriving)

time: 104 us -> 101 us (0.971)
  waiting for transfers between devices: 42.9 us -> 37.8 us
  starting transfers between devices: 39.9 us -> 42.5 us
    ppermute x25 -> x27, waiting for transfers between devices: 37.8 us -> 32.6 us  [swapped(): return lax.ppermute(value, 'expert', [(i, i ^ mask) for i in range(size)])]
    ppermute x25 -> x27, starting transfers between devices: 34 us -> 36.6 us  [swapped(): return lax.ppermute(value, 'expert', [(i, i ^ mask) for i in range(size)])]
  transfers between devices with their start and end apart: 29 -> 31, of which waited for: 21 -> 20; matrix products, arithmetic and copies ran while one was open for 1% -> 1% of each run, Pallas kernels for 6% -> 9%
where the time goes in v6:
time: 101 us
  starting transfers between devices  42.5 us (42%)
  waiting for transfers between devices  37.8 us (37%)
  Pallas kernels  13.3 us (13%)
  local copies, waits for them, and re-layouts  5.85 us (6%)
  other arithmetic  1.03 us (1%)
    ppermute x27, starting transfers between devices, swapped(): return lax.ppermute(value, 'expert', [(i, i ^ mask) for i in range(size)])  36.6 us
    ppermute x27, waiting for transfers between devices, swapped(): return lax.ppermute(value, 'expert', [(i, i ^ mask) for i in range(size)])  32.6 us
    pallas_call x4, Pallas kernels, serve(): pl.pallas_call(functools.partial(serve_kernel, features, hidden_count, ch...  11.1 us
    ppermute x4, starting transfers between devices, next_section(): return lax.ppermute(value, ('section', 'expert'), pairs)  5.91 us
    ppermute x4, waiting for transfers between devices, next_section(): return lax.ppermute(value, ('section', 'expert'), pairs)  5.28 us
    unnamed x16, local copies, waits for them, and re-layouts  4.88 us
  transfers between devices with their start and end apart: 31, of which 20 were waited for; matrix products, arithmetic and copies ran while one was open for 1% of the time, Pallas kernels for 9%

profile of v6, /device:TPU:0, one launch (start us, length us, event | category | flops | bytes accessed | tf_op | source)
XLA Modules:
  0.0 100.7 jit_solution(11822226548104877173)
XLA Ops:
  2.4 4.0 %collective-permute-start = (bf16[2,32,1152]{2,1,0:T(8,128)(2,1)}, bf16[2,32,1152]{2,1,0:T(8,128)(2,1)S(1)}, u32[]{:S(2)}, u32[]{:S(2)}) collective-permute-start(bf16[2,32,1152]{2,1,0:T(8,128)(2,1)} %get-tuple-element.57), channel_id=1, source_target_pairs={{0,8},{1,9},{2,10},{3,11},{4,12},{5,13},{6,14},{7,15},{8,0},{9,1},... | collective-permute-start | bytes 442376 | tf_op jit(solution)/shard_map/ppermute | solution.py:163
  8.0 1.9 %copy-done = bf16[1,1,1024,1536]{3,2,1,0:T(8,128)(2,1)S(1)} copy-done((bf16[1,1,1024,1536]{3,2,1,0:T(8,128)(2,1)S(1)}, bf16[1,1,1024,1536]{3,2,1,0:T(8,128)(2,1)}, u32[]{:S(2)}) %copy-start) | copy-done | bytes 3145752
  17.0 1.9 %collective-permute-start.3 = (bf16[2,32,1152]{2,1,0:T(8,128)(2,1)S(1)}, bf16[2,32,1152]{2,1,0:T(8,128)(2,1)S(1)}, u32[]{:S(2)}, u32[]{:S(2)}) collective-permute-start(bf16[2,32,1152]{2,1,0:T(8,128)(2,1)S(1)} %pad_maximum_fusion.4), channel_id=1, source_target_pairs={{0,2},{1,3},{2,0},{3,1},{4,6},{5,7},{6,4},{7,5},{8,10},{9,11},{10,... | collective-permute-start | bytes 442376 | tf_op jit(solution)/shard_map/ppermute | solution.py:163
  19.3 4.6 %collective-permute-done.3 = bf16[2,32,1152]{2,1,0:T(8,128)(2,1)S(1)} collective-permute-done((bf16[2,32,1152]{2,1,0:T(8,128)(2,1)S(1)}, bf16[2,32,1152]{2,1,0:T(8,128)(2,1)S(1)}, u32[]{:S(2)}, u32[]{:S(2)}) %collective-permute-start.3) | collective-permute-done | bytes 147488 | tf_op jit(solution)/shard_map/ppermute | solution.py:163
  23.9 1.8 %collective-permute-start.4 = (bf16[4,32,1152]{2,1,0:T(8,128)(2,1)S(1)}, bf16[4,32,1152]{2,1,0:T(8,128)(2,1)S(1)}, u32[]{:S(2)}, u32[]{:S(2)}) collective-permute-start(bf16[4,32,1152]{2,1,0:T(8,128)(2,1)S(1)} %pad_maximum_fusion.near.near_tail), channel_id=1, source_target_pairs={{0,4},{1,5},{2,6},{3,7},{4,0},{5,1},{6,2},{7,3},{8,12},{9,13},{10,... | collective-permute-start | bytes 884744 | tf_op jit(solution)/shard_map/ppermute | solution.py:163
  25.8 2.4 %collective-permute-done.5.far.far_tail = bf16[4,32,1152]{2,1,0:T(8,128)(2,1)S(1)} collective-permute-done((bf16[4,32,1152]{2,1,0:T(8,128)(2,1)S(1)}, bf16[4,32,1152]{2,1,0:T(8,128)(2,1)S(1)}, u32[]{:S(2)}, u32[]{:S(2)}) %collective-permute-start.5) | collective-permute-done | bytes 294944 | tf_op jit(solution)/shard_map/ppermute | solution.py:163
  28.2 2.8 %serve.4 = (f32[4,32,1024]{2,1,0:T(8,128)S(1)}, bf16[4,32,1024]{2,1,0:T(8,128)(2,1)S(1)}) custom-call(bf16[4,32,1152]{2,1,0:T(8,128)(2,1)S(1)} %pad_maximum_fusion.1.near.near_tail, bf16[4,32,1152]{2,1,0:T(8,128)(2,1)S(1)} %collective-permute-done.5.far.far_tail, bf16[4,32,1152]{2,1,0:T(8,128)(2,1)S(1)} %pad_maximum_fusion.1.near.near_tail, ...), custom_call_target="tpu_custom_call" | custom-call | flops 2415919104 | bytes 9437184 | tf_op jit(solution)/shard_map/serve/pallas_call | solution.py:228
  31.2 2.8 %serve.5 = (f32[4,32,1024]{2,1,0:T(8,128)S(1)}, bf16[4,32,1024]{2,1,0:T(8,128)(2,1)S(1)}) custom-call(bf16[4,32,1152]{2,1,0:T(8,128)(2,1)S(1)} %pad_maximum_fusion.near.near_tail, bf16[4,32,1152]{2,1,0:T(8,128)(2,1)S(1)} %collective-permute-done.4.far.far_tail, bf16[4,32,1152]{2,1,0:T(8,128)(2,1)S(1)} %pad_maximum_fusion.near.near_tail, ...), custom_call_target="tpu_custom_call" | custom-call | flops 2415919104 | bytes 9437184 | tf_op jit(solution)/shard_map/serve/pallas_call | solution.py:228
  34.0 2.8 %collective-permute-start.12 = (bf16[4,32,1024]{2,1,0:T(8,128)(2,1)S(1)}, bf16[4,32,1024]{2,1,0:T(8,128)(2,1)S(1)}, u32[]{:S(2)}, u32[]{:S(2)}) collective-permute-start(bf16[4,32,1024]{2,1,0:T(8,128)(2,1)S(1)} %get-tuple-element.74), channel_id=1, source_target_pairs={{0,4},{1,5},{2,6},{3,7},{4,0},{5,1},{6,2},{7,3},{8,12},{9,13},{10,... | collective-permute-start | bytes 786440 | tf_op jit(solution)/shard_map/ppermute | solution.py:163
  38.3 4.1 %collective-permute-done.12.returned = bf16[4,32,1024]{2,1,0:T(8,128)(2,1)S(1)} collective-permute-done((bf16[4,32,1024]{2,1,0:T(8,128)(2,1)S(1)}, bf16[4,32,1024]{2,1,0:T(8,128)(2,1)S(1)}, u32[]{:S(2)}, u32[]{:S(2)}) %collective-permute-start.12) | collective-permute-done | bytes 262176 | tf_op jit(solution)/shard_map/ppermute | solution.py:163
  42.5 4.6 %collective-permute-start.13 = (bf16[32,1024]{1,0:T(8,128)(2,1)S(1)}, bf16[32,1024]{1,0:T(8,128)(2,1)S(1)}, u32[]{:S(2)}, u32[]{:S(2)}) collective-permute-start(bf16[32,1024]{1,0:T(8,128)(2,1)S(1)} %get-tuple-element.76), channel_id=1, source_target_pairs={{0,10},{1,11},{2,8},{3,9},{4,14},{5,15},{6,12},{7,13},{8,2},{9,3},... | collective-permute-start | bytes 196616 | tf_op jit(solution)/shard_map/ppermute | solution.py:163
  47.8 2.9 %collective-permute-start.10 = (bf16[32,1024]{1,0:T(8,128)(2,1)S(1)}, bf16[32,1024]{1,0:T(8,128)(2,1)S(1)}, u32[]{:S(2)}, u32[]{:S(2)}) collective-permute-start(bf16[32,1024]{1,0:T(8,128)(2,1)S(1)} %get-tuple-element.70), channel_id=1, source_target_pairs={{0,8},{1,9},{2,10},{3,11},{4,12},{5,13},{6,14},{7,15},{8,0},{9,1},... | collective-permute-start | bytes 196616 | tf_op jit(solution)/shard_map/ppermute | solution.py:163
  53.2 2.2 %collective-permute-done.15.refs_9_ = bf16[32,1024]{1,0:T(8,128)(2,1)S(1)} collective-permute-done((bf16[32,1024]{1,0:T(8,128)(2,1)S(1)}, bf16[32,1024]{1,0:T(8,128)(2,1)S(1)}, u32[]{:S(2)}, u32[]{:S(2)}) %collective-permute-start.15) | collective-permute-done | bytes 65568 | tf_op jit(solution)/shard_map/ppermute | solution.py:163
  60.8 2.6 %collective-permute-start.18 = (bf16[32,1024]{1,0:T(8,128)(2,1)S(1)}, bf16[32,1024]{1,0:T(8,128)(2,1)S(1)}, u32[]{:S(2)}, u32[]{:S(2)}) collective-permute-start(bf16[32,1024]{1,0:T(8,128)(2,1)S(1)} %get-tuple-element.82), channel_id=1, source_target_pairs={{0,28},{1,29},{2,30},{3,31},{4,24},{5,25},{6,26},{7,27},{8,20},{9,... | collective-permute-start | bytes 196616 | tf_op jit(solution)/shard_map/ppermute | solution.py:173
  63.8 4.0 %collective-permute-done.18 = bf16[32,1024]{1,0:T(8,128)(2,1)S(1)} collective-permute-done((bf16[32,1024]{1,0:T(8,128)(2,1)S(1)}, bf16[32,1024]{1,0:T(8,128)(2,1)S(1)}, u32[]{:S(2)}, u32[]{:S(2)}) %collective-permute-start.18) | collective-permute-done | bytes 65568 | tf_op jit(solution)/shard_map/ppermute | solution.py:173
  71.3 3.2 %collective-permute-done.20 = bf16[2,32,1024]{2,1,0:T(8,128)(2,1)S(1)} collective-permute-done((bf16[2,32,1024]{2,1,0:T(8,128)(2,1)S(1)}, bf16[2,32,1024]{2,1,0:T(8,128)(2,1)S(1)}, u32[]{:S(2)}, u32[]{:S(2)}) %collective-permute-start.20) | collective-permute-done | bytes 131104 | tf_op jit(solution)/shard_map/ppermute | solution.py:163
  74.9 2.5 %collective-permute-done.22.far = bf16[4,32,1024]{2,1,0:T(8,128)(2,1)S(1)} collective-permute-done((bf16[4,32,1024]{2,1,0:T(8,128)(2,1)S(1)}, bf16[4,32,1024]{2,1,0:T(8,128)(2,1)S(1)}, u32[]{:S(2)}, u32[]{:S(2)}) %collective-permute-start.22) | collective-permute-done | bytes 262176 | tf_op jit(solution)/shard_map/ppermute | solution.py:163
  77.4 2.8 %serve.6 = (f32[4,32,1024]{2,1,0:T(8,128)S(1)}, bf16[4,32,1024]{2,1,0:T(8,128)(2,1)S(1)}) custom-call(bf16[4,32,1024]{2,1,0:T(8,128)(2,1)S(1)} %pad_maximum_fusion.3.near, bf16[4,32,1024]{2,1,0:T(8,128)(2,1)S(1)} %collective-permute-done.22.far, bf16[4,32,1152]{2,1,0:T(8,128)(2,1)S(1)} %pad_maximum_fusion.1.near.near_tail, ...), custom_call_target="tpu_custom_call" | custom-call | flops 2415919104 | bytes 9437184 | tf_op jit(solution)/shard_map/serve/pallas_call | solution.py:228
  81.0 2.8 %serve.7 = (f32[4,32,1024]{2,1,0:T(8,128)S(1)}, bf16[4,32,1024]{2,1,0:T(8,128)(2,1)S(1)}) custom-call(bf16[4,32,1024]{2,1,0:T(8,128)(2,1)S(1)} %pad_maximum_fusion.2.near, bf16[4,32,1024]{2,1,0:T(8,128)(2,1)S(1)} %collective-permute-done.21.far, bf16[4,32,1152]{2,1,0:T(8,128)(2,1)S(1)} %pad_maximum_fusion.near.near_tail, ...), custom_call_target="tpu_custom_call" | custom-call | flops 2415919104 | bytes 9437184 | tf_op jit(solution)/shard_map/serve/pallas_call | solution.py:228
  84.1 2.5 %collective-permute-done.23.returned = bf16[4,32,1024]{2,1,0:T(8,128)(2,1)S(1)} collective-permute-done((bf16[4,32,1024]{2,1,0:T(8,128)(2,1)S(1)}, bf16[4,32,1024]{2,1,0:T(8,128)(2,1)S(1)}, u32[]{:S(2)}, u32[]{:S(2)}) %collective-permute-start.23) | collective-permute-done | bytes 262176 | tf_op jit(solution)/shard_map/ppermute | solution.py:163
  86.7 2.0 %collective-permute-start.24 = (bf16[32,1024]{1,0:T(8,128)(2,1)S(1)}, bf16[32,1024]{1,0:T(8,128)(2,1)S(1)}, u32[]{:S(2)}, u32[]{:S(2)}) collective-permute-start(bf16[32,1024]{1,0:T(8,128)(2,1)S(1)} %get-tuple-element.91), channel_id=1, source_target_pairs={{0,12},{1,13},{2,14},{3,15},{4,8},{5,9},{6,10},{7,11},{8,4},{9,5},... | collective-permute-start | bytes 196616 | tf_op jit(solution)/shard_map/ppermute | solution.py:163
  88.7 2.5 %collective-permute-start.26 = (bf16[32,1024]{1,0:T(8,128)(2,1)S(1)}, bf16[32,1024]{1,0:T(8,128)(2,1)S(1)}, u32[]{:S(2)}, u32[]{:S(2)}) collective-permute-start(bf16[32,1024]{1,0:T(8,128)(2,1)S(1)} %get-tuple-element.93), channel_id=1, source_target_pairs={{0,4},{1,5},{2,6},{3,7},{4,0},{5,1},{6,2},{7,3},{8,12},{9,13},{10,... | collective-permute-start | bytes 196616 | tf_op jit(solution)/shard_map/ppermute | solution.py:163
  92.8 1.9 %collective-permute-start.29 = (bf16[32,1024]{1,0:T(8,128)(2,1)S(1)}, bf16[32,1024]{1,0:T(8,128)(2,1)S(1)}, u32[]{:S(2)}, u32[]{:S(2)}) collective-permute-start(bf16[32,1024]{1,0:T(8,128)(2,1)S(1)} %get-tuple-element.99), channel_id=1, source_target_pairs={{0,2},{1,3},{2,0},{3,1},{4,6},{5,7},{6,4},{7,5},{8,10},{9,11},{10,... | collective-permute-start | bytes 196616 | tf_op jit(solution)/shard_map/ppermute | solution.py:163
  94.7 1.9 %collective-permute-start.30 = (bf16[32,1024]{1,0:T(8,128)(2,1)S(1)}, bf16[32,1024]{1,0:T(8,128)(2,1)S(1)}, u32[]{:S(2)}, u32[]{:S(2)}) collective-permute-start(bf16[32,1024]{1,0:T(8,128)(2,1)S(1)} %get-tuple-element.100), channel_id=1, source_target_pairs={{0,8},{1,9},{2,10},{3,11},{4,12},{5,13},{6,14},{7,15},{8,0},{9,1},... | collective-permute-start | bytes 196616 | tf_op jit(solution)/shard_map/ppermute | solution.py:163
  (79 shorter events, 33.1 us)
Async XLA Ops:
  1.8 26.4 %collective-permute-start.6 = (bf16[1,1024,1536]{2,1,0:T(8,128)(2,1)}, bf16[1,1024,1536]{2,1,0:T(8,128)(2,1)S(1)}, u32[]{:S(2)}, u32[]{:S(2)}) collective-permute-start(bf16[1,1024,1536]{2,1,0:T(8,128)(2,1)} %bitcast.41), channel_id=1, source_target_pairs={{0,1},{1,0},{2,3},{3,2},{4,5},{5,4},{6,7},{7,6},{8,9},{9,8},{10,11... | collective-permute-start | bytes 9437192 | tf_op jit(solution)/shard_map/ppermute | solution.py:163
  2.3 25.9 %collective-permute-start.7 = (bf16[1,768,1024]{2,1,0:T(8,128)(2,1)}, bf16[1,768,1024]{2,1,0:T(8,128)(2,1)S(1)}, u32[]{:S(2)}, u32[]{:S(2)}) collective-permute-start(bf16[1,768,1024]{2,1,0:T(8,128)(2,1)} %bitcast.47), channel_id=1, source_target_pairs={{0,1},{1,0},{2,3},{3,2},{4,5},{5,4},{6,7},{7,6},{8,9},{9,8},{10,11... | collective-permute-start | bytes 4718600 | tf_op jit(solution)/shard_map/ppermute | solution.py:163
  2.4 13.7 %collective-permute-start = (bf16[2,32,1152]{2,1,0:T(8,128)(2,1)}, bf16[2,32,1152]{2,1,0:T(8,128)(2,1)S(1)}, u32[]{:S(2)}, u32[]{:S(2)}) collective-permute-start(bf16[2,32,1152]{2,1,0:T(8,128)(2,1)} %get-tuple-element.57), channel_id=1, source_target_pairs={{0,8},{1,9},{2,10},{3,11},{4,12},{5,13},{6,14},{7,15},{8,0},{9,1},... | collective-permute-start | bytes 442376 | tf_op jit(solution)/shard_map/ppermute | solution.py:163
  6.4 7.8 %collective-permute-start.1 = (bf16[32,1152]{1,0:T(8,128)(2,1)}, bf16[32,1152]{1,0:T(8,128)(2,1)S(1)}, u32[]{:S(2)}, u32[]{:S(2)}) collective-permute-start(bf16[32,1152]{1,0:T(8,128)(2,1)} %get-tuple-element.56.after), channel_id=1, source_target_pairs={{0,12},{1,13},{2,14},{3,15},{4,8},{5,9},{6,10},{7,11},{8,4},{9,5},... | collective-permute-start | bytes 221192 | tf_op jit(solution)/shard_map/ppermute | solution.py:163
  7.8 7.4 %collective-permute-start.2 = (bf16[32,1152]{1,0:T(8,128)(2,1)}, bf16[32,1152]{1,0:T(8,128)(2,1)S(1)}, u32[]{:S(2)}, u32[]{:S(2)}) collective-permute-start(bf16[32,1152]{1,0:T(8,128)(2,1)} %get-tuple-element.56.after), channel_id=1, source_target_pairs={{0,4},{1,5},{2,6},{3,7},{4,0},{5,1},{6,2},{7,3},{8,12},{9,13},{10,... | collective-permute-start | bytes 221192 | tf_op jit(solution)/shard_map/ppermute | solution.py:163
  17.0 6.8 %collective-permute-start.3 = (bf16[2,32,1152]{2,1,0:T(8,128)(2,1)S(1)}, bf16[2,32,1152]{2,1,0:T(8,128)(2,1)S(1)}, u32[]{:S(2)}, u32[]{:S(2)}) collective-permute-start(bf16[2,32,1152]{2,1,0:T(8,128)(2,1)S(1)} %pad_maximum_fusion.4), channel_id=1, source_target_pairs={{0,2},{1,3},{2,0},{3,1},{4,6},{5,7},{6,4},{7,5},{8,10},{9,11},{10,... | collective-permute-start | bytes 442376 | tf_op jit(solution)/shard_map/ppermute | solution.py:163
  19.0 9.2 %collective-permute-start.5 = (bf16[4,32,1152]{2,1,0:T(8,128)(2,1)S(1)}, bf16[4,32,1152]{2,1,0:T(8,128)(2,1)S(1)}, u32[]{:S(2)}, u32[]{:S(2)}) collective-permute-start(bf16[4,32,1152]{2,1,0:T(8,128)(2,1)S(1)} %pad_maximum_fusion.1.near.near_tail), channel_id=1, source_target_pairs={{0,2},{1,3},{2,0},{3,1},{4,6},{5,7},{6,4},{7,5},{8,10},{9,11},{10,... | collective-permute-start | bytes 884744 | tf_op jit(solution)/shard_map/ppermute | solution.py:163
  23.9 7.3 %collective-permute-start.4 = (bf16[4,32,1152]{2,1,0:T(8,128)(2,1)S(1)}, bf16[4,32,1152]{2,1,0:T(8,128)(2,1)S(1)}, u32[]{:S(2)}, u32[]{:S(2)}) collective-permute-start(bf16[4,32,1152]{2,1,0:T(8,128)(2,1)S(1)} %pad_maximum_fusion.near.near_tail), channel_id=1, source_target_pairs={{0,4},{1,5},{2,6},{3,7},{4,0},{5,1},{6,2},{7,3},{8,12},{9,13},{10,... | collective-permute-start | bytes 884744 | tf_op jit(solution)/shard_map/ppermute | solution.py:163
  34.0 8.4 %collective-permute-start.12 = (bf16[4,32,1024]{2,1,0:T(8,128)(2,1)S(1)}, bf16[4,32,1024]{2,1,0:T(8,128)(2,1)S(1)}, u32[]{:S(2)}, u32[]{:S(2)}) collective-permute-start(bf16[4,32,1024]{2,1,0:T(8,128)(2,1)S(1)} %get-tuple-element.74), channel_id=1, source_target_pairs={{0,4},{1,5},{2,6},{3,7},{4,0},{5,1},{6,2},{7,3},{8,12},{9,13},{10,... | collective-permute-start | bytes 786440 | tf_op jit(solution)/shard_map/ppermute | solution.py:163
  36.8 10.9 %collective-permute-start.8 = (bf16[4,32,1024]{2,1,0:T(8,128)(2,1)S(1)}, bf16[4,32,1024]{2,1,0:T(8,128)(2,1)S(1)}, u32[]{:S(2)}, u32[]{:S(2)}) collective-permute-start(bf16[4,32,1024]{2,1,0:T(8,128)(2,1)S(1)} %get-tuple-element.67), channel_id=1, source_target_pairs={{0,2},{1,3},{2,0},{3,1},{4,6},{5,7},{6,4},{7,5},{8,10},{9,11},{10,... | collective-permute-start | bytes 786440 | tf_op jit(solution)/shard_map/ppermute | solution.py:163
  42.5 9.1 %collective-permute-start.13 = (bf16[32,1024]{1,0:T(8,128)(2,1)S(1)}, bf16[32,1024]{1,0:T(8,128)(2,1)S(1)}, u32[]{:S(2)}, u32[]{:S(2)}) collective-permute-start(bf16[32,1024]{1,0:T(8,128)(2,1)S(1)} %get-tuple-element.76), channel_id=1, source_target_pairs={{0,10},{1,11},{2,8},{3,9},{4,14},{5,15},{6,12},{7,13},{8,2},{9,3},... | collective-permute-start | bytes 196616 | tf_op jit(solution)/shard_map/ppermute | solution.py:163
  47.6 7.9 %collective-permute-start.15 = (bf16[32,1024]{1,0:T(8,128)(2,1)S(1)}, bf16[32,1024]{1,0:T(8,128)(2,1)S(1)}, u32[]{:S(2)}, u32[]{:S(2)}) collective-permute-start(bf16[32,1024]{1,0:T(8,128)(2,1)S(1)} %get-tuple-element.78), channel_id=1, source_target_pairs={{0,8},{1,9},{2,10},{3,11},{4,12},{5,13},{6,14},{7,15},{8,0},{9,1},... | collective-permute-start | bytes 196616 | tf_op jit(solution)/shard_map/ppermute | solution.py:163
  47.8 8.8 %collective-permute-start.10 = (bf16[32,1024]{1,0:T(8,128)(2,1)S(1)}, bf16[32,1024]{1,0:T(8,128)(2,1)S(1)}, u32[]{:S(2)}, u32[]{:S(2)}) collective-permute-start(bf16[32,1024]{1,0:T(8,128)(2,1)S(1)} %get-tuple-element.70), channel_id=1, source_target_pairs={{0,8},{1,9},{2,10},{3,11},{4,12},{5,13},{6,14},{7,15},{8,0},{9,1},... | collective-permute-start | bytes 196616 | tf_op jit(solution)/shard_map/ppermute | solution.py:163
  51.6 6.2 %collective-permute-start.9 = (bf16[32,1024]{1,0:T(8,128)(2,1)S(1)}, bf16[32,1024]{1,0:T(8,128)(2,1)S(1)}, u32[]{:S(2)}, u32[]{:S(2)}) collective-permute-start(bf16[32,1024]{1,0:T(8,128)(2,1)S(1)} %get-tuple-element.69), channel_id=1, source_target_pairs={{0,12},{1,13},{2,14},{3,15},{4,8},{5,9},{6,10},{7,11},{8,4},{9,5},... | collective-permute-start | bytes 196616 | tf_op jit(solution)/shard_map/ppermute | solution.py:163
  57.9 11.2 %collective-permute-start.16 = (bf16[2,32,1024]{2,1,0:T(8,128)(2,1)S(1)}, bf16[2,32,1024]{2,1,0:T(8,128)(2,1)S(1)}, u32[]{:S(2)}, u32[]{:S(2)}) collective-permute-start(bf16[2,32,1024]{2,1,0:T(8,128)(2,1)S(1)} %get-tuple-element.81), channel_id=1, source_target_pairs={{0,16},{1,17},{2,18},{3,19},{4,20},{5,21},{6,22},{7,23},{8,24},{9,... | collective-permute-start | bytes 393224 | tf_op jit(solution)/shard_map/ppermute | solution.py:173
  59.4 9.6 %collective-permute-start.17 = (bf16[2,32,1024]{2,1,0:T(8,128)(2,1)S(1)}, bf16[2,32,1024]{2,1,0:T(8,128)(2,1)S(1)}, u32[]{:S(2)}, u32[]{:S(2)}) collective-permute-start(bf16[2,32,1024]{2,1,0:T(8,128)(2,1)S(1)} %get-tuple-element.81), channel_id=1, source_target_pairs={{0,24},{1,25},{2,26},{3,27},{4,28},{5,29},{6,30},{7,31},{8,16},{9,... | collective-permute-start | bytes 393224 | tf_op jit(solution)/shard_map/ppermute | solution.py:173
  60.8 7.0 %collective-permute-start.18 = (bf16[32,1024]{1,0:T(8,128)(2,1)S(1)}, bf16[32,1024]{1,0:T(8,128)(2,1)S(1)}, u32[]{:S(2)}, u32[]{:S(2)}) collective-permute-start(bf16[32,1024]{1,0:T(8,128)(2,1)S(1)} %get-tuple-element.82), channel_id=1, source_target_pairs={{0,28},{1,29},{2,30},{3,31},{4,24},{5,25},{6,26},{7,27},{8,20},{9,... | collective-permute-start | bytes 196616 | tf_op jit(solution)/shard_map/ppermute | solution.py:173
  70.0 7.4 %collective-permute-start.22 = (bf16[4,32,1024]{2,1,0:T(8,128)(2,1)S(1)}, bf16[4,32,1024]{2,1,0:T(8,128)(2,1)S(1)}, u32[]{:S(2)}, u32[]{:S(2)}) collective-permute-start(bf16[4,32,1024]{2,1,0:T(8,128)(2,1)S(1)} %pad_maximum_fusion.3.near), channel_id=1, source_target_pairs={{0,2},{1,3},{2,0},{3,1},{4,6},{5,7},{6,4},{7,5},{8,10},{9,11},{10,... | collective-permute-start | bytes 786440 | tf_op jit(solution)/shard_map/ppermute | solution.py:163
  74.6 6.4 %collective-permute-start.21 = (bf16[4,32,1024]{2,1,0:T(8,128)(2,1)S(1)}, bf16[4,32,1024]{2,1,0:T(8,128)(2,1)S(1)}, u32[]{:S(2)}, u32[]{:S(2)}) collective-permute-start(bf16[4,32,1024]{2,1,0:T(8,128)(2,1)S(1)} %pad_maximum_fusion.2.near), channel_id=1, source_target_pairs={{0,4},{1,5},{2,6},{3,7},{4,0},{5,1},{6,2},{7,3},{8,12},{9,13},{10,... | collective-permute-start | bytes 786440 | tf_op jit(solution)/shard_map/ppermute | solution.py:163
  80.2 6.4 %collective-permute-start.23 = (bf16[4,32,1024]{2,1,0:T(8,128)(2,1)S(1)}, bf16[4,32,1024]{2,1,0:T(8,128)(2,1)S(1)}, u32[]{:S(2)}, u32[]{:S(2)}) collective-permute-start(bf16[4,32,1024]{2,1,0:T(8,128)(2,1)S(1)} %get-tuple-element.89), channel_id=1, source_target_pairs={{0,2},{1,3},{2,0},{3,1},{4,6},{5,7},{6,4},{7,5},{8,10},{9,11},{10,... | collective-permute-start | bytes 786440 | tf_op jit(solution)/shard_map/ppermute | solution.py:163
  83.8 8.3 %collective-permute-start.27 = (bf16[4,32,1024]{2,1,0:T(8,128)(2,1)S(1)}, bf16[4,32,1024]{2,1,0:T(8,128)(2,1)S(1)}, u32[]{:S(2)}, u32[]{:S(2)}) collective-permute-start(bf16[4,32,1024]{2,1,0:T(8,128)(2,1)S(1)} %get-tuple-element.96), channel_id=1, source_target_pairs={{0,4},{1,5},{2,6},{3,7},{4,0},{5,1},{6,2},{7,3},{8,12},{9,13},{10,... | collective-permute-start | bytes 786440 | tf_op jit(solution)/shard_map/ppermute | solution.py:163
  86.7 8.0 %collective-permute-start.24 = (bf16[32,1024]{1,0:T(8,128)(2,1)S(1)}, bf16[32,1024]{1,0:T(8,128)(2,1)S(1)}, u32[]{:S(2)}, u32[]{:S(2)}) collective-permute-start(bf16[32,1024]{1,0:T(8,128)(2,1)S(1)} %get-tuple-element.91), channel_id=1, source_target_pairs={{0,12},{1,13},{2,14},{3,15},{4,8},{5,9},{6,10},{7,11},{8,4},{9,5},... | collective-permute-start | bytes 196616 | tf_op jit(solution)/shard_map/ppermute | solution.py:163
  88.7 8.0 %collective-permute-start.25 = (bf16[32,1024]{1,0:T(8,128)(2,1)S(1)}, bf16[32,1024]{1,0:T(8,128)(2,1)S(1)}, u32[]{:S(2)}, u32[]{:S(2)}) collective-permute-start(bf16[32,1024]{1,0:T(8,128)(2,1)S(1)} %get-tuple-element.92), channel_id=1, source_target_pairs={{0,8},{1,9},{2,10},{3,11},{4,12},{5,13},{6,14},{7,15},{8,0},{9,1},... | collective-permute-start | bytes 196616 | tf_op jit(solution)/shard_map/ppermute | solution.py:163
  88.7 8.0 %collective-permute-start.26 = (bf16[32,1024]{1,0:T(8,128)(2,1)S(1)}, bf16[32,1024]{1,0:T(8,128)(2,1)S(1)}, u32[]{:S(2)}, u32[]{:S(2)}) collective-permute-start(bf16[32,1024]{1,0:T(8,128)(2,1)S(1)} %get-tuple-element.93), channel_id=1, source_target_pairs={{0,4},{1,5},{2,6},{3,7},{4,0},{5,1},{6,2},{7,3},{8,12},{9,13},{10,... | collective-permute-start | bytes 196616 | tf_op jit(solution)/shard_map/ppermute | solution.py:163
  (15 other events, 124.0 us)

commit v7 on v6

--- a/solution.py
+++ b/solution.py
@@ -251,6 +251,13 @@
 
 def tied(*values):
     return lax.optimization_barrier(values)
+
+
+def summed(inflow, parts):
+    total = inflow.astype(jnp.float32)
+    for part in parts:
+        total = total + part.reshape(total.shape).astype(jnp.float32)
+    return total.astype(jnp.bfloat16)
 
 
 def local(in_flight, arriving, norm_gain, gate_up, w_down, expert_ids, route_weights):
@@ -318,7 +325,10 @@
             sent.append(one_sent)
         parts = []
         for micro in micros:
-            own, *sends = combine(sums[micro], swapped(sent[micro], 2 if micro == 0 else masks[-1]))
+            back = swapped(sent[micro], 2 if micro == 0 else masks[-1])
+            if micro > 0:
+                back, parts[micro - 1][0] = tied(back, parts[micro - 1][0])
+            own, *sends = combine(sums[micro], back)
             returned = []
             for number in range(len(sends), 0, -1):
                 if micro == 0:
@@ -330,14 +340,10 @@
                 returned.append(swapped(sends[number - 1], mask))
             parts.append([own, *returned])
         if step < steps - 1:
+            inflows[0], parts[0] = summed(inflows[0], parts[0]), []
             *results, both, first = leave(step, inflows, parts, arriving)
         else:
-            results = []
-            for micro in micros:
-                total = inflows[micro].astype(jnp.float32)
-                for part in parts[micro]:
-                    total = total + part.reshape(total.shape).astype(jnp.float32)
-                results.append(total.astype(jnp.bfloat16))
+            results = [summed(inflows[micro], parts[micro]) for micro in micros]
         outputs.append(jnp.stack(results))
     return jnp.stack(outputs)[:, None]
 

time: 101 us -> 103 us (1.020)
  starting transfers between devices: 42.5 us -> 45.6 us
  waiting for transfers between devices: 37.8 us -> 36.3 us
    ppermute x27, starting transfers between devices: 36.6 us -> 38.2 us  [swapped(): return lax.ppermute(value, 'expert', [(i, i ^ mask) for i in range(size)])]
    ppermute x4, starting transfers between devices: 5.91 us -> 7.38 us  [next_section(): return lax.ppermute(value, ('section', 'expert'), pairs)]
    ppermute x27, waiting for transfers between devices: 32.6 us -> 31.1 us  [swapped(): return lax.ppermute(value, 'expert', [(i, i ^ mask) for i in range(size)])]
  transfers between devices with their start and end apart: 31 -> 31, of which waited for: 20 -> 18; matrix products, arithmetic and copies ran while one was open for 1% -> 1% of each run, Pallas kernels for 9% -> 11%
where the time goes in v7:
time: 103 us; the launch traced here: 102 us
  starting transfers between devices  45.6 us (44%)
  waiting for transfers between devices  36.3 us (35%)
  Pallas kernels  13.2 us (13%)
  local copies, waits for them, and re-layouts  5.85 us (6%)
  other arithmetic  1.08 us (1%)
    ppermute x27, starting transfers between devices, swapped(): return lax.ppermute(value, 'expert', [(i, i ^ mask) for i in range(size)])  38.2 us
    ppermute x27, waiting for transfers between devices, swapped(): return lax.ppermute(value, 'expert', [(i, i ^ mask) for i in range(size)])  31.1 us
    pallas_call x4, Pallas kernels, serve(): pl.pallas_call(functools.partial(serve_kernel, features, hidden_count, ch...  11.1 us
    ppermute x4, starting transfers between devices, next_section(): return lax.ppermute(value, ('section', 'expert'), pairs)  7.38 us
    ppermute x4, waiting for transfers between devices, next_section(): return lax.ppermute(value, ('section', 'expert'), pairs)  5.17 us
    unnamed x16, local copies, waits for them, and re-layouts  4.88 us
  transfers between devices with their start and end apart: 31, of which 18 were waited for; matrix products, arithmetic and copies ran while one was open for 1% of the time, Pallas kernels for 11%

profile of v7, /device:TPU:0, one launch (start us, length us, event | category | flops | bytes accessed | tf_op | source)
XLA Modules:
  0.0 102.3 jit_solution(9979319448985146293)
XLA Ops:
  0.0 1.8 %first_payloads.1 = (bf16[2,32,1152]{2,1,0:T(8,128)(2,1)}, bf16[32,1152]{1,0:T(8,128)(2,1)}) custom-call(bf16[2,32,1024]{2,1,0:T(8,128)(2,1)} %bitcast.56, s32[2,2,8,32]{3,2,1,0:T(8,128)} %bitcast.61, f32[2,2,8,32]{3,2,1,0:T(8,128)} %bitcast.62), custom_call_target="tpu_custom_call" | custom-call | tf_op jit(solution)/shard_map/first_payloads/pallas_call | solution.py:64
  2.4 4.0 %collective-permute-start = (bf16[2,32,1152]{2,1,0:T(8,128)(2,1)}, bf16[2,32,1152]{2,1,0:T(8,128)(2,1)S(1)}, u32[]{:S(2)}, u32[]{:S(2)}) collective-permute-start(bf16[2,32,1152]{2,1,0:T(8,128)(2,1)} %get-tuple-element.61), channel_id=1, source_target_pairs={{0,8},{1,9},{2,10},{3,11},{4,12},{5,13},{6,14},{7,15},{8,0},{9,1},... | collective-permute-start | bytes 442376 | tf_op jit(solution)/shard_map/ppermute | solution.py:163
  8.0 1.9 %copy-done = bf16[1,1,1024,1536]{3,2,1,0:T(8,128)(2,1)S(1)} copy-done((bf16[1,1,1024,1536]{3,2,1,0:T(8,128)(2,1)S(1)}, bf16[1,1,1024,1536]{3,2,1,0:T(8,128)(2,1)}, u32[]{:S(2)}) %copy-start) | copy-done | bytes 3145752
  17.0 1.9 %collective-permute-start.3 = (bf16[2,32,1152]{2,1,0:T(8,128)(2,1)S(1)}, bf16[2,32,1152]{2,1,0:T(8,128)(2,1)S(1)}, u32[]{:S(2)}, u32[]{:S(2)}) collective-permute-start(bf16[2,32,1152]{2,1,0:T(8,128)(2,1)S(1)} %pad_maximum_fusion.4), channel_id=1, source_target_pairs={{0,2},{1,3},{2,0},{3,1},{4,6},{5,7},{6,4},{7,5},{8,10},{9,11},{10,... | collective-permute-start | bytes 442376 | tf_op jit(solution)/shard_map/ppermute | solution.py:163
  19.3 4.6 %collective-permute-done.3 = bf16[2,32,1152]{2,1,0:T(8,128)(2,1)S(1)} collective-permute-done((bf16[2,32,1152]{2,1,0:T(8,128)(2,1)S(1)}, bf16[2,32,1152]{2,1,0:T(8,128)(2,1)S(1)}, u32[]{:S(2)}, u32[]{:S(2)}) %collective-permute-start.3) | collective-permute-done | bytes 147488 | tf_op jit(solution)/shard_map/ppermute | solution.py:163
  23.9 1.8 %collective-permute-start.4 = (bf16[4,32,1152]{2,1,0:T(8,128)(2,1)S(1)}, bf16[4,32,1152]{2,1,0:T(8,128)(2,1)S(1)}, u32[]{:S(2)}, u32[]{:S(2)}) collective-permute-start(bf16[4,32,1152]{2,1,0:T(8,128)(2,1)S(1)} %pad_maximum_fusion.near.near_tail), channel_id=1, source_target_pairs={{0,4},{1,5},{2,6},{3,7},{4,0},{5,1},{6,2},{7,3},{8,12},{9,13},{10,... | collective-permute-start | bytes 884744 | tf_op jit(solution)/shard_map/ppermute | solution.py:163
  25.8 2.4 %collective-permute-done.5.far.far_tail = bf16[4,32,1152]{2,1,0:T(8,128)(2,1)S(1)} collective-permute-done((bf16[4,32,1152]{2,1,0:T(8,128)(2,1)S(1)}, bf16[4,32,1152]{2,1,0:T(8,128)(2,1)S(1)}, u32[]{:S(2)}, u32[]{:S(2)}) %collective-permute-start.5) | collective-permute-done | bytes 294944 | tf_op jit(solution)/shard_map/ppermute | solution.py:163
  28.2 2.8 %serve.4 = (f32[4,32,1024]{2,1,0:T(8,128)S(1)}, bf16[4,32,1024]{2,1,0:T(8,128)(2,1)S(1)}) custom-call(bf16[4,32,1152]{2,1,0:T(8,128)(2,1)S(1)} %pad_maximum_fusion.1.near.near_tail, bf16[4,32,1152]{2,1,0:T(8,128)(2,1)S(1)} %collective-permute-done.5.far.far_tail, bf16[4,32,1152]{2,1,0:T(8,128)(2,1)S(1)} %pad_maximum_fusion.1.near.near_tail, ...), custom_call_target="tpu_custom_call" | custom-call | flops 2415919104 | bytes 9437184 | tf_op jit(solution)/shard_map/serve/pallas_call | solution.py:228
  32.3 2.8 %serve.5 = (f32[4,32,1024]{2,1,0:T(8,128)S(1)}, bf16[4,32,1024]{2,1,0:T(8,128)(2,1)S(1)}) custom-call(bf16[4,32,1152]{2,1,0:T(8,128)(2,1)S(1)} %pad_maximum_fusion.near.near_tail, bf16[4,32,1152]{2,1,0:T(8,128)(2,1)S(1)} %collective-permute-done.4.far.far_tail, bf16[4,32,1152]{2,1,0:T(8,128)(2,1)S(1)} %pad_maximum_fusion.near.near_tail, ...), custom_call_target="tpu_custom_call" | custom-call | flops 2415919104 | bytes 9437184 | tf_op jit(solution)/shard_map/serve/pallas_call | solution.py:228
  35.1 3.2 %collective-permute-start.8 = (bf16[4,32,1024]{2,1,0:T(8,128)(2,1)S(1)}, bf16[4,32,1024]{2,1,0:T(8,128)(2,1)S(1)}, u32[]{:S(2)}, u32[]{:S(2)}) collective-permute-start(bf16[4,32,1024]{2,1,0:T(8,128)(2,1)S(1)} %get-tuple-element.71), channel_id=1, source_target_pairs={{0,4},{1,5},{2,6},{3,7},{4,0},{5,1},{6,2},{7,3},{8,12},{9,13},{10,... | collective-permute-start | bytes 786440 | tf_op jit(solution)/shard_map/ppermute | solution.py:163
  38.4 4.0 %collective-permute-start.10 = (bf16[32,1024]{1,0:T(8,128)(2,1)S(1)}, bf16[32,1024]{1,0:T(8,128)(2,1)S(1)}, u32[]{:S(2)}, u32[]{:S(2)}) collective-permute-start(bf16[32,1024]{1,0:T(8,128)(2,1)S(1)} %get-tuple-element.76), channel_id=1, source_target_pairs={{0,12},{1,13},{2,14},{3,15},{4,8},{5,9},{6,10},{7,11},{8,4},{9,5},... | collective-permute-start | bytes 196616 | tf_op jit(solution)/shard_map/ppermute | solution.py:163
  45.1 4.3 %collective-permute-start.13 = (bf16[32,1024]{1,0:T(8,128)(2,1)S(1)}, bf16[32,1024]{1,0:T(8,128)(2,1)S(1)}, u32[]{:S(2)}, u32[]{:S(2)}) collective-permute-start(bf16[32,1024]{1,0:T(8,128)(2,1)S(1)} %get-tuple-element.82), channel_id=1, source_target_pairs={{0,10},{1,11},{2,8},{3,9},{4,14},{5,15},{6,12},{7,13},{8,2},{9,3},... | collective-permute-start | bytes 196616 | tf_op jit(solution)/shard_map/ppermute | solution.py:163
  51.1 2.8 %collective-permute-done.13.refs_3_ = bf16[32,1024]{1,0:T(8,128)(2,1)S(1)} collective-permute-done((bf16[32,1024]{1,0:T(8,128)(2,1)S(1)}, bf16[32,1024]{1,0:T(8,128)(2,1)S(1)}, u32[]{:S(2)}, u32[]{:S(2)}) %collective-permute-start.13) | collective-permute-done | bytes 65568 | tf_op jit(solution)/shard_map/ppermute | solution.py:163
  54.0 2.2 %collective-permute-done.15.refs_5_ = bf16[32,1024]{1,0:T(8,128)(2,1)S(1)} collective-permute-done((bf16[32,1024]{1,0:T(8,128)(2,1)S(1)}, bf16[32,1024]{1,0:T(8,128)(2,1)S(1)}, u32[]{:S(2)}, u32[]{:S(2)}) %collective-permute-start.15) | collective-permute-done | bytes 65568 | tf_op jit(solution)/shard_map/ppermute | solution.py:163
  57.8 5.8 %collective-permute-start.18 = (bf16[32,1024]{1,0:T(8,128)(2,1)S(1)}, bf16[32,1024]{1,0:T(8,128)(2,1)S(1)}, u32[]{:S(2)}, u32[]{:S(2)}) collective-permute-start(bf16[32,1024]{1,0:T(8,128)(2,1)S(1)} %get-tuple-element.88), channel_id=1, source_target_pairs={{0,28},{1,29},{2,30},{3,31},{4,24},{5,25},{6,26},{7,27},{8,20},{9,... | collective-permute-start | bytes 196616 | tf_op jit(solution)/shard_map/ppermute | solution.py:173
  63.6 3.7 %collective-permute-done.18 = bf16[32,1024]{1,0:T(8,128)(2,1)S(1)} collective-permute-done((bf16[32,1024]{1,0:T(8,128)(2,1)S(1)}, bf16[32,1024]{1,0:T(8,128)(2,1)S(1)}, u32[]{:S(2)}, u32[]{:S(2)}) %collective-permute-start.18) | collective-permute-done | bytes 65568 | tf_op jit(solution)/shard_map/ppermute | solution.py:173
  69.0 2.1 %collective-permute-start.22 = (bf16[4,32,1024]{2,1,0:T(8,128)(2,1)S(1)}, bf16[4,32,1024]{2,1,0:T(8,128)(2,1)S(1)}, u32[]{:S(2)}, u32[]{:S(2)}) collective-permute-start(bf16[4,32,1024]{2,1,0:T(8,128)(2,1)S(1)} %pad_maximum_fusion.3.near), channel_id=1, source_target_pairs={{0,2},{1,3},{2,0},{3,1},{4,6},{5,7},{6,4},{7,5},{8,10},{9,11},{10,... | collective-permute-start | bytes 786440 | tf_op jit(solution)/shard_map/ppermute | solution.py:163
  71.0 2.8 %collective-permute-done.20 = bf16[2,32,1024]{2,1,0:T(8,128)(2,1)S(1)} collective-permute-done((bf16[2,32,1024]{2,1,0:T(8,128)(2,1)S(1)}, bf16[2,32,1024]{2,1,0:T(8,128)(2,1)S(1)}, u32[]{:S(2)}, u32[]{:S(2)}) %collective-permute-start.20) | collective-permute-done | bytes 131104 | tf_op jit(solution)/shard_map/ppermute | solution.py:163
  74.0 4.8 %collective-permute-done.22.far = bf16[4,32,1024]{2,1,0:T(8,128)(2,1)S(1)} collective-permute-done((bf16[4,32,1024]{2,1,0:T(8,128)(2,1)S(1)}, bf16[4,32,1024]{2,1,0:T(8,128)(2,1)S(1)}, u32[]{:S(2)}, u32[]{:S(2)}) %collective-permute-start.22) | collective-permute-done | bytes 262176 | tf_op jit(solution)/shard_map/ppermute | solution.py:163
  78.8 2.8 %serve.6 = (f32[4,32,1024]{2,1,0:T(8,128)S(1)}, bf16[4,32,1024]{2,1,0:T(8,128)(2,1)S(1)}) custom-call(bf16[4,32,1024]{2,1,0:T(8,128)(2,1)S(1)} %pad_maximum_fusion.3.near, bf16[4,32,1024]{2,1,0:T(8,128)(2,1)S(1)} %collective-permute-done.22.far, bf16[4,32,1152]{2,1,0:T(8,128)(2,1)S(1)} %pad_maximum_fusion.1.near.near_tail, ...), custom_call_target="tpu_custom_call" | custom-call | flops 2415919104 | bytes 9437184 | tf_op jit(solution)/shard_map/serve/pallas_call | solution.py:228
  83.0 2.8 %serve.7 = (f32[4,32,1024]{2,1,0:T(8,128)S(1)}, bf16[4,32,1024]{2,1,0:T(8,128)(2,1)S(1)}) custom-call(bf16[4,32,1024]{2,1,0:T(8,128)(2,1)S(1)} %pad_maximum_fusion.2.near, bf16[4,32,1024]{2,1,0:T(8,128)(2,1)S(1)} %collective-permute-done.21.far, bf16[4,32,1152]{2,1,0:T(8,128)(2,1)S(1)} %pad_maximum_fusion.near.near_tail, ...), custom_call_target="tpu_custom_call" | custom-call | flops 2415919104 | bytes 9437184 | tf_op jit(solution)/shard_map/serve/pallas_call | solution.py:228
  85.9 3.5 %collective-permute-done.24.returned = bf16[4,32,1024]{2,1,0:T(8,128)(2,1)S(1)} collective-permute-done((bf16[4,32,1024]{2,1,0:T(8,128)(2,1)S(1)}, bf16[4,32,1024]{2,1,0:T(8,128)(2,1)S(1)}, u32[]{:S(2)}, u32[]{:S(2)}) %collective-permute-start.24) | collective-permute-done | bytes 262176 | tf_op jit(solution)/shard_map/ppermute | solution.py:163
  89.6 4.3 %collective-permute-start.27 = (bf16[32,1024]{1,0:T(8,128)(2,1)S(1)}, bf16[32,1024]{1,0:T(8,128)(2,1)S(1)}, u32[]{:S(2)}, u32[]{:S(2)}) collective-permute-start(bf16[32,1024]{1,0:T(8,128)(2,1)S(1)} %get-tuple-element.102), channel_id=1, source_target_pairs={{0,4},{1,5},{2,6},{3,7},{4,0},{5,1},{6,2},{7,3},{8,12},{9,13},{10,... | collective-permute-start | bytes 196616 | tf_op jit(solution)/shard_map/ppermute | solution.py:163
  95.6 2.8 %collective-permute-start.30 = (bf16[32,1024]{1,0:T(8,128)(2,1)S(1)}, bf16[32,1024]{1,0:T(8,128)(2,1)S(1)}, u32[]{:S(2)}, u32[]{:S(2)}) collective-permute-start(bf16[32,1024]{1,0:T(8,128)(2,1)S(1)} %get-tuple-element.108), channel_id=1, source_target_pairs={{0,8},{1,9},{2,10},{3,11},{4,12},{5,13},{6,14},{7,15},{8,0},{9,1},... | collective-permute-start | bytes 196616 | tf_op jit(solution)/shard_map/ppermute | solution.py:163
  (80 shorter events, 26.0 us)
Async XLA Ops:
  1.8 26.4 %collective-permute-start.6 = (bf16[1,1024,1536]{2,1,0:T(8,128)(2,1)}, bf16[1,1024,1536]{2,1,0:T(8,128)(2,1)S(1)}, u32[]{:S(2)}, u32[]{:S(2)}) collective-permute-start(bf16[1,1024,1536]{2,1,0:T(8,128)(2,1)} %bitcast.42), channel_id=1, source_target_pairs={{0,1},{1,0},{2,3},{3,2},{4,5},{5,4},{6,7},{7,6},{8,9},{9,8},{10,11... | collective-permute-start | bytes 9437192 | tf_op jit(solution)/shard_map/ppermute | solution.py:163
  2.3 25.9 %collective-permute-start.7 = (bf16[1,768,1024]{2,1,0:T(8,128)(2,1)}, bf16[1,768,1024]{2,1,0:T(8,128)(2,1)S(1)}, u32[]{:S(2)}, u32[]{:S(2)}) collective-permute-start(bf16[1,768,1024]{2,1,0:T(8,128)(2,1)} %bitcast.48), channel_id=1, source_target_pairs={{0,1},{1,0},{2,3},{3,2},{4,5},{5,4},{6,7},{7,6},{8,9},{9,8},{10,11... | collective-permute-start | bytes 4718600 | tf_op jit(solution)/shard_map/ppermute | solution.py:163
  2.4 13.7 %collective-permute-start = (bf16[2,32,1152]{2,1,0:T(8,128)(2,1)}, bf16[2,32,1152]{2,1,0:T(8,128)(2,1)S(1)}, u32[]{:S(2)}, u32[]{:S(2)}) collective-permute-start(bf16[2,32,1152]{2,1,0:T(8,128)(2,1)} %get-tuple-element.61), channel_id=1, source_target_pairs={{0,8},{1,9},{2,10},{3,11},{4,12},{5,13},{6,14},{7,15},{8,0},{9,1},... | collective-permute-start | bytes 442376 | tf_op jit(solution)/shard_map/ppermute | solution.py:163
  6.4 7.8 %collective-permute-start.1 = (bf16[32,1152]{1,0:T(8,128)(2,1)}, bf16[32,1152]{1,0:T(8,128)(2,1)S(1)}, u32[]{:S(2)}, u32[]{:S(2)}) collective-permute-start(bf16[32,1152]{1,0:T(8,128)(2,1)} %get-tuple-element.60.after), channel_id=1, source_target_pairs={{0,12},{1,13},{2,14},{3,15},{4,8},{5,9},{6,10},{7,11},{8,4},{9,5},... | collective-permute-start | bytes 221192 | tf_op jit(solution)/shard_map/ppermute | solution.py:163
  7.8 7.4 %collective-permute-start.2 = (bf16[32,1152]{1,0:T(8,128)(2,1)}, bf16[32,1152]{1,0:T(8,128)(2,1)S(1)}, u32[]{:S(2)}, u32[]{:S(2)}) collective-permute-start(bf16[32,1152]{1,0:T(8,128)(2,1)} %get-tuple-element.60.after), channel_id=1, source_target_pairs={{0,4},{1,5},{2,6},{3,7},{4,0},{5,1},{6,2},{7,3},{8,12},{9,13},{10,... | collective-permute-start | bytes 221192 | tf_op jit(solution)/shard_map/ppermute | solution.py:163
  17.0 6.8 %collective-permute-start.3 = (bf16[2,32,1152]{2,1,0:T(8,128)(2,1)S(1)}, bf16[2,32,1152]{2,1,0:T(8,128)(2,1)S(1)}, u32[]{:S(2)}, u32[]{:S(2)}) collective-permute-start(bf16[2,32,1152]{2,1,0:T(8,128)(2,1)S(1)} %pad_maximum_fusion.4), channel_id=1, source_target_pairs={{0,2},{1,3},{2,0},{3,1},{4,6},{5,7},{6,4},{7,5},{8,10},{9,11},{10,... | collective-permute-start | bytes 442376 | tf_op jit(solution)/shard_map/ppermute | solution.py:163
  19.0 9.2 %collective-permute-start.5 = (bf16[4,32,1152]{2,1,0:T(8,128)(2,1)S(1)}, bf16[4,32,1152]{2,1,0:T(8,128)(2,1)S(1)}, u32[]{:S(2)}, u32[]{:S(2)}) collective-permute-start(bf16[4,32,1152]{2,1,0:T(8,128)(2,1)S(1)} %pad_maximum_fusion.1.near.near_tail), channel_id=1, source_target_pairs={{0,2},{1,3},{2,0},{3,1},{4,6},{5,7},{6,4},{7,5},{8,10},{9,11},{10,... | collective-permute-start | bytes 884744 | tf_op jit(solution)/shard_map/ppermute | solution.py:163
  23.9 8.4 %collective-permute-start.4 = (bf16[4,32,1152]{2,1,0:T(8,128)(2,1)S(1)}, bf16[4,32,1152]{2,1,0:T(8,128)(2,1)S(1)}, u32[]{:S(2)}, u32[]{:S(2)}) collective-permute-start(bf16[4,32,1152]{2,1,0:T(8,128)(2,1)S(1)} %pad_maximum_fusion.near.near_tail), channel_id=1, source_target_pairs={{0,4},{1,5},{2,6},{3,7},{4,0},{5,1},{6,2},{7,3},{8,12},{9,13},{10,... | collective-permute-start | bytes 884744 | tf_op jit(solution)/shard_map/ppermute | solution.py:163
  31.0 7.3 %collective-permute-start.9 = (bf16[4,32,1024]{2,1,0:T(8,128)(2,1)S(1)}, bf16[4,32,1024]{2,1,0:T(8,128)(2,1)S(1)}, u32[]{:S(2)}, u32[]{:S(2)}) collective-permute-start(bf16[4,32,1024]{2,1,0:T(8,128)(2,1)S(1)} %get-tuple-element.73), channel_id=1, source_target_pairs={{0,2},{1,3},{2,0},{3,1},{4,6},{5,7},{6,4},{7,5},{8,10},{9,11},{10,... | collective-permute-start | bytes 786440 | tf_op jit(solution)/shard_map/ppermute | solution.py:163
  35.1 10.0 %collective-permute-start.8 = (bf16[4,32,1024]{2,1,0:T(8,128)(2,1)S(1)}, bf16[4,32,1024]{2,1,0:T(8,128)(2,1)S(1)}, u32[]{:S(2)}, u32[]{:S(2)}) collective-permute-start(bf16[4,32,1024]{2,1,0:T(8,128)(2,1)S(1)} %get-tuple-element.71), channel_id=1, source_target_pairs={{0,4},{1,5},{2,6},{3,7},{4,0},{5,1},{6,2},{7,3},{8,12},{9,13},{10,... | collective-permute-start | bytes 786440 | tf_op jit(solution)/shard_map/ppermute | solution.py:163
  38.4 12.6 %collective-permute-start.10 = (bf16[32,1024]{1,0:T(8,128)(2,1)S(1)}, bf16[32,1024]{1,0:T(8,128)(2,1)S(1)}, u32[]{:S(2)}, u32[]{:S(2)}) collective-permute-start(bf16[32,1024]{1,0:T(8,128)(2,1)S(1)} %get-tuple-element.76), channel_id=1, source_target_pairs={{0,12},{1,13},{2,14},{3,15},{4,8},{5,9},{6,10},{7,11},{8,4},{9,5},... | collective-permute-start | bytes 196616 | tf_op jit(solution)/shard_map/ppermute | solution.py:163
  42.4 8.6 %collective-permute-start.11 = (bf16[32,1024]{1,0:T(8,128)(2,1)S(1)}, bf16[32,1024]{1,0:T(8,128)(2,1)S(1)}, u32[]{:S(2)}, u32[]{:S(2)}) collective-permute-start(bf16[32,1024]{1,0:T(8,128)(2,1)S(1)} %get-tuple-element.77), channel_id=1, source_target_pairs={{0,8},{1,9},{2,10},{3,11},{4,12},{5,13},{6,14},{7,15},{8,0},{9,1},... | collective-permute-start | bytes 196616 | tf_op jit(solution)/shard_map/ppermute | solution.py:163
  43.4 7.6 %collective-permute-start.12 = (bf16[32,1024]{1,0:T(8,128)(2,1)S(1)}, bf16[32,1024]{1,0:T(8,128)(2,1)S(1)}, u32[]{:S(2)}, u32[]{:S(2)}) collective-permute-start(bf16[32,1024]{1,0:T(8,128)(2,1)S(1)} %get-tuple-element.78), channel_id=1, source_target_pairs={{0,4},{1,5},{2,6},{3,7},{4,0},{5,1},{6,2},{7,3},{8,12},{9,13},{10,... | collective-permute-start | bytes 196616 | tf_op jit(solution)/shard_map/ppermute | solution.py:163
  45.1 8.7 %collective-permute-start.13 = (bf16[32,1024]{1,0:T(8,128)(2,1)S(1)}, bf16[32,1024]{1,0:T(8,128)(2,1)S(1)}, u32[]{:S(2)}, u32[]{:S(2)}) collective-permute-start(bf16[32,1024]{1,0:T(8,128)(2,1)S(1)} %get-tuple-element.82), channel_id=1, source_target_pairs={{0,10},{1,11},{2,8},{3,9},{4,14},{5,15},{6,12},{7,13},{8,2},{9,3},... | collective-permute-start | bytes 196616 | tf_op jit(solution)/shard_map/ppermute | solution.py:163
  56.2 12.5 %collective-permute-start.16 = (bf16[2,32,1024]{2,1,0:T(8,128)(2,1)S(1)}, bf16[2,32,1024]{2,1,0:T(8,128)(2,1)S(1)}, u32[]{:S(2)}, u32[]{:S(2)}) collective-permute-start(bf16[2,32,1024]{2,1,0:T(8,128)(2,1)S(1)} %get-tuple-element.87), channel_id=1, source_target_pairs={{0,16},{1,17},{2,18},{3,19},{4,20},{5,21},{6,22},{7,23},{8,24},{9,... | collective-permute-start | bytes 393224 | tf_op jit(solution)/shard_map/ppermute | solution.py:173
  57.8 11.0 %collective-permute-start.17 = (bf16[2,32,1024]{2,1,0:T(8,128)(2,1)S(1)}, bf16[2,32,1024]{2,1,0:T(8,128)(2,1)S(1)}, u32[]{:S(2)}, u32[]{:S(2)}) collective-permute-start(bf16[2,32,1024]{2,1,0:T(8,128)(2,1)S(1)} %get-tuple-element.87), channel_id=1, source_target_pairs={{0,24},{1,25},{2,26},{3,27},{4,28},{5,29},{6,30},{7,31},{8,16},{9,... | collective-permute-start | bytes 393224 | tf_op jit(solution)/shard_map/ppermute | solution.py:173
  57.8 9.6 %collective-permute-start.18 = (bf16[32,1024]{1,0:T(8,128)(2,1)S(1)}, bf16[32,1024]{1,0:T(8,128)(2,1)S(1)}, u32[]{:S(2)}, u32[]{:S(2)}) collective-permute-start(bf16[32,1024]{1,0:T(8,128)(2,1)S(1)} %get-tuple-element.88), channel_id=1, source_target_pairs={{0,28},{1,29},{2,30},{3,31},{4,24},{5,25},{6,26},{7,27},{8,20},{9,... | collective-permute-start | bytes 196616 | tf_op jit(solution)/shard_map/ppermute | solution.py:173
  69.0 9.8 %collective-permute-start.22 = (bf16[4,32,1024]{2,1,0:T(8,128)(2,1)S(1)}, bf16[4,32,1024]{2,1,0:T(8,128)(2,1)S(1)}, u32[]{:S(2)}, u32[]{:S(2)}) collective-permute-start(bf16[4,32,1024]{2,1,0:T(8,128)(2,1)S(1)} %pad_maximum_fusion.3.near), channel_id=1, source_target_pairs={{0,2},{1,3},{2,0},{3,1},{4,6},{5,7},{6,4},{7,5},{8,10},{9,11},{10,... | collective-permute-start | bytes 786440 | tf_op jit(solution)/shard_map/ppermute | solution.py:163
  73.9 9.1 %collective-permute-start.21 = (bf16[4,32,1024]{2,1,0:T(8,128)(2,1)S(1)}, bf16[4,32,1024]{2,1,0:T(8,128)(2,1)S(1)}, u32[]{:S(2)}, u32[]{:S(2)}) collective-permute-start(bf16[4,32,1024]{2,1,0:T(8,128)(2,1)S(1)} %pad_maximum_fusion.2.near), channel_id=1, source_target_pairs={{0,4},{1,5},{2,6},{3,7},{4,0},{5,1},{6,2},{7,3},{8,12},{9,13},{10,... | collective-permute-start | bytes 786440 | tf_op jit(solution)/shard_map/ppermute | solution.py:163
  81.6 7.8 %collective-permute-start.24 = (bf16[4,32,1024]{2,1,0:T(8,128)(2,1)S(1)}, bf16[4,32,1024]{2,1,0:T(8,128)(2,1)S(1)}, u32[]{:S(2)}, u32[]{:S(2)}) collective-permute-start(bf16[4,32,1024]{2,1,0:T(8,128)(2,1)S(1)} %get-tuple-element.97), channel_id=1, source_target_pairs={{0,2},{1,3},{2,0},{3,1},{4,6},{5,7},{6,4},{7,5},{8,10},{9,11},{10,... | collective-permute-start | bytes 786440 | tf_op jit(solution)/shard_map/ppermute | solution.py:163
  85.8 8.1 %collective-permute-start.23 = (bf16[4,32,1024]{2,1,0:T(8,128)(2,1)S(1)}, bf16[4,32,1024]{2,1,0:T(8,128)(2,1)S(1)}, u32[]{:S(2)}, u32[]{:S(2)}) collective-permute-start(bf16[4,32,1024]{2,1,0:T(8,128)(2,1)S(1)} %get-tuple-element.95), channel_id=1, source_target_pairs={{0,4},{1,5},{2,6},{3,7},{4,0},{5,1},{6,2},{7,3},{8,12},{9,13},{10,... | collective-permute-start | bytes 786440 | tf_op jit(solution)/shard_map/ppermute | solution.py:163
  89.5 8.9 %collective-permute-start.26 = (bf16[32,1024]{1,0:T(8,128)(2,1)S(1)}, bf16[32,1024]{1,0:T(8,128)(2,1)S(1)}, u32[]{:S(2)}, u32[]{:S(2)}) collective-permute-start(bf16[32,1024]{1,0:T(8,128)(2,1)S(1)} %get-tuple-element.101), channel_id=1, source_target_pairs={{0,8},{1,9},{2,10},{3,11},{4,12},{5,13},{6,14},{7,15},{8,0},{9,1},... | collective-permute-start | bytes 196616 | tf_op jit(solution)/shard_map/ppermute | solution.py:163
  89.6 8.9 %collective-permute-start.27 = (bf16[32,1024]{1,0:T(8,128)(2,1)S(1)}, bf16[32,1024]{1,0:T(8,128)(2,1)S(1)}, u32[]{:S(2)}, u32[]{:S(2)}) collective-permute-start(bf16[32,1024]{1,0:T(8,128)(2,1)S(1)} %get-tuple-element.102), channel_id=1, source_target_pairs={{0,4},{1,5},{2,6},{3,7},{4,0},{5,1},{6,2},{7,3},{8,12},{9,13},{10,... | collective-permute-start | bytes 196616 | tf_op jit(solution)/shard_map/ppermute | solution.py:163
  94.0 6.3 %collective-permute-start.28 = (bf16[32,1024]{1,0:T(8,128)(2,1)S(1)}, bf16[32,1024]{1,0:T(8,128)(2,1)S(1)}, u32[]{:S(2)}, u32[]{:S(2)}) collective-permute-start(bf16[32,1024]{1,0:T(8,128)(2,1)S(1)} %get-tuple-element.106), channel_id=1, source_target_pairs={{0,10},{1,11},{2,8},{3,9},{4,14},{5,15},{6,12},{7,13},{8,2},{9,3},... | collective-permute-start | bytes 196616 | tf_op jit(solution)/shard_map/ppermute | solution.py:163
  (15 other events, 108.4 us)

commit v8 on v4

--- a/solution.py
+++ b/solution.py
@@ -39,7 +39,7 @@
 
 
 def first_kernel(experts_all, inflow_hbm, ids_hbm, weights_hbm, *refs):
-    payloads, (inflow, ids, weights, sem) = refs[:-4], refs[-4:]
+    both, inflow, ids, weights, sem = refs
     copies = [
         pltpu.make_async_copy(source, target, sem.at[number])
         for number, (source, target) in enumerate(
@@ -51,10 +51,8 @@
     for copy in copies:
         copy.wait()
     features = inflow.shape[-1]
-    tails = token_weights(experts_all, payloads[0].shape[-1] - features, ids, weights)
-    for micro, payload in enumerate(payloads):
-        payload[:, :features] = inflow[micro]
-        payload[:, features:] = tails[micro]
+    both[:, :, :features] = inflow[...]
+    both[:, :, features:] = token_weights(experts_all, both.shape[-1] - features, ids, weights)
 
 
 def first_payloads(inflow, ids, weights, experts_all):
@@ -62,9 +60,9 @@
     width = -(-2 * experts_all * ids.shape[0] // LANES) * LANES
     return pl.pallas_call(
         functools.partial(first_kernel, experts_all),
-        out_shape=(jax.ShapeDtypeStruct((tokens, features + width), jnp.bfloat16),) * micro_count,
+        out_shape=jax.ShapeDtypeStruct((micro_count, tokens, features + width), jnp.bfloat16),
         in_specs=[pl.BlockSpec(memory_space=pltpu.HBM)] * 3,
-        out_specs=[pl.BlockSpec(memory_space=pltpu.VMEM)] * micro_count,
+        out_specs=pl.BlockSpec(memory_space=pltpu.VMEM),
         scratch_shapes=[
             pltpu.VMEM(inflow.shape, inflow.dtype),
             pltpu.VMEM(ids.shape, ids.dtype),
@@ -264,13 +262,13 @@
     steps = expert_ids.shape[0]
     micro_count = in_flight.shape[1]
     micros = range(micro_count)
-    payloads = first_payloads(
+    both = first_payloads(
         in_flight[0],
         jnp.swapaxes(expert_ids[:, 0], -1, -2),
         jnp.swapaxes(route_weights[:, 0], -1, -2),
         experts_all,
     )
-    *payloads, gate_up, w_down = tied(*payloads, gate_up, w_down)
+    both, gate_up, w_down = tied(both, gate_up, w_down)
     own_in, own_out = gate_up[0], w_down[0]
     far_in, far_out = swap_core(own_in), swap_core(own_out)
     gain = norm_gain
@@ -278,18 +276,17 @@
     outputs = []
     for step in range(steps):
         near, far, own, parts, results = [], [], [], [], []
-        if step > 0:
+        if step == 0:
+            hopped = [swap_outer(both, by) for by in range(outer - 1, 0, -1)] + [both]
+        else:
             hopped = [next_section(leaving, by) for by in range(outer - 1, -1, -1)]
         for micro in micros:
-            if step == 0:
-                payload = payloads[micro]
-                blocks = [swap_outer(payload, by) for by in range(outer - 1, 0, -1)] + [payload]
-            else:
-                blocks = [block[micro] for block in hopped]
+            blocks = [block[micro] for block in hopped]
+            if step > 0:
                 inflows[micro] = blocks[-1]
             near.append(jnp.stack(blocks[::-1]))
             if step == 0 and micro == 0:
-                gain = hold(payload, own_in, own_out, gain)
+                gain = hold(both, own_in, own_out, gain)
                 near[0], gain = tied(near[0], gain)
             far.append(swap_inner(near[micro]))
         if step == 0:

time: 99.9 us -> 103 us (1.031)
  waiting for transfers between devices: 32.2 us -> 41.3 us
  starting transfers between devices: 48.1 us -> 41.1 us
    ppermute x8, waiting for transfers between devices: 15 us -> 20.7 us  [swap_inner(): return lax.ppermute(value, 'expert', [(i, i ^ 2) for i in range(size)])]
    ppermute x18 -> x15, starting transfers between devices: 28.8 us -> 23.1 us  [swap_outer(): return lax.ppermute(value, 'expert', [(i, i ^ 4 * by) for i in range(size)])]
    ppermute x4, waiting for transfers between devices: 5.09 us -> 6.93 us  [next_section(): return lax.ppermute(value, ('section', 'expert'), pairs)]
    ppermute x18 -> x15, waiting for transfers between devices: 12.1 us -> 13.7 us  [swap_outer(): return lax.ppermute(value, 'expert', [(i, i ^ 4 * by) for i in range(size)])]
    unnamed x18 -> x16, local copies, waits for them, and re-layouts: 4.89 us -> 4.91 us
  transfers between devices with their start and end apart: 32 -> 29, of which waited for: 20 -> 15; matrix products, arithmetic and copies ran while one was open for 0% -> 1% of each run, Pallas kernels for 11% -> 11%
where the time goes in v8:
time: 103 us
  waiting for transfers between devices  41.3 us (40%)
  starting transfers between devices  41.1 us (40%)
  Pallas kernels  13.3 us (13%)
  local copies, waits for them, and re-layouts  5.96 us (6%)
    ppermute x15, starting transfers between devices, swap_outer(): return lax.ppermute(value, 'expert', [(i, i ^ 4 * by) for i in range(size)])  23.1 us
    ppermute x8, waiting for transfers between devices, swap_inner(): return lax.ppermute(value, 'expert', [(i, i ^ 2) for i in range(size)])  20.7 us
    ppermute x15, waiting for transfers between devices, swap_outer(): return lax.ppermute(value, 'expert', [(i, i ^ 4 * by) for i in range(size)])  13.7 us
    pallas_call x4, Pallas kernels, serve(): pl.pallas_call(functools.partial(serve_kernel, features, hidden_count, ch...  11.2 us
    ppermute x8, starting transfers between devices, swap_inner(): return lax.ppermute(value, 'expert', [(i, i ^ 2) for i in range(size)])  10.7 us
    ppermute x4, waiting for transfers between devices, next_section(): return lax.ppermute(value, ('section', 'expert'), pairs)  6.93 us
    ppermute x4, starting transfers between devices, next_section(): return lax.ppermute(value, ('section', 'expert'), pairs)  6.81 us
    unnamed x16, local copies, waits for them, and re-layouts  4.91 us
  transfers between devices with their start and end apart: 29, of which 15 were waited for; matrix products, arithmetic and copies ran while one was open for 1% of the time, Pallas kernels for 11%

profile of v8, /device:TPU:0, one launch (start us, length us, event | category | flops | bytes accessed | tf_op | source)
XLA Modules:
  0.0 102.9 jit_solution(8230706324416010774)
XLA Ops:
  0.0 1.8 %first_payloads.1.after = bf16[2,32,1152]{2,1,0:T(8,128)(2,1)} custom-call(bf16[2,32,1024]{2,1,0:T(8,128)(2,1)} %bitcast.47, s32[2,2,8,32]{3,2,1,0:T(8,128)} %bitcast.48, f32[2,2,8,32]{3,2,1,0:T(8,128)} %bitcast.49), custom_call_target="tpu_custom_call" | custom-call | tf_op jit(solution)/shard_map/first_payloads/pallas_call | solution.py:61
  2.3 4.7 %collective-permute-start.2 = (bf16[2,32,1152]{2,1,0:T(8,128)(2,1)}, bf16[2,32,1152]{2,1,0:T(8,128)(2,1)S(1)}, u32[]{:S(2)}, u32[]{:S(2)}) collective-permute-start(bf16[2,32,1152]{2,1,0:T(8,128)(2,1)} %first_payloads.1.after), channel_id=1, source_target_pairs={{0,12},{1,13},{2,14},{3,15},{4,8},{5,9},{6,10},{7,11},{8,4},{9,5},... | collective-permute-start | bytes 442376 | tf_op jit(solution)/shard_map/ppermute | solution.py:164
  8.6 1.9 %copy-done = bf16[1,1,1024,1536]{3,2,1,0:T(8,128)(2,1)S(1)} copy-done((bf16[1,1,1024,1536]{3,2,1,0:T(8,128)(2,1)S(1)}, bf16[1,1,1024,1536]{3,2,1,0:T(8,128)(2,1)}, u32[]{:S(2)}) %copy-start) | copy-done | bytes 3145752
  13.5 6.8 %collective-permute-done.1 = bf16[2,32,1152]{2,1,0:T(8,128)(2,1)S(1)} collective-permute-done((bf16[2,32,1152]{2,1,0:T(8,128)(2,1)}, bf16[2,32,1152]{2,1,0:T(8,128)(2,1)S(1)}, u32[]{:S(2)}, u32[]{:S(2)}) %collective-permute-start.1) | collective-permute-done | bytes 147488 | tf_op jit(solution)/shard_map/ppermute | solution.py:164
  22.6 7.8 %collective-permute-done.10.far.far_tail = bf16[4,32,1152]{2,1,0:T(8,128)(2,1)S(1)} collective-permute-done((bf16[4,32,1152]{2,1,0:T(8,128)(2,1)S(1)}, bf16[4,32,1152]{2,1,0:T(8,128)(2,1)S(1)}, u32[]{:S(2)}, u32[]{:S(2)}) %collective-permute-start.10) | collective-permute-done | bytes 294944 | tf_op jit(solution)/shard_map/ppermute | solution.py:159
  30.4 2.8 %serve.5 = (f32[4,32,1024]{2,1,0:T(8,128)S(1)}, bf16[4,32,1024]{2,1,0:T(8,128)(2,1)S(1)}) custom-call(bf16[4,32,1152]{2,1,0:T(8,128)(2,1)S(1)} %pad_maximum_fusion.1.near.near_tail, bf16[4,32,1152]{2,1,0:T(8,128)(2,1)S(1)} %collective-permute-done.10.far.far_tail, bf16[4,32,1152]{2,1,0:T(8,128)(2,1)S(1)} %pad_maximum_fusion.1.near.near_tail, ...), custom_call_target="tpu_custom_call" | custom-call | flops 2415919104 | bytes 9437184 | tf_op jit(solution)/shard_map/serve/pallas_call | solution.py:229
  34.8 1.9 %collective-permute-done.3.far.far_tail = bf16[4,32,1152]{2,1,0:T(8,128)(2,1)S(1)} collective-permute-done((bf16[4,32,1152]{2,1,0:T(8,128)(2,1)S(1)}, bf16[4,32,1152]{2,1,0:T(8,128)(2,1)S(1)}, u32[]{:S(2)}, u32[]{:S(2)}) %collective-permute-start.3) | collective-permute-done | bytes 294944 | tf_op jit(solution)/shard_map/ppermute | solution.py:159
  36.7 2.8 %serve.4 = (f32[4,32,1024]{2,1,0:T(8,128)S(1)}, bf16[4,32,1024]{2,1,0:T(8,128)(2,1)S(1)}) custom-call(bf16[4,32,1152]{2,1,0:T(8,128)(2,1)S(1)} %pad_maximum_fusion.near.near_tail, bf16[4,32,1152]{2,1,0:T(8,128)(2,1)S(1)} %collective-permute-done.3.far.far_tail, bf16[4,32,1152]{2,1,0:T(8,128)(2,1)S(1)} %pad_maximum_fusion.near.near_tail, ...), custom_call_target="tpu_custom_call" | custom-call | flops 2415919104 | bytes 9437184 | tf_op jit(solution)/shard_map/serve/pallas_call | solution.py:229
  42.4 2.5 %collective-permute-start.12 = (bf16[32,1024]{1,0:T(8,128)(2,1)S(1)}, bf16[32,1024]{1,0:T(8,128)(2,1)S(1)}, u32[]{:S(2)}, u32[]{:S(2)}) collective-permute-start(bf16[32,1024]{1,0:T(8,128)(2,1)S(1)} %get-tuple-element.51), channel_id=1, source_target_pairs={{0,12},{1,13},{2,14},{3,15},{4,8},{5,9},{6,10},{7,11},{8,4},{9,5},... | collective-permute-start | bytes 196616 | tf_op jit(solution)/shard_map/ppermute | solution.py:164
  44.9 1.9 %collective-permute-start.14 = (bf16[32,1024]{1,0:T(8,128)(2,1)S(1)}, bf16[32,1024]{1,0:T(8,128)(2,1)S(1)}, u32[]{:S(2)}, u32[]{:S(2)}) collective-permute-start(bf16[32,1024]{1,0:T(8,128)(2,1)S(1)} %get-tuple-element.53), channel_id=1, source_target_pairs={{0,4},{1,5},{2,6},{3,7},{4,0},{5,1},{6,2},{7,3},{8,12},{9,13},{10,... | collective-permute-start | bytes 196616 | tf_op jit(solution)/shard_map/ppermute | solution.py:164
  46.9 2.5 %collective-permute-start.7 = (bf16[32,1024]{1,0:T(8,128)(2,1)S(1)}, bf16[32,1024]{1,0:T(8,128)(2,1)S(1)}, u32[]{:S(2)}, u32[]{:S(2)}) collective-permute-start(bf16[32,1024]{1,0:T(8,128)(2,1)S(1)} %get-tuple-element.45), channel_id=1, source_target_pairs={{0,12},{1,13},{2,14},{3,15},{4,8},{5,9},{6,10},{7,11},{8,4},{9,5},... | collective-permute-start | bytes 196616 | tf_op jit(solution)/shard_map/ppermute | solution.py:164
  49.4 1.9 %collective-permute-start.9 = (bf16[32,1024]{1,0:T(8,128)(2,1)S(1)}, bf16[32,1024]{1,0:T(8,128)(2,1)S(1)}, u32[]{:S(2)}, u32[]{:S(2)}) collective-permute-start(bf16[32,1024]{1,0:T(8,128)(2,1)S(1)} %get-tuple-element.47), channel_id=1, source_target_pairs={{0,4},{1,5},{2,6},{3,7},{4,0},{5,1},{6,2},{7,3},{8,12},{9,13},{10,... | collective-permute-start | bytes 196616 | tf_op jit(solution)/shard_map/ppermute | solution.py:164
  54.9 4.4 %collective-permute-start.18 = (bf16[2,32,1024]{2,1,0:T(8,128)(2,1)S(1)}, bf16[2,32,1024]{2,1,0:T(8,128)(2,1)S(1)}, u32[]{:S(2)}, u32[]{:S(2)}) collective-permute-start(bf16[2,32,1024]{2,1,0:T(8,128)(2,1)S(1)} %get-tuple-element.56), channel_id=1, source_target_pairs={{0,28},{1,29},{2,30},{3,31},{4,24},{5,25},{6,26},{7,27},{8,20},{9,... | collective-permute-start | bytes 393224 | tf_op jit(solution)/shard_map/ppermute | solution.py:174
  59.3 1.9 %collective-permute-start.16 = (bf16[2,32,1024]{2,1,0:T(8,128)(2,1)S(1)}, bf16[2,32,1024]{2,1,0:T(8,128)(2,1)S(1)}, u32[]{:S(2)}, u32[]{:S(2)}) collective-permute-start(bf16[2,32,1024]{2,1,0:T(8,128)(2,1)S(1)} %get-tuple-element.56), channel_id=1, source_target_pairs={{0,20},{1,21},{2,22},{3,23},{4,16},{5,17},{6,18},{7,19},{8,28},{9,... | collective-permute-start | bytes 393224 | tf_op jit(solution)/shard_map/ppermute | solution.py:174
  61.7 2.0 %collective-permute-done.18 = bf16[2,32,1024]{2,1,0:T(8,128)(2,1)S(1)} collective-permute-done((bf16[2,32,1024]{2,1,0:T(8,128)(2,1)S(1)}, bf16[2,32,1024]{2,1,0:T(8,128)(2,1)S(1)}, u32[]{:S(2)}, u32[]{:S(2)}) %collective-permute-start.18) | collective-permute-done | bytes 131104 | tf_op jit(solution)/shard_map/ppermute | solution.py:174
  63.7 3.7 %collective-permute-done.17 = bf16[2,32,1024]{2,1,0:T(8,128)(2,1)S(1)} collective-permute-done((bf16[2,32,1024]{2,1,0:T(8,128)(2,1)S(1)}, bf16[2,32,1024]{2,1,0:T(8,128)(2,1)S(1)}, u32[]{:S(2)}, u32[]{:S(2)}) %collective-permute-start.17) | collective-permute-done | bytes 131104 | tf_op jit(solution)/shard_map/ppermute | solution.py:174
  71.0 7.1 %collective-permute-done.24.far = bf16[4,32,1024]{2,1,0:T(8,128)(2,1)S(1)} collective-permute-done((bf16[4,32,1024]{2,1,0:T(8,128)(2,1)S(1)}, bf16[4,32,1024]{2,1,0:T(8,128)(2,1)S(1)}, u32[]{:S(2)}, u32[]{:S(2)}) %collective-permute-start.24) | collective-permute-done | bytes 262176 | tf_op jit(solution)/shard_map/ppermute | solution.py:159
  78.1 2.8 %serve.7 = (f32[4,32,1024]{2,1,0:T(8,128)S(1)}, bf16[4,32,1024]{2,1,0:T(8,128)(2,1)S(1)}) custom-call(bf16[4,32,1024]{2,1,0:T(8,128)(2,1)S(1)} %pad_maximum_fusion.3.near, bf16[4,32,1024]{2,1,0:T(8,128)(2,1)S(1)} %collective-permute-done.24.far, bf16[4,32,1152]{2,1,0:T(8,128)(2,1)S(1)} %pad_maximum_fusion.1.near.near_tail, ...), custom_call_target="tpu_custom_call" | custom-call | flops 2415919104 | bytes 9437184 | tf_op jit(solution)/shard_map/serve/pallas_call | solution.py:229
  83.7 2.8 %serve.6 = (f32[4,32,1024]{2,1,0:T(8,128)S(1)}, bf16[4,32,1024]{2,1,0:T(8,128)(2,1)S(1)}) custom-call(bf16[4,32,1024]{2,1,0:T(8,128)(2,1)S(1)} %pad_maximum_fusion.2.near, bf16[4,32,1024]{2,1,0:T(8,128)(2,1)S(1)} %collective-permute-done.19.far, bf16[4,32,1152]{2,1,0:T(8,128)(2,1)S(1)} %pad_maximum_fusion.near.near_tail, ...), custom_call_target="tpu_custom_call" | custom-call | flops 2415919104 | bytes 9437184 | tf_op jit(solution)/shard_map/serve/pallas_call | solution.py:229
  89.6 2.8 %collective-permute-start.26 = (bf16[32,1024]{1,0:T(8,128)(2,1)S(1)}, bf16[32,1024]{1,0:T(8,128)(2,1)S(1)}, u32[]{:S(2)}, u32[]{:S(2)}) collective-permute-start(bf16[32,1024]{1,0:T(8,128)(2,1)S(1)} %get-tuple-element.66), channel_id=1, source_target_pairs={{0,12},{1,13},{2,14},{3,15},{4,8},{5,9},{6,10},{7,11},{8,4},{9,5},... | collective-permute-start | bytes 196616 | tf_op jit(solution)/shard_map/ppermute | solution.py:164
  92.4 1.7 %collective-permute-start.28 = (bf16[32,1024]{1,0:T(8,128)(2,1)S(1)}, bf16[32,1024]{1,0:T(8,128)(2,1)S(1)}, u32[]{:S(2)}, u32[]{:S(2)}) collective-permute-start(bf16[32,1024]{1,0:T(8,128)(2,1)S(1)} %get-tuple-element.68), channel_id=1, source_target_pairs={{0,4},{1,5},{2,6},{3,7},{4,0},{5,1},{6,2},{7,3},{8,12},{9,13},{10,... | collective-permute-start | bytes 196616 | tf_op jit(solution)/shard_map/ppermute | solution.py:164
  94.2 2.8 %collective-permute-start.21 = (bf16[32,1024]{1,0:T(8,128)(2,1)S(1)}, bf16[32,1024]{1,0:T(8,128)(2,1)S(1)}, u32[]{:S(2)}, u32[]{:S(2)}) collective-permute-start(bf16[32,1024]{1,0:T(8,128)(2,1)S(1)} %get-tuple-element.60), channel_id=1, source_target_pairs={{0,12},{1,13},{2,14},{3,15},{4,8},{5,9},{6,10},{7,11},{8,4},{9,5},... | collective-permute-start | bytes 196616 | tf_op jit(solution)/shard_map/ppermute | solution.py:164
  96.9 1.7 %collective-permute-start.23 = (bf16[32,1024]{1,0:T(8,128)(2,1)S(1)}, bf16[32,1024]{1,0:T(8,128)(2,1)S(1)}, u32[]{:S(2)}, u32[]{:S(2)}) collective-permute-start(bf16[32,1024]{1,0:T(8,128)(2,1)S(1)} %get-tuple-element.62), channel_id=1, source_target_pairs={{0,4},{1,5},{2,6},{3,7},{4,0},{5,1},{6,2},{7,3},{8,12},{9,13},{10,... | collective-permute-start | bytes 196616 | tf_op jit(solution)/shard_map/ppermute | solution.py:164
  100.3 1.8 %collective-permute-done.22 = bf16[32,1024]{1,0:T(8,128)(2,1)S(1)} collective-permute-done((bf16[32,1024]{1,0:T(8,128)(2,1)S(1)}, bf16[32,1024]{1,0:T(8,128)(2,1)S(1)}, u32[]{:S(2)}, u32[]{:S(2)}) %collective-permute-start.22) | collective-permute-done | bytes 65568 | tf_op jit(solution)/shard_map/ppermute | solution.py:164
  (78 shorter events, 28.2 us)
Async XLA Ops:
  1.8 28.6 %collective-permute-start.4 = (bf16[1,1024,1536]{2,1,0:T(8,128)(2,1)}, bf16[1,1024,1536]{2,1,0:T(8,128)(2,1)S(1)}, u32[]{:S(2)}, u32[]{:S(2)}) collective-permute-start(bf16[1,1024,1536]{2,1,0:T(8,128)(2,1)} %bitcast.33), channel_id=1, source_target_pairs={{0,1},{1,0},{2,3},{3,2},{4,5},{5,4},{6,7},{7,6},{8,9},{9,8},{10,11... | collective-permute-start | bytes 9437192 | tf_op jit(solution)/shard_map/ppermute | solution.py:154
  2.3 11.2 %collective-permute-start.2 = (bf16[2,32,1152]{2,1,0:T(8,128)(2,1)}, bf16[2,32,1152]{2,1,0:T(8,128)(2,1)S(1)}, u32[]{:S(2)}, u32[]{:S(2)}) collective-permute-start(bf16[2,32,1152]{2,1,0:T(8,128)(2,1)} %first_payloads.1.after), channel_id=1, source_target_pairs={{0,12},{1,13},{2,14},{3,15},{4,8},{5,9},{6,10},{7,11},{8,4},{9,5},... | collective-permute-start | bytes 442376 | tf_op jit(solution)/shard_map/ppermute | solution.py:164
  7.0 13.3 %collective-permute-start.1 = (bf16[2,32,1152]{2,1,0:T(8,128)(2,1)}, bf16[2,32,1152]{2,1,0:T(8,128)(2,1)S(1)}, u32[]{:S(2)}, u32[]{:S(2)}) collective-permute-start(bf16[2,32,1152]{2,1,0:T(8,128)(2,1)} %first_payloads.1.after), channel_id=1, source_target_pairs={{0,8},{1,9},{2,10},{3,11},{4,12},{5,13},{6,14},{7,15},{8,0},{9,1},... | collective-permute-start | bytes 442376 | tf_op jit(solution)/shard_map/ppermute | solution.py:164
  7.0 13.3 %collective-permute-start = (bf16[2,32,1152]{2,1,0:T(8,128)(2,1)}, bf16[2,32,1152]{2,1,0:T(8,128)(2,1)S(1)}, u32[]{:S(2)}, u32[]{:S(2)}) collective-permute-start(bf16[2,32,1152]{2,1,0:T(8,128)(2,1)} %first_payloads.1.after), channel_id=1, source_target_pairs={{0,4},{1,5},{2,6},{3,7},{4,0},{5,1},{6,2},{7,3},{8,12},{9,13},{10,... | collective-permute-start | bytes 442376 | tf_op jit(solution)/shard_map/ppermute | solution.py:164
  7.6 22.7 %collective-permute-start.5 = (bf16[1,768,1024]{2,1,0:T(8,128)(2,1)}, bf16[1,768,1024]{2,1,0:T(8,128)(2,1)S(1)}, u32[]{:S(2)}, u32[]{:S(2)}) collective-permute-start(bf16[1,768,1024]{2,1,0:T(8,128)(2,1)} %bitcast.39), channel_id=1, source_target_pairs={{0,1},{1,0},{2,3},{3,2},{4,5},{5,4},{6,7},{7,6},{8,9},{9,8},{10,11... | collective-permute-start | bytes 4718600 | tf_op jit(solution)/shard_map/ppermute | solution.py:154
  20.4 10.0 %collective-permute-start.10 = (bf16[4,32,1152]{2,1,0:T(8,128)(2,1)S(1)}, bf16[4,32,1152]{2,1,0:T(8,128)(2,1)S(1)}, u32[]{:S(2)}, u32[]{:S(2)}) collective-permute-start(bf16[4,32,1152]{2,1,0:T(8,128)(2,1)S(1)} %pad_maximum_fusion.1.near.near_tail), channel_id=1, source_target_pairs={{0,2},{1,3},{2,0},{3,1},{4,6},{5,7},{6,4},{7,5},{8,10},{9,11},{10,... | collective-permute-start | bytes 884744 | tf_op jit(solution)/shard_map/ppermute | solution.py:159
  22.0 14.7 %collective-permute-start.3 = (bf16[4,32,1152]{2,1,0:T(8,128)(2,1)S(1)}, bf16[4,32,1152]{2,1,0:T(8,128)(2,1)S(1)}, u32[]{:S(2)}, u32[]{:S(2)}) collective-permute-start(bf16[4,32,1152]{2,1,0:T(8,128)(2,1)S(1)} %pad_maximum_fusion.near.near_tail), channel_id=1, source_target_pairs={{0,2},{1,3},{2,0},{3,1},{4,6},{5,7},{6,4},{7,5},{8,10},{9,11},{10,... | collective-permute-start | bytes 884744 | tf_op jit(solution)/shard_map/ppermute | solution.py:159
  33.2 9.1 %collective-permute-start.11 = (bf16[4,32,1024]{2,1,0:T(8,128)(2,1)S(1)}, bf16[4,32,1024]{2,1,0:T(8,128)(2,1)S(1)}, u32[]{:S(2)}, u32[]{:S(2)}) collective-permute-start(bf16[4,32,1024]{2,1,0:T(8,128)(2,1)S(1)} %get-tuple-element.49), channel_id=1, source_target_pairs={{0,2},{1,3},{2,0},{3,1},{4,6},{5,7},{6,4},{7,5},{8,10},{9,11},{10,... | collective-permute-start | bytes 786440 | tf_op jit(solution)/shard_map/ppermute | solution.py:159
  39.5 7.3 %collective-permute-start.6 = (bf16[4,32,1024]{2,1,0:T(8,128)(2,1)S(1)}, bf16[4,32,1024]{2,1,0:T(8,128)(2,1)S(1)}, u32[]{:S(2)}, u32[]{:S(2)}) collective-permute-start(bf16[4,32,1024]{2,1,0:T(8,128)(2,1)S(1)} %get-tuple-element.43), channel_id=1, source_target_pairs={{0,2},{1,3},{2,0},{3,1},{4,6},{5,7},{6,4},{7,5},{8,10},{9,11},{10,... | collective-permute-start | bytes 786440 | tf_op jit(solution)/shard_map/ppermute | solution.py:159
  42.4 7.1 %collective-permute-start.12 = (bf16[32,1024]{1,0:T(8,128)(2,1)S(1)}, bf16[32,1024]{1,0:T(8,128)(2,1)S(1)}, u32[]{:S(2)}, u32[]{:S(2)}) collective-permute-start(bf16[32,1024]{1,0:T(8,128)(2,1)S(1)} %get-tuple-element.51), channel_id=1, source_target_pairs={{0,12},{1,13},{2,14},{3,15},{4,8},{5,9},{6,10},{7,11},{8,4},{9,5},... | collective-permute-start | bytes 196616 | tf_op jit(solution)/shard_map/ppermute | solution.py:164
  44.9 7.0 %collective-permute-start.13 = (bf16[32,1024]{1,0:T(8,128)(2,1)S(1)}, bf16[32,1024]{1,0:T(8,128)(2,1)S(1)}, u32[]{:S(2)}, u32[]{:S(2)}) collective-permute-start(bf16[32,1024]{1,0:T(8,128)(2,1)S(1)} %get-tuple-element.52), channel_id=1, source_target_pairs={{0,8},{1,9},{2,10},{3,11},{4,12},{5,13},{6,14},{7,15},{8,0},{9,1},... | collective-permute-start | bytes 196616 | tf_op jit(solution)/shard_map/ppermute | solution.py:164
  44.9 7.0 %collective-permute-start.14 = (bf16[32,1024]{1,0:T(8,128)(2,1)S(1)}, bf16[32,1024]{1,0:T(8,128)(2,1)S(1)}, u32[]{:S(2)}, u32[]{:S(2)}) collective-permute-start(bf16[32,1024]{1,0:T(8,128)(2,1)S(1)} %get-tuple-element.53), channel_id=1, source_target_pairs={{0,4},{1,5},{2,6},{3,7},{4,0},{5,1},{6,2},{7,3},{8,12},{9,13},{10,... | collective-permute-start | bytes 196616 | tf_op jit(solution)/shard_map/ppermute | solution.py:164
  46.9 6.2 %collective-permute-start.7 = (bf16[32,1024]{1,0:T(8,128)(2,1)S(1)}, bf16[32,1024]{1,0:T(8,128)(2,1)S(1)}, u32[]{:S(2)}, u32[]{:S(2)}) collective-permute-start(bf16[32,1024]{1,0:T(8,128)(2,1)S(1)} %get-tuple-element.45), channel_id=1, source_target_pairs={{0,12},{1,13},{2,14},{3,15},{4,8},{5,9},{6,10},{7,11},{8,4},{9,5},... | collective-permute-start | bytes 196616 | tf_op jit(solution)/shard_map/ppermute | solution.py:164
  54.9 8.8 %collective-permute-start.18 = (bf16[2,32,1024]{2,1,0:T(8,128)(2,1)S(1)}, bf16[2,32,1024]{2,1,0:T(8,128)(2,1)S(1)}, u32[]{:S(2)}, u32[]{:S(2)}) collective-permute-start(bf16[2,32,1024]{2,1,0:T(8,128)(2,1)S(1)} %get-tuple-element.56), channel_id=1, source_target_pairs={{0,28},{1,29},{2,30},{3,31},{4,24},{5,25},{6,26},{7,27},{8,20},{9,... | collective-permute-start | bytes 393224 | tf_op jit(solution)/shard_map/ppermute | solution.py:174
  59.3 8.1 %collective-permute-start.17 = (bf16[2,32,1024]{2,1,0:T(8,128)(2,1)S(1)}, bf16[2,32,1024]{2,1,0:T(8,128)(2,1)S(1)}, u32[]{:S(2)}, u32[]{:S(2)}) collective-permute-start(bf16[2,32,1024]{2,1,0:T(8,128)(2,1)S(1)} %get-tuple-element.56), channel_id=1, source_target_pairs={{0,24},{1,25},{2,26},{3,27},{4,28},{5,29},{6,30},{7,31},{8,16},{9,... | collective-permute-start | bytes 393224 | tf_op jit(solution)/shard_map/ppermute | solution.py:174
  59.3 8.1 %collective-permute-start.16 = (bf16[2,32,1024]{2,1,0:T(8,128)(2,1)S(1)}, bf16[2,32,1024]{2,1,0:T(8,128)(2,1)S(1)}, u32[]{:S(2)}, u32[]{:S(2)}) collective-permute-start(bf16[2,32,1024]{2,1,0:T(8,128)(2,1)S(1)} %get-tuple-element.56), channel_id=1, source_target_pairs={{0,20},{1,21},{2,22},{3,23},{4,16},{5,17},{6,18},{7,19},{8,28},{9,... | collective-permute-start | bytes 393224 | tf_op jit(solution)/shard_map/ppermute | solution.py:174
  61.2 7.5 %collective-permute-start.15 = (bf16[2,32,1024]{2,1,0:T(8,128)(2,1)S(1)}, bf16[2,32,1024]{2,1,0:T(8,128)(2,1)S(1)}, u32[]{:S(2)}, u32[]{:S(2)}) collective-permute-start(bf16[2,32,1024]{2,1,0:T(8,128)(2,1)S(1)} %get-tuple-element.56), channel_id=1, source_target_pairs={{0,16},{1,17},{2,18},{3,19},{4,20},{5,21},{6,22},{7,23},{8,24},{9,... | collective-permute-start | bytes 393224 | tf_op jit(solution)/shard_map/ppermute | solution.py:174
  68.8 9.3 %collective-permute-start.24 = (bf16[4,32,1024]{2,1,0:T(8,128)(2,1)S(1)}, bf16[4,32,1024]{2,1,0:T(8,128)(2,1)S(1)}, u32[]{:S(2)}, u32[]{:S(2)}) collective-permute-start(bf16[4,32,1024]{2,1,0:T(8,128)(2,1)S(1)} %pad_maximum_fusion.3.near), channel_id=1, source_target_pairs={{0,2},{1,3},{2,0},{3,1},{4,6},{5,7},{6,4},{7,5},{8,10},{9,11},{10,... | collective-permute-start | bytes 786440 | tf_op jit(solution)/shard_map/ppermute | solution.py:159
  70.4 13.3 %collective-permute-start.19 = (bf16[4,32,1024]{2,1,0:T(8,128)(2,1)S(1)}, bf16[4,32,1024]{2,1,0:T(8,128)(2,1)S(1)}, u32[]{:S(2)}, u32[]{:S(2)}) collective-permute-start(bf16[4,32,1024]{2,1,0:T(8,128)(2,1)S(1)} %pad_maximum_fusion.2.near), channel_id=1, source_target_pairs={{0,2},{1,3},{2,0},{3,1},{4,6},{5,7},{6,4},{7,5},{8,10},{9,11},{10,... | collective-permute-start | bytes 786440 | tf_op jit(solution)/shard_map/ppermute | solution.py:159
  80.9 8.7 %collective-permute-start.25 = (bf16[4,32,1024]{2,1,0:T(8,128)(2,1)S(1)}, bf16[4,32,1024]{2,1,0:T(8,128)(2,1)S(1)}, u32[]{:S(2)}, u32[]{:S(2)}) collective-permute-start(bf16[4,32,1024]{2,1,0:T(8,128)(2,1)S(1)} %get-tuple-element.64), channel_id=1, source_target_pairs={{0,2},{1,3},{2,0},{3,1},{4,6},{5,7},{6,4},{7,5},{8,10},{9,11},{10,... | collective-permute-start | bytes 786440 | tf_op jit(solution)/shard_map/ppermute | solution.py:159
  86.5 7.6 %collective-permute-start.20 = (bf16[4,32,1024]{2,1,0:T(8,128)(2,1)S(1)}, bf16[4,32,1024]{2,1,0:T(8,128)(2,1)S(1)}, u32[]{:S(2)}, u32[]{:S(2)}) collective-permute-start(bf16[4,32,1024]{2,1,0:T(8,128)(2,1)S(1)} %get-tuple-element.58), channel_id=1, source_target_pairs={{0,2},{1,3},{2,0},{3,1},{4,6},{5,7},{6,4},{7,5},{8,10},{9,11},{10,... | collective-permute-start | bytes 786440 | tf_op jit(solution)/shard_map/ppermute | solution.py:159
  89.6 7.3 %collective-permute-start.26 = (bf16[32,1024]{1,0:T(8,128)(2,1)S(1)}, bf16[32,1024]{1,0:T(8,128)(2,1)S(1)}, u32[]{:S(2)}, u32[]{:S(2)}) collective-permute-start(bf16[32,1024]{1,0:T(8,128)(2,1)S(1)} %get-tuple-element.66), channel_id=1, source_target_pairs={{0,12},{1,13},{2,14},{3,15},{4,8},{5,9},{6,10},{7,11},{8,4},{9,5},... | collective-permute-start | bytes 196616 | tf_op jit(solution)/shard_map/ppermute | solution.py:164
  92.4 6.3 %collective-permute-start.27 = (bf16[32,1024]{1,0:T(8,128)(2,1)S(1)}, bf16[32,1024]{1,0:T(8,128)(2,1)S(1)}, u32[]{:S(2)}, u32[]{:S(2)}) collective-permute-start(bf16[32,1024]{1,0:T(8,128)(2,1)S(1)} %get-tuple-element.67), channel_id=1, source_target_pairs={{0,8},{1,9},{2,10},{3,11},{4,12},{5,13},{6,14},{7,15},{8,0},{9,1},... | collective-permute-start | bytes 196616 | tf_op jit(solution)/shard_map/ppermute | solution.py:164
  92.4 6.3 %collective-permute-start.28 = (bf16[32,1024]{1,0:T(8,128)(2,1)S(1)}, bf16[32,1024]{1,0:T(8,128)(2,1)S(1)}, u32[]{:S(2)}, u32[]{:S(2)}) collective-permute-start(bf16[32,1024]{1,0:T(8,128)(2,1)S(1)} %get-tuple-element.68), channel_id=1, source_target_pairs={{0,4},{1,5},{2,6},{3,7},{4,0},{5,1},{6,2},{7,3},{8,12},{9,13},{10,... | collective-permute-start | bytes 196616 | tf_op jit(solution)/shard_map/ppermute | solution.py:164
  (13 other events, 105.6 us)
